TPU v7x, 32 devices: a whole 2x2x4 slice. The times are simulated.
32 devices in a mesh: wide: 8 (over y, x, core), narrow: 4 (over z).
Axes of the slice: x: 2, y: 2, z: 4, core: 2. Of those that a mesh axis runs over, the one named last changes fastest.
Arguments:
- block_in: bfloat16 [32, 1024, 768], P(('wide', 'narrow')), may hold values from -6 to 6
- seq_lengths: int32 [32], P(('wide', 'narrow')), may hold values from 192 to 1024, as said below
- routes: int32 [32, 1024, 1], P(('wide', 'narrow')), may hold values from 0 to 7; in each aligned block of 1024 rows (0 to 1023, 1024 to 2047, ..., all dimensions but the last counted through in order) at most 192 rows name the same one
- first_gain: float32 [768], replicated, may hold values from 0.1 to 1.9
- first_shift: float32 [768], replicated, may hold values from -3 to 3
- query_weight: bfloat16 [768, 768], replicated, may hold values from -0.21875 to 0.21875
- key_weight: bfloat16 [768, 768], replicated, may hold values from -0.21875 to 0.21875
- value_weight: bfloat16 [768, 768], replicated, may hold values from -0.21875 to 0.21875
- output_weight: bfloat16 [768, 768], replicated, may hold values from -1.75 to 1.75
- second_gain: float32 [768], replicated, may hold values from 0.1 to 1.9
- second_shift: float32 [768], replicated, may hold values from -3 to 3
- centroids: bfloat16 [768, 8], replicated, may hold values from -0.21875 to 0.21875
- hidden_weight: bfloat16 [8, 768, 3072], P('wide', None, 'narrow'), may hold values from -0.21875 to 0.21875
- down_weight: bfloat16 [8, 3072, 768], P('wide', 'narrow'), may hold values from -0.21875 to 0.21875
- cotangent: bfloat16 [32, 1024, 768], P(('wide', 'narrow')), may hold values from -6 to 6
Outputs:
- block_out: bfloat16 [32, 1024, 768], P(('wide', 'narrow'))
- input_grad: bfloat16 [32, 1024, 768], P(('wide', 'narrow'))
- first_gain_grad: float32 [768], replicated
- first_shift_grad: float32 [768], replicated
- query_grad: float32 [768, 768], replicated
- key_grad: float32 [768, 768], replicated
- value_grad: float32 [768, 768], replicated
- output_weight_grad: float32 [768, 768], replicated
- second_gain_grad: float32 [768], replicated
- second_shift_grad: float32 [768], replicated
- centroids_grad: float32 [768, 8], replicated
- hidden_grad: float32 [8, 768, 3072], P('wide', None, 'narrow')
- down_grad: float32 [8, 3072, 768], P('wide', 'narrow')
Inputs may be any that keep to these rules, and one draw needn't show every extreme that they name: `seq_lengths`: each sequence's true length; some sequence has all 1024 slots live. `routes`: among the tokens of one device (1 x 1024 consecutive slots, padding included) no expert is named by more than 192 tokens, a bound that some block reaches.
All inputs are finite; a program needn't handle non-finite values.
Results may differ from a plain program's by a relative error of at most 0.015.
Values may be sent and summed in bfloat16 or wider, within the bound.
No kernel may reach another device: no remote copies, remote signals or barrier semaphores. Data moves between devices by JAX's collectives and lax.ppermute only.
A program may use at most 384 MiB of HBM per device.

v0:
```python
import jax
import jax.numpy as jnp
from jax import lax
from jax.sharding import PartitionSpec as P

HEADS = 12


EPSILON = 1e-05
MASKED_SCORE = -1000000000.0
EXACT = lax.Precision.HIGHEST


def normalize(values, gain, shift):
    centre = jnp.mean(values, -1, keepdims=True)
    centered = values - centre
    spread = jnp.mean(centered * centered, -1, keepdims=True)
    return centered * lax.rsqrt(spread + EPSILON) * gain + shift


def block_scores(query, keys, start, seq_len, scale):
    scores = jnp.einsum("qhd,khd->hqk", query, keys, preferred_element_type=jnp.float32) * scale
    query_pos = start + lax.broadcasted_iota(jnp.int32, (query.shape[0], keys.shape[0]), 0)
    key_pos = lax.broadcasted_iota(jnp.int32, (query.shape[0], keys.shape[0]), 1)
    allowed = (key_pos <= query_pos) & (key_pos < seq_len)
    return jnp.where(allowed[None], scores, MASKED_SCORE)


def gelu_exact(values):
    return jax.nn.gelu(values, approximate=False)


def expert_forward(inputs, first_w, second_w):
    before = jnp.einsum("erd,edf->erf", inputs, first_w, preferred_element_type=jnp.float32)
    active = gelu_exact(before).astype(jnp.bfloat16)
    result = jnp.einsum("erf,efd->erd", active, second_w, preferred_element_type=jnp.float32)
    return (before, active, result)


def expert_backward(inputs, before, active, incoming, first_w, second_w):
    grad_second = jnp.einsum("erf,erd->efd", active, incoming, preferred_element_type=jnp.float32)
    grad_active = jnp.einsum("erd,efd->erf", incoming, second_w, preferred_element_type=jnp.float32)
    unused, gelu_back = jax.vjp(gelu_exact, before)
    grad_before = gelu_back(grad_active)[0].astype(jnp.bfloat16)
    grad_first = jnp.einsum("erd,erf->edf", inputs, grad_before, preferred_element_type=jnp.float32)
    grad_inputs = jnp.einsum(
        "erf,edf->erd", grad_before, first_w, preferred_element_type=jnp.float32
    )
    return (grad_first, grad_second, grad_inputs)


def shards(
    block_in,
    seq_lengths,
    routes,
    first_gain,
    first_shift,
    query_weight,
    key_weight,
    value_weight,
    output_weight,
    second_gain,
    second_shift,
    centroids,
    hidden_weight,
    down_weight,
    cotangent,
):
    seqs_here, length, width = block_in.shape
    head_size = width // HEADS
    scale = head_size ** (-0.5)
    qblock = min(512, length)
    tokens = seqs_here * length
    experts_all = centroids.shape[1]
    capacity = 3 * tokens // (2 * experts_all)
    qkv_weight = jnp.concatenate([query_weight, key_weight, value_weight], 1)
    inputs_wide = block_in.astype(jnp.float32)
    positions = lax.broadcasted_iota(jnp.int32, (seqs_here, length), 1)
    live = positions < seq_lengths[:, None]
    seq = 0
    normed_low = normalize(inputs_wide[seq], first_gain, first_shift).astype(jnp.bfloat16)
    projected = jnp.dot(normed_low, qkv_weight, preferred_element_type=jnp.float32).astype(
        jnp.bfloat16
    )
    query = projected[:, :width].reshape(length, HEADS, head_size)
    keys = projected[:, width : 2 * width].reshape(length, HEADS, head_size)
    values = projected[:, 2 * width :].reshape(length, HEADS, head_size)
    mixed_parts = []
    logsum_parts = []
    for block in range(length // qblock):
        start = block * qblock
        finish = start + qblock
        scores = block_scores(query[start:finish], keys[:finish], start, seq_lengths[seq], scale)
        highest = jnp.max(scores, -1, keepdims=True)
        expo = jnp.exp(scores - highest)
        totals = jnp.sum(expo, -1, keepdims=True)
        probs = (expo / totals).astype(jnp.bfloat16)
        logsum_parts.append(highest + jnp.log(totals))
        mixed_parts.append(
            jnp.einsum("hqk,khd->qhd", probs, values[:finish], preferred_element_type=jnp.float32)
        )
    mixed = jnp.concatenate(mixed_parts, 0).reshape(length, width).astype(jnp.bfloat16)
    records = [(normed_low, query, keys, values, logsum_parts, mixed)]
    mixed_all = jnp.concatenate([record[5] for record in records], 0)
    attended = jnp.dot(mixed_all, output_weight, preferred_element_type=jnp.float32)
    resid = inputs_wide.reshape(tokens, width) + attended
    normed_second = normalize(resid, second_gain, second_shift).astype(jnp.bfloat16)
    live_flat = live.reshape(tokens)
    route_flat = routes.reshape(tokens)
    expert_ids = lax.broadcasted_iota(jnp.int32, (tokens, experts_all), 1)
    picked = route_flat[:, None] == expert_ids
    ones_live = (picked & live_flat[:, None]).astype(jnp.int32)
    earlier = jnp.cumsum(ones_live, 0, dtype=jnp.int32) - ones_live
    slot = jnp.sum(earlier * ones_live, 1, dtype=jnp.int32)
    target = route_flat * capacity + slot
    slot_ids = lax.broadcasted_iota(jnp.int32, (tokens, experts_all * capacity), 1)
    table = ((target[:, None] == slot_ids) & live_flat[:, None]).astype(jnp.bfloat16)
    dispatched = jnp.einsum("tc,td->cd", table, normed_second, preferred_element_type=jnp.float32)
    dispatched = dispatched.astype(jnp.bfloat16).reshape(experts_all, capacity, width)
    logits = jnp.dot(normed_second, centroids, preferred_element_type=jnp.float32)
    chosen = jnp.sum(jnp.where(picked, logits, 0.0), 1)
    gate = jax.nn.sigmoid(chosen)
    arrived = lax.all_to_all(dispatched, "wide", split_axis=0, concat_axis=1, tiled=True)
    gathered = lax.all_gather(arrived, "narrow", axis=1, tiled=True)
    before, active, partial_out = expert_forward(gathered, hidden_weight, down_weight)
    finished = lax.psum_scatter(
        partial_out.astype(jnp.bfloat16), "narrow", scatter_dimension=1, tiled=True
    )
    returned = lax.all_to_all(finished, "wide", split_axis=1, concat_axis=0, tiled=True)
    expert_rows = jnp.dot(
        table, returned.reshape(experts_all * capacity, width), preferred_element_type=jnp.float32
    )
    block_out = (
        (resid + gate[:, None] * expert_rows).astype(jnp.bfloat16).reshape(seqs_here, length, width)
    )
    upstream = cotangent.astype(jnp.float32).reshape(tokens, width) * live_flat[:, None].astype(
        jnp.float32
    )
    grad_rows = (gate[:, None] * upstream).astype(jnp.bfloat16)
    grad_gate = jnp.sum(upstream * expert_rows, 1)
    grad_chosen = grad_gate * gate * (1.0 - gate)
    grad_logits = jnp.where(picked, grad_chosen[:, None], 0.0)
    grad_centroids = jnp.einsum(
        "td,te->de", normed_second.astype(jnp.float32), grad_logits, precision=EXACT
    )
    grad_router = jnp.dot(grad_logits, centroids.astype(jnp.float32).T, precision=EXACT)
    grad_dispatched = jnp.einsum("tc,td->cd", table, grad_rows, preferred_element_type=jnp.float32)
    grad_dispatched = grad_dispatched.astype(jnp.bfloat16).reshape(experts_all, capacity, width)
    grad_arrived = lax.all_to_all(grad_dispatched, "wide", split_axis=0, concat_axis=1, tiled=True)
    grad_gathered = lax.all_gather(grad_arrived, "narrow", axis=1, tiled=True)
    grad_hidden, grad_down, grad_part = expert_backward(
        gathered, before, active, grad_gathered, hidden_weight, down_weight
    )
    grad_back = lax.psum_scatter(
        grad_part.astype(jnp.bfloat16), "narrow", scatter_dimension=1, tiled=True
    )
    grad_returned = lax.all_to_all(grad_back, "wide", split_axis=1, concat_axis=0, tiled=True)
    grad_normed_second = (
        jnp.dot(
            table,
            grad_returned.reshape(experts_all * capacity, width),
            preferred_element_type=jnp.float32,
        )
        + grad_router
    )
    unused, second_back = jax.vjp(normalize, resid, second_gain, second_shift)
    grad_resid_norm, grad_second_gain, grad_second_shift = second_back(grad_normed_second)
    grad_resid = upstream + grad_resid_norm
    grad_attn_low = grad_resid.astype(jnp.bfloat16)
    grad_output_weight = jnp.einsum(
        "td,te->de", mixed_all, grad_attn_low, preferred_element_type=jnp.float32
    )
    grad_mixed = jnp.dot(grad_attn_low, output_weight.T, preferred_element_type=jnp.float32).astype(
        jnp.bfloat16
    )
    seq = 0
    normed_low, query, keys, values, logsum_parts, unused_mixed = records[seq]
    grad_seq_mixed = grad_mixed.reshape(length, HEADS, head_size)
    grad_query_parts = []
    grad_keys = jnp.zeros((length, HEADS, head_size), jnp.float32)
    grad_values = jnp.zeros((length, HEADS, head_size), jnp.float32)
    for block in range(length // qblock):
        start = block * qblock
        finish = start + qblock
        scores = block_scores(query[start:finish], keys[:finish], start, seq_lengths[seq], scale)
        probs = jnp.exp(scores - logsum_parts[block])
        grad_block = grad_seq_mixed[start:finish]
        grad_probs = jnp.einsum(
            "qhd,khd->hqk", grad_block, values[:finish], preferred_element_type=jnp.float32
        )
        centre = jnp.sum(probs * grad_probs, -1, keepdims=True)
        grad_scores = (probs * (grad_probs - centre)).astype(jnp.bfloat16)
        grad_query_parts.append(
            jnp.einsum(
                "hqk,khd->qhd", grad_scores, keys[:finish], preferred_element_type=jnp.float32
            )
            * scale
        )
        grad_keys = grad_keys.at[:finish].add(
            jnp.einsum(
                "hqk,qhd->khd", grad_scores, query[start:finish], preferred_element_type=jnp.float32
            )
            * scale
        )
        grad_values = grad_values.at[:finish].add(
            jnp.einsum(
                "hqk,qhd->khd",
                probs.astype(jnp.bfloat16),
                grad_block,
                preferred_element_type=jnp.float32,
            )
        )
    grad_projected = jnp.concatenate(
        [
            jnp.concatenate(grad_query_parts, 0).reshape(length, width),
            grad_keys.reshape(length, width),
            grad_values.reshape(length, width),
        ],
        1,
    ).astype(jnp.bfloat16)
    grad_qkv_weight = jnp.einsum(
        "td,te->de", normed_low, grad_projected, preferred_element_type=jnp.float32
    )
    grad_normed_first = jnp.dot(grad_projected, qkv_weight.T, preferred_element_type=jnp.float32)
    unused_value, first_back = jax.vjp(normalize, inputs_wide[seq], first_gain, first_shift)
    grad_in_norm, grad_gain_one, grad_shift_one = first_back(grad_normed_first)
    grad_inputs = [grad_resid + grad_in_norm]
    input_grad = jnp.stack(grad_inputs, 0).astype(jnp.bfloat16)
    summed = lax.psum(
        (
            grad_gain_one,
            grad_shift_one,
            grad_qkv_weight,
            grad_output_weight,
            grad_second_gain,
            grad_second_shift,
            grad_centroids,
        ),
        ("wide", "narrow"),
    )
    (
        first_gain_grad,
        first_shift_grad,
        qkv_grad,
        output_weight_grad,
        second_gain_grad,
        second_shift_grad,
        centroids_grad,
    ) = summed
    query_grad = qkv_grad[:, :width]
    key_grad = qkv_grad[:, width : 2 * width]
    value_grad = qkv_grad[:, 2 * width :]
    return (
        block_out,
        input_grad,
        first_gain_grad,
        first_shift_grad,
        query_grad,
        key_grad,
        value_grad,
        output_weight_grad,
        second_gain_grad,
        second_shift_grad,
        centroids_grad,
        grad_hidden,
        grad_down,
    )


def solution(mesh):
    in_specs = (
        P(("wide", "narrow"), None, None),
        P(("wide", "narrow")),
        P(("wide", "narrow"), None, None),
        P(),
        P(),
        P(),
        P(),
        P(),
        P(),
        P(),
        P(),
        P(),
        P("wide", None, "narrow"),
        P("wide", "narrow", None),
        P(("wide", "narrow"), None, None),
    )
    out_specs = (
        P(("wide", "narrow"), None, None),
        P(("wide", "narrow"), None, None),
        P(),
        P(),
        P(),
        P(),
        P(),
        P(),
        P(),
        P(),
        P(),
        P("wide", None, "narrow"),
        P("wide", "narrow", None),
    )
    return jax.shard_map(shards, mesh=mesh, in_specs=in_specs, out_specs=out_specs, check_vma=False)
```

profile of v0, /device:TPU:0, one launch (start us, length us, event | category | flops | bytes accessed | tf_op | source)
XLA Modules:
  0.0 1409.4 jit_solution(3249379801084786582)
XLA Ops:
  11.8 4.5 convolution_convert_fusion.2
  38.7 3.4 fusion.37
  46.9 5.8 fusion.106
  52.7 10.7 fusion.24
  63.4 12.3 fusion
  78.8 8.5 fusion.105
  88.9 3.4 fusion.152
  98.4 34.5 %all_to_all.42 = bf16[8,192,768]{2,1,0:T(8,128)(2,1)} all-to-all(bf16[8,192,768]{2,1,0:T(8,128)(2,1)S(1)} %bitcast.228), channel_id=1, replica_groups=mesh['wide'=8,'narrow'=4] {'wide'}, dimensions={0} | all-to-all | bytes 4718592 | tf_op jit(solution)/shard_map/all_to_all | solution.py:123
  132.9 166.2 %all-gather.3.cloned.1.call-done = bf16[1,6144,768]{2,1,0:T(8,128)(2,1)} async-done(((bf16[1,1536,768]{2,1,0:T(8,128)(2,1)}), bf16[1,6144,768]{2,1,0:T(8,128)(2,1)}) %all-gather.3.cloned.1.call-update) | async-done | bytes 9437200 | tf_op jit(solution)/shard_map/all_gather | solution.py:124
  299.2 49.3 %multiply_convert_fusion.1 = (bf16[6144,768]{1,0:T(8,128)(2,1)S(1)}, f32[6144,768]{1,0:T(8,128)}, f32[6144,768]{1,0:T(8,128)}) fusion(bf16[1,768,768]{2,1,0:T(8,128)(2,1)S(1)} %copy-done, bf16[1,6144,768]{2,1,0:T(8,128)(2,1)} %all-gather.3.cloned.1.call-done), kind=kOutput, calls=%fused_computation.11 | convolution fusion | flops 7554465792 | bytes 57802752 | tf_op jit(solution)/shard_map/erd,edf->erf/dot_general | solution.py:34
  348.4 3.6 copy-done.80
  352.1 9.5 fusion.22
  361.6 159.6 %reduce-scatter.3.cloned.1.call-done = bf16[1,1536,768]{2,1,0:T(8,128)(2,1)} async-done(((bf16[1,6144,768]{2,1,0:T(8,128)(2,1)}), bf16[1,1536,768]{2,1,0:T(8,128)(2,1)}) %reduce-scatter.3.cloned.1.call-update) | async-done | bytes 2359312 | tf_op jit(solution)/shard_map/reduce_scatter | solution.py:126
  521.2 5.6 copy.133
  527.4 24.1 %reduce.11 = bf16[1536,768]{1,0:T(8,128)(2,1)S(1)} reduce(bf16[1536,1,768]{2,1,0:T(2,128)(2,1)} %bitcast.204, bf16[]{:T(256)} %broadcast.614), dimensions={1}, to_apply=%bitcast.196.reduce_sub_computation | reduce | bytes 4718594
  554.8 4.5 all-to-all-start.1
  562.5 26.3 %all-to-all-done.1 = bf16[8,2,73728]{2,1,0:T(2,128)(2,1)} async-done(((bf16[8,2,73728]{2,1,0:T(2,128)(2,1)}), bf16[8,2,73728]{2,1,0:T(2,128)(2,1)}, u32[]{:S(2)}, u32[]{:S(2)}) %all-to-all-start.1) | async-done | bytes 2359328 | tf_op jit(solution)/shard_map/all_to_all | solution.py:129
  588.7 7.0 reshape.544
  595.8 7.5 fusion.65
  603.3 3.5 fusion.53
  606.8 32.6 %all_to_all.43 = bf16[8,192,768]{2,1,0:T(8,128)(2,1)} all-to-all(bf16[8,192,768]{2,1,0:T(8,128)(2,1)S(1)} %bitcast.229), channel_id=1, replica_groups=mesh['wide'=8,'narrow'=4] {'wide'}, dimensions={0} | all-to-all | bytes 4718592 | tf_op jit(solution)/shard_map/all_to_all | solution.py:149
  639.5 165.9 %all-gather.5.cloned.1.call-done = bf16[1,6144,768]{2,1,0:T(8,128)(2,1)} async-done(((bf16[1,1536,768]{2,1,0:T(8,128)(2,1)}), bf16[1,6144,768]{2,1,0:T(8,128)(2,1)}) %all-gather.5.cloned.1.call-update) | async-done | bytes 9437200 | tf_op jit(solution)/shard_map/all_gather | solution.py:150
  805.4 25.8 %add_convert_fusion = bf16[6144,768]{1,0:T(8,128)(2,1)} fusion(f32[6144,768]{1,0:T(8,128)} %get-tuple-element.144, f32[6144,768]{1,0:T(8,128)} %get-tuple-element.165, bf16[1,6144,768]{2,1,0:T(8,128)(2,1)} %all-gather.5.cloned.1.call-done, bf16[1,768,768]{2,1,0:T(8,128)(2,1)} %param.40), kind=kOutput, calls=%fused_computation.10 | convolution fusion | flops 7313817600 | bytes 57802752 | tf_op jit(solution)/shard_map/erd,efd->erf/dot_general | solution.py:42
  831.1 13.4 fusion.23
  844.6 159.6 %reduce-scatter.5.cloned.1.call-done = bf16[1,1536,768]{2,1,0:T(8,128)(2,1)} async-done(((bf16[1,6144,768]{2,1,0:T(8,128)(2,1)}), bf16[1,1536,768]{2,1,0:T(8,128)(2,1)}) %reduce-scatter.5.cloned.1.call-update) | async-done | bytes 2359312 | tf_op jit(solution)/shard_map/reduce_scatter | solution.py:154
  1004.2 5.6 copy.132
  1009.8 25.5 %reduce.12 = bf16[1536,768]{1,0:T(8,128)(2,1)} reduce(bf16[1536,1,768]{2,1,0:T(2,128)(2,1)} %bitcast.205, bf16[]{:T(256)} %broadcast.614), dimensions={1}, to_apply=%bitcast.195.reduce_sub_computation | reduce | bytes 4718594
  1035.4 5.9 reshape.545
  1041.3 4.5 all-to-all-start.3
  1048.5 26.8 %all-to-all-done.3 = bf16[8,2,73728]{2,1,0:T(2,128)(2,1)} async-done(((bf16[8,2,73728]{2,1,0:T(2,128)(2,1)}), bf16[8,2,73728]{2,1,0:T(2,128)(2,1)}, u32[]{:S(2)}, u32[]{:S(2)}) %all-to-all-start.3) | async-done | bytes 2359328 | tf_op jit(solution)/shard_map/all_to_all | solution.py:157
  1075.3 7.5 reshape.546
  1082.8 5.5 fusion.29
  1102.1 4.0 fusion.98
  1106.1 7.0 multiply_reduce_fusion.1
  1113.1 7.0 multiply_convert_fusion.2
  1124.5 20.2 %multiply_reduce_fusion = (f32[12,512]{1,0:T(8,128)S(1)}, f32[12,512,1024]{2,1,0:T(8,128)}) fusion(f32[12,512]{1,0:T(8,128)S(1)} %copy-done.42, f32[12,512,1024]{2,1,0:T(8,128)} %get-tuple-element.160, pred[512,1024]{1,0:T(8,128)(4,1)S(1)} %copy-done.18, bf16[512,12,64]{0,2,1:T(8,128)(2,1)S(1)} %bitcast.224, bf16[1024,12,64]{0,2,1:T(8,128)(2,1)} %bitcast.216), kind=kOutput, calls=%fused_computation.2 | convolution fusion | flops 836757504 | bytes 53264384 | tf_op jit(solution)/shard_map/qhd,khd->hqk/dot_general | solution.py:188
  1144.7 12.1 fusion.66
  1156.8 22.1 %multiply_convert_fusion = bf16[12,512,1024]{2,1,0:T(8,128)(2,1)} fusion(f32[12,512,1024]{2,1,0:T(8,128)} %get-tuple-element.172, f32[12,512]{1,0:T(8,128)S(1)} %get-tuple-element.171, f32[12,512]{1,0:T(8,128)S(1)} %copy-done.42, f32[12,512,1024]{2,1,0:T(8,128)} %get-tuple-element.160, pred[512,1024]{1,0:T(8,128)(4,1)S(1)} %copy-done.18), kind=kLoop, calls=%fused_computation.1 | loop fusion | flops 37748736 | bytes 63488000 | tf_op jit(solution)/shard_map/convert_element_type | solution.py:192
  1178.9 8.6 fusion.103
  1187.6 7.0 fusion.67
  1196.3 7.0 fusion.81
  1203.4 14.4 %fusion.89 = f32[1,768,768]{2,1,0:T(8,128)} fusion(bf16[6144,768]{1,0:T(8,128)(2,1)} %copy-done.80, bf16[1,6144,768]{2,1,0:T(8,128)(2,1)} %all-gather.5.cloned.1.call-done), kind=kOutput, calls=%fused_computation.116 | convolution fusion | flops 7247757312 | bytes 21233664 | tf_op jit(solution)/shard_map/erf,erd->efd/dot_general | solution.py:41
  1217.8 14.3 %fusion.86 = f32[1,768,768]{2,1,0:T(8,128)} fusion(bf16[6144,768]{1,0:T(8,128)(2,1)} %add_convert_fusion, bf16[1,6144,768]{2,1,0:T(8,128)(2,1)} %all-gather.3.cloned.1.call-done), kind=kOutput, calls=%fused_computation.115 | convolution fusion | flops 7247757312 | bytes 21233664 | tf_op jit(solution)/shard_map/erd,erf->edf/dot_general | solution.py:45
  1234.6 9.1 fusion.153
  1243.7 3.7 copy.106
  1258.0 41.7 %all-reduce.2 = (f32[768]{0:T(1024)}, f32[768]{0:T(1024)}, f32[768]{0:T(1024)}, f32[768]{0:T(1024)}, f32[768,8]{0,1:T(8,128)}) all-reduce(f32[768]{0:T(1024)S(1)} %get-tuple-element.131, f32[768]{0:T(1024)S(1)} %get-tuple-element.173, f32[768]{0:T(1024)S(1)} %copy-done.68, ...), channel_id=1, replica_groups=mesh['wide'=8,'narrow'=4] {'wide','narrow'}, use_global_device_ids=true, to_apply=%region_22.23 | all-reduce | flops 9216 | bytes 73728 | tf_op jit(solution)/shard_map/psum | solution.py:229
  1299.7 95.0 %all-reduce.6.cloned.1.call-done = (f32[768,2304]{1,0:T(8,128)}, f32[768,768]{1,0:T(8,128)}) async-done(((f32[768,2304]{1,0:T(8,128)}, f32[768,768]{1,0:T(8,128)}), (f32[768,2304]{1,0:T(8,128)}, f32[768,768]{1,0:T(8,128)})) %all-reduce.6.cloned.1.call-update) | async-done | bytes 9437200 | tf_op jit(solution)/shard_map/psum | solution.py:229
  1394.7 6.4 fusion.148
  (242 shorter events, 85.4 us)
Async XLA Ops:
  7.2 292.0 %copy-start = (bf16[1,768,768]{2,1,0:T(8,128)(2,1)S(1)}, bf16[1,768,768]{2,1,0:T(8,128)(2,1)}, u32[]{:S(2)}) copy-start(bf16[1,768,768]{2,1,0:T(8,128)(2,1)} %param.39) | copy-start | bytes 3538948
  7.2 292.0 %all-gather.3.cloned.1.call-start = ((), (), s32[]{:S(2)}) async-start(), calls=%async_computation.6 | async-start | bytes 11796480 | tf_op jit(solution)/shard_map/all_gather | solution.py:124
  9.1 79.8 %copy-start.3 = (bf16[1,1024,768]{1,2,0:T(8,128)(2,1)}, bf16[1,1024,768]{1,2,0:T(8,128)(2,1)S(1)}, u32[]{:S(2)}) copy-start(bf16[1,1024,768]{1,2,0:T(8,128)(2,1)S(1)} %copy.90) | copy-start | bytes 4718596
  20.6 74.5 %copy-start.73 = (pred[1024]{0:T(1024)(128)(4,1)}, pred[1024]{0:T(1024)(128)(4,1)S(1)}, u32[]{:S(2)}) copy-start(pred[1024]{0:T(1024)(128)(4,1)S(1)} %iota_compare_fusion.7) | copy-start | bytes 3076
  23.5 71.6 %copy-start.71 = (s32[1024]{0:T(1024)}, s32[1024]{0:T(1024)S(1)}, u32[]{:S(2)}) copy-start(s32[1024]{0:T(1024)S(1)} %multiply_add_fusion) | copy-start | bytes 12292
  23.7 21.1 %copy-start.23 = (pred[512,512]{0,1:T(8,128)(4,1)}, pred[512,512]{0,1:T(8,128)(4,1)S(1)}, u32[]{:S(2)}) copy-start(pred[512,512]{0,1:T(8,128)(4,1)S(1)} %fusion.112) | copy-start | bytes 786436
  24.1 51.7 %copy-start.17 = (pred[512,1024]{1,0:T(8,128)(4,1)}, pred[512,1024]{1,0:T(8,128)(4,1)S(1)}, u32[]{:S(2)}) copy-start(pred[512,1024]{1,0:T(8,128)(4,1)S(1)} %fusion.80) | copy-start | bytes 1572868
  44.7 7.9 copy-start.45
  46.9 5.8 copy-start.15
  46.9 5.8 copy-start.20
  52.7 23.1 %copy-start.25 = (bf16[1024,768]{0,1:T(8,128)(2,1)S(1)}, bf16[1024,768]{0,1:T(8,128)(2,1)}, u32[]{:S(2)}) copy-start(bf16[1024,768]{0,1:T(8,128)(2,1)} %copy.95) | copy-start | bytes 4718596
  63.4 12.3 copy-start.40
  63.4 15.4 %copy-start.1 = (f32[12,512,1024]{2,1,0:T(8,128)S(1)}, f32[12,512,1024]{2,1,0:T(8,128)}, u32[]{:S(2)}) copy-start(f32[12,512,1024]{2,1,0:T(8,128)} %get-tuple-element.160) | copy-start | bytes 75497472
  75.7 11.6 copy-start.47
  88.9 5.7 copy-start.66
  88.9 5.7 copy-start.70
  132.9 219.2 %copy-start.75 = (bf16[1,768,768]{2,1,0:T(8,128)(2,1)S(1)}, bf16[1,768,768]{2,1,0:T(8,128)(2,1)}, u32[]{:S(2)}) copy-start(bf16[1,768,768]{2,1,0:T(8,128)(2,1)} %param.40) | copy-start | bytes 3538948
  132.9 388.3 %reduce-scatter.3.cloned.1.call-start = ((), (), s32[]{:S(2)}) async-start(), calls=%async_computation.7 | async-start | bytes 11796480 | tf_op jit(solution)/shard_map/reduce_scatter | solution.py:126
  554.8 7.3 copy-start.11
  554.8 7.3 copy-start.44
  554.8 7.3 copy-start.56
  554.8 34.0 %all-to-all-start.1 = ((bf16[8,2,73728]{2,1,0:T(2,128)(2,1)}), bf16[8,2,73728]{2,1,0:T(2,128)(2,1)}, u32[]{:S(2)}, u32[]{:S(2)}) async-start(bf16[8,2,73728]{2,1,0:T(2,128)(2,1)} %reshape.543), calls=%async_computation.2 | async-start | bytes 4718592 | tf_op jit(solution)/shard_map/all_to_all | solution.py:129
  559.3 246.1 %all-gather.5.cloned.1.call-start = ((), (), s32[]{:S(2)}) async-start(), calls=%async_computation.8 | async-start | bytes 11796480 | tf_op jit(solution)/shard_map/all_gather | solution.py:150
  562.4 33.3 %copy-start.72 = (s32[1024]{0:T(1024)S(1)}, s32[1024]{0:T(1024)}, u32[]{:S(2)}) copy-start(s32[1024]{0:T(1024)} %copy-done.71) | copy-start | bytes 12292
  562.5 33.3 %copy-start.74 = (pred[1024]{0:T(1024)(128)(4,1)S(1)}, pred[1024]{0:T(1024)(128)(4,1)}, u32[]{:S(2)}) copy-start(pred[1024]{0:T(1024)(128)(4,1)} %copy-done.73) | copy-start | bytes 3076
  595.8 7.5 copy-start.12
  639.4 364.8 %reduce-scatter.5.cloned.1.call-start = ((), (), s32[]{:S(2)}) async-start(), calls=%async_computation.9 | async-start | bytes 11796480 | tf_op jit(solution)/shard_map/reduce_scatter | solution.py:154
  1035.3 10.5 copy-start.39
  1035.3 10.5 copy-start.46
  1041.3 34.0 %all-to-all-start.3 = ((bf16[8,2,73728]{2,1,0:T(2,128)(2,1)}), bf16[8,2,73728]{2,1,0:T(2,128)(2,1)}, u32[]{:S(2)}, u32[]{:S(2)}) async-start(bf16[8,2,73728]{2,1,0:T(2,128)(2,1)} %reshape.545), calls=%async_computation.5 | async-start | bytes 4718592 | tf_op jit(solution)/shard_map/all_to_all | solution.py:157
  1045.8 348.9 %all-reduce.6.cloned.1.call-start = ((), (), s32[]{:S(2)}) async-start(), calls=%async_computation.10 | async-start | bytes 18874368 | tf_op jit(solution)/shard_map/psum | solution.py:229
  1082.8 5.5 copy-start.6
  1082.8 5.5 copy-start.52
  1082.8 5.5 copy-start.55
  1082.8 5.6 copy-start.67
  1113.1 7.1 copy-start.19
  1156.8 38.1 %copy-start.79 = (bf16[1024,12,64]{0,2,1:T(8,128)(2,1)}, bf16[1024,12,64]{0,2,1:T(8,128)(2,1)S(1)}, u32[]{:S(2)}) copy-start(bf16[1024,12,64]{0,2,1:T(8,128)(2,1)S(1)} %fusion.66) | copy-start | bytes 4718596
  1156.8 22.1 %copy-start.16 = (bf16[1024,768]{0,1:T(8,128)(2,1)S(1)}, bf16[1024,768]{0,1:T(8,128)(2,1)}, u32[]{:S(2)}) copy-start(bf16[1024,768]{0,1:T(8,128)(2,1)} %copy.97) | copy-start | bytes 4718596
  1178.9 8.7 copy-start.21
  1178.9 8.7 copy-start.26
  1187.6 8.7 copy-start.4
  1187.6 8.7 copy-start.50
  1187.6 8.7 copy-start.58
  1187.6 8.7 copy-start.64
  1187.6 8.7 copy-start.78
  1252.5 5.5 copy-start.68
  1252.5 5.5 copy-start.69
  1394.7 6.4 copy-start.30
  (43 other events, 123.6 us)
Sparse Core Ops, SparseCore 0:
  133.0 166.1 all-gather.2
  361.7 159.4 reduce-scatter.2
  639.5 165.7 all-gather.4
  844.7 159.4 reduce-scatter.4
  1203.5 191.1 all-reduce.5
where the time goes:
time: 1420 us; the launch traced here: 1410 us
  waiting for transfers between devices  800 us (56%)
  matrix products  271 us (19%)
  other arithmetic  110 us (8%)
  blocking collectives  109 us (8%)
  local copies, waits for them, and re-layouts  94.2 us (7%)
  between operations  15.9 us (1%)
    all_gather x1, waiting for transfers between devices, shards(): gathered = lax.all_gather(arrived, 'narrow', axis=1, tiled=True)  166 us
    all_gather x1, waiting for transfers between devices, shards(): grad_gathered = lax.all_gather(grad_arrived, 'narrow', axis=1, tiled=True)  166 us
    reduce_scatter x1, waiting for transfers between devices, shards(): lax.psum_scatter(partial_out.astype(jnp.bfloat16), 'narrow', scatter_dime...  160 us
    reduce_scatter x1, waiting for transfers between devices, shards(): lax.psum_scatter(grad_part.astype(jnp.bfloat16), 'narrow', scatter_dimens...  160 us
    psum x1, waiting for transfers between devices, shards(): lax.psum((grad_gain_one, grad_shift_one, grad_qkv_weight, grad_output_wei...  95 us
    unnamed x180, local copies, waits for them, and re-layouts  54.3 us
    unnamed x4, other arithmetic  49.7 us
    dot_general x1, matrix products, expert_forward(): jnp.einsum('erd,edf->erf', inputs, first_w, preferred_element_type=jnp.fl...  49.3 us
  transfers between devices with their start and end apart: 7, of which 7 were waited for; matrix products, arithmetic and copies ran while one was open for 4% of the time, Pallas kernels for 0%

commit v1 on v0

v1 whole, which is shorter than its diff:
```python
import functools
import jax
import jax.numpy as jnp
from jax import lax
from jax.experimental import pallas as pl
from jax.experimental.pallas import tpu as pltpu
from jax.sharding import PartitionSpec as P

F32 = jnp.float32
BF16 = jnp.bfloat16
HEADS = 12
EPSILON = 1e-05
MASKED_SCORE = -1000000000.0
PAIR = 128
QTILE = 256


def dot(left, right):
    return jnp.dot(left, right, preferred_element_type=F32)


def dot_tn(left, right):
    return lax.dot_general(left, right, (((0,), (0,)), ((), ())), preferred_element_type=F32)


def dot_nt(left, right):
    return lax.dot_general(left, right, (((1,), (1,)), ((), ())), preferred_element_type=F32)


def lanes_of(head, shape):
    lane = lax.broadcasted_iota(jnp.int32, shape, 1)
    return (lane >= head * (PAIR // 2)) & (lane < (head + 1) * (PAIR // 2))


def attend_kernel(scale, len_ref, q_ref, k_ref, v_ref, mixed_ref, logsum_ref):
    length = q_ref.shape[0]
    tile = min(QTILE, length)
    seq_len = len_ref[0]
    for at in range(length // tile):
        start, finish = at * tile, (at + 1) * tile
        query = q_ref[start:finish, :] * scale
        keys = k_ref[:finish, :]
        values = v_ref[:finish, :]
        key_pos = lax.broadcasted_iota(jnp.int32, (1, finish), 1)
        bias = jnp.where(key_pos < seq_len, 0.0, MASKED_SCORE)
        row = lax.broadcasted_iota(jnp.int32, (tile, tile), 0)
        col = lax.broadcasted_iota(jnp.int32, (tile, tile), 1)
        mixed = None
        for head in range(2):
            zero = jnp.zeros((), BF16)
            q_head = jnp.where(lanes_of(head, query.shape), query, zero)
            scores = dot_nt(q_head, keys) + bias
            last = jnp.where(col <= row, scores[:, start:], MASKED_SCORE)
            scores = last if start == 0 else jnp.concatenate([scores[:, :start], last], 1)
            highest = jnp.max(scores, 1, keepdims=True)
            expo = jnp.exp(scores - highest)
            total = jnp.sum(expo, 1, keepdims=True)
            v_head = jnp.where(lanes_of(head, values.shape), values, zero)
            part = dot(expo.astype(BF16), v_head) * (1.0 / total)
            mixed = part if mixed is None else mixed + part
            logsum = jnp.broadcast_to(highest + jnp.log(total), (tile, PAIR)).T
            logsum_ref[0, head : head + 1, start:finish] = logsum[:1]
        mixed_ref[start:finish, :] = mixed.astype(BF16)


def attend(projected, seq_lengths, heads, scale):
    length, width3 = projected.shape
    width = width3 // 3
    pairs = width // PAIR
    return pl.pallas_call(
        functools.partial(attend_kernel, scale),
        grid_spec=pltpu.PrefetchScalarGridSpec(
            num_scalar_prefetch=1,
            grid=(pairs,),
            in_specs=[
                pl.BlockSpec((length, PAIR), lambda i, s: (0, i)),
                pl.BlockSpec((length, PAIR), lambda i, s: (0, pairs + i)),
                pl.BlockSpec((length, PAIR), lambda i, s: (0, 2 * pairs + i)),
            ],
            out_specs=[
                pl.BlockSpec((length, PAIR), lambda i, s: (0, i)),
                pl.BlockSpec((1, 8, length), lambda i, s: (i, 0, 0)),
            ],
        ),
        out_shape=[
            jax.ShapeDtypeStruct((length, width), BF16),
            jax.ShapeDtypeStruct((pairs, 8, length), F32),
        ],
        compiler_params=pltpu.CompilerParams(vmem_limit_bytes=48 * 1024 * 1024),
        cost_estimate=pl.CostEstimate(
            flops=4 * length * length * width, bytes_accessed=8 * length * width, transcendentals=0
        ),
        name="attend",
    )(seq_lengths, projected, projected, projected)


def attend_back_kernel(
    scale, count, last, len_ref, q_ref, k_ref, v_ref, g_ref, logsum_ref, normed_ref, wq_ref, wk_ref,
    wv_ref, mixed_ref, attn_ref, *refs,
):
    if last:
        sum_ref, in_ref, gain_ref, resid_ref, weight_ref, out_ref, sums_ref = refs[:7]
        grads, normed_t, grad_normed = refs[7:]
    else:
        weight_ref, grad_normed, grads, normed_t = refs
    length = q_ref.shape[0]
    tile = min(QTILE, length)
    seq_len = len_ref[0]
    step = pl.program_id(0)

    @pl.when(step == 0)
    def _():
        for at in range(length // tile):
            normed_t[:, at * tile : (at + 1) * tile] = normed_ref[at * tile : (at + 1) * tile, :].T
        if last:
            grad_normed[...] = sum_ref[...]
        else:
            grad_normed[...] = jnp.zeros_like(grad_normed)

    @pl.when(step < count)
    def _():
        dk_sum = [None] * (length // tile)
        dv_sum = [None] * (length // tile)
        for at in range(length // tile):
            start, finish = at * tile, (at + 1) * tile
            query = q_ref[start:finish, :] * scale
            grad = g_ref[start:finish, :]
            keys = k_ref[:finish, :]
            values = v_ref[:finish, :]
            key_pos = lax.broadcasted_iota(jnp.int32, (finish, 1), 0)
            bias = jnp.where(key_pos < seq_len, 0.0, MASKED_SCORE)
            row = lax.broadcasted_iota(jnp.int32, (tile, tile), 0)
            col = lax.broadcasted_iota(jnp.int32, (tile, tile), 1)
            grad_query = None
            for head in range(2):
                zero = jnp.zeros((), BF16)
                q_head = jnp.where(lanes_of(head, query.shape), query, zero)
                g_head = jnp.where(lanes_of(head, query.shape), grad, zero)
                k_head = jnp.where(lanes_of(head, keys.shape), keys, zero)
                scores = dot_nt(keys, q_head) + bias
                diagonal = jnp.where(row <= col, scores[start:], MASKED_SCORE)
                scores = (
                    diagonal if start == 0 else jnp.concatenate([scores[:start], diagonal], 0)
                )
                probs = jnp.exp(scores - logsum_ref[0, head : head + 1, start:finish])
                grad_probs = dot_nt(values, g_head)
                product = probs * grad_probs
                centre = jnp.sum(product, 0, keepdims=True)
                grad_scores = (product - probs * centre).astype(BF16)
                dv = dot(probs.astype(BF16), g_head)
                dk = dot(grad_scores, q_head)
                for j in range(at + 1):
                    here = slice(j * tile, (j + 1) * tile)
                    dk_sum[j] = dk[here] if dk_sum[j] is None else dk_sum[j] + dk[here]
                    dv_sum[j] = dv[here] if dv_sum[j] is None else dv_sum[j] + dv[here]
                part = dot_tn(grad_scores, k_head)
                grad_query = part if grad_query is None else grad_query + part
            grads[start:finish, :PAIR] = (grad_query * scale).astype(BF16)
        for j in range(length // tile):
            here = slice(j * tile, (j + 1) * tile)
            grads[here, PAIR : 2 * PAIR] = dk_sum[j].astype(BF16)
            grads[here, 2 * PAIR :] = dv_sum[j].astype(BF16)
        weight_ref[...] = dot(normed_t[...], grads[...])
        weights = jnp.concatenate([wq_ref[...], wk_ref[...], wv_ref[...]], 1)
        for at in range(length // tile):
            here = slice(at * tile, (at + 1) * tile)
            grad_normed[here, :] += dot_nt(grads[here, :], weights)

    @pl.when(step == count)
    def _():
        weight_ref[...] = dot_tn(mixed_ref[...], attn_ref[...])
        if last:
            gain_sum, shift_sum = 0.0, 0.0
            for at in range(length // tile):
                here = slice(at * tile, (at + 1) * tile)
                grad = grad_normed[here, :]
                standard, back_norm = norm_back(in_ref[0, here, :].astype(F32), gain_ref[...], grad)
                out_ref[0, here, :] = (resid_ref[here, :] + back_norm).astype(BF16)
                gain_sum += jnp.sum(grad * standard, 0, keepdims=True)
                shift_sum += jnp.sum(grad, 0, keepdims=True)
            sums_ref[0:1, :] = gain_sum
            sums_ref[1:2, :] = shift_sum
            sums_ref[2:8, :] = jnp.zeros((6, sums_ref.shape[1]), F32)


def attend_back(
    projected, grad_mixed, logsum, seq_lengths, scale, part, count, normed, qkv, mixed, grad_attn,
    *more,
):
    length, width = normed.shape
    pairs = width // PAIR
    first = part * count
    last = part == 1
    block = (length, PAIR)
    columns = 3 * PAIR

    def at(i):
        return first + jnp.minimum(i, count - 1)

    wspec = pl.BlockSpec((width, PAIR), lambda i, s: (0, at(i)))
    wide = jax.ShapeDtypeStruct((length, width), F32)
    weight_shape = jax.ShapeDtypeStruct((width, (count + 1) * columns), F32)
    weight_spec = pl.BlockSpec((width, columns), lambda i, s: (0, i))
    in_specs = [
        pl.BlockSpec(block, lambda i, s: (0, at(i))),
        pl.BlockSpec(block, lambda i, s: (0, pairs + at(i))),
        pl.BlockSpec(block, lambda i, s: (0, 2 * pairs + at(i))),
        pl.BlockSpec(block, lambda i, s: (0, at(i))),
        pl.BlockSpec((1, 8, length), lambda i, s: (at(i), 0, 0)),
        whole((length, width)),
        wspec, wspec, wspec,
        whole((length, width)),
        pl.BlockSpec((length, columns), lambda i, s: (0, part), pipeline_mode=pl.Buffered(1)),
    ]
    scratch = [pltpu.VMEM((length, columns), BF16), pltpu.VMEM((width, length), BF16)]
    if last:
        in_specs += [
            whole((length, width)), whole((1, length, width)), whole((1, width)), whole((length, width)),
        ]
        out_specs = [weight_spec, whole((1, length, width)), whole((8, width))]
        out_shape = [
            weight_shape, jax.ShapeDtypeStruct((1, length, width), BF16),
            jax.ShapeDtypeStruct((8, width), F32),
        ]
        scratch += [pltpu.VMEM((length, width), F32)]
    else:
        out_specs = [weight_spec, whole((length, width))]
        out_shape = [weight_shape, wide]
    return pl.pallas_call(
        functools.partial(attend_back_kernel, scale, count, last),
        grid_spec=pltpu.PrefetchScalarGridSpec(
            num_scalar_prefetch=1,
            grid=(count + 1,),
            in_specs=in_specs,
            out_specs=out_specs,
            scratch_shapes=scratch,
        ),
        out_shape=out_shape,
        compiler_params=pltpu.CompilerParams(vmem_limit_bytes=58 * 1024 * 1024),
        cost_estimate=pl.CostEstimate(
            flops=20 * length * length * count * PAIR,
            bytes_accessed=14 * length * count * PAIR,
            transcendentals=0,
        ),
        name="attend_back",
    )(seq_lengths, projected, projected, projected, grad_mixed, logsum, normed, *qkv, mixed, grad_attn, *more)


ERFC = (0.254829592, -0.284496736, 1.421413741, -1.453152027, 1.061405429)
ERFC_RATE = 0.3275911 * 0.5**0.5
ROWS = 256


def gelu_pair(value):
    size = jnp.abs(value)
    t = 1.0 / (1.0 + ERFC_RATE * size)
    poly = t * (
        ERFC[0] + t * (ERFC[1] + t * (ERFC[2] + t * (ERFC[3] + t * ERFC[4])))
    )
    bell = jnp.exp(-0.5 * value * value)
    tail = 0.5 * poly * bell
    below = jnp.where(value < 0, tail, 1.0 - tail)
    return value * below, below + value * (bell * 0.3989422804014327)


def join_pieces(w_ref, w_all):
    pieces, unused, hidden, unused_width = w_ref.shape
    for p in range(pieces):
        for k in range(2):
            w_all[k, p * hidden : (p + 1) * hidden, :] = w_ref[p, k]


def expert_tile(x, g, w_all, active_ref, pre_ref, at):
    units = w_all.shape[1]
    chunk = units if units <= 512 else 512 if units % 512 == 0 else 384
    for start in range(0, units, chunk):
        cols = slice(start, start + chunk)
        active, slope = gelu_pair(dot_nt(x, w_all[0, cols, :]))
        active_ref[at, cols] = active.astype(BF16)
        pre_ref[at, cols] = (dot_nt(g, w_all[1, cols, :]) * slope).astype(BF16)
    return dot(active_ref[at, :], w_all[1]), dot(pre_ref[at, :], w_all[0])


def expert_first_kernel(
    tiles, x_ref, u_ref, cent_ref, w_ref, out_ref, in_ref, dw_ref, g_ref, xt_ref, gt_ref, gate_ref,
    active, grad_pre, w_all,
):
    rows = x_ref.shape[0]
    step = pl.program_id(0)

    @pl.when(step == 0)
    def _():
        join_pieces(w_ref, w_all)

    @pl.when(step < tiles)
    def _():
        at = pl.ds(pl.multiple_of(step * rows, rows), rows)
        x = x_ref[...]
        chosen = jnp.sum(x.astype(F32) * cent_ref[...], 1, keepdims=True)
        gate = 1.0 / (1.0 + jnp.exp(-chosen))
        gate_ref[...] = gate
        g = (gate * u_ref[...].astype(F32)).astype(BF16)
        g_ref[...] = g
        xt_ref[:, at] = x.T
        gt_ref[:, at] = g.T
        out_ref[...], in_ref[...] = expert_tile(x, g, w_all, active, grad_pre, at)

    @pl.when(step >= tiles)
    def _():
        hidden = dw_ref.shape[3]
        cols = pl.ds(pl.multiple_of((step - tiles) * hidden, hidden), hidden)
        dw_ref[0, 0] = dot(xt_ref[...], grad_pre[:, cols]).astype(BF16)
        dw_ref[0, 1] = dot(gt_ref[...], active[:, cols]).astype(BF16)


def expert_middle_kernel(
    x_ref, g_ref, out_in, in_in, w_ref, out_ref, in_ref, active_ref, pre_ref, w_all
):
    @pl.when(pl.program_id(0) == 0)
    def _():
        join_pieces(w_ref, w_all)

    out, grad_in = expert_tile(x_ref[...], g_ref[...], w_all, active_ref, pre_ref, slice(None))
    out_ref[...] = out_in[...] + out
    in_ref[...] = in_in[...] + grad_in


def expert_last_kernel(
    x_ref, g_ref, u_ref, gate_ref, cent_ref, out_in, in_in, w_ref,
    low_ref, back_ref, cent_grad_ref, active_ref, pre_ref, w_all,
):
    @pl.when(pl.program_id(0) == 0)
    def _():
        join_pieces(w_ref, w_all)
        cent_grad_ref[...] = jnp.zeros_like(cent_grad_ref)

    x = x_ref[...]
    out, grad_in = expert_tile(x, g_ref[...], w_all, active_ref, pre_ref, slice(None))
    low = (out_in[...] + out).astype(BF16)
    low_ref[...] = low
    gate = gate_ref[...]
    chosen = jnp.sum(u_ref[...].astype(F32) * low.astype(F32), 1, keepdims=True)
    chosen = chosen * gate * (1.0 - gate)
    back_ref[...] = (in_in[...] + grad_in + chosen * cent_ref[...]).astype(BF16)
    cent_grad_ref[...] += jnp.sum(chosen * x.astype(F32), 0, keepdims=True)


def expert_weights_kernel(xt_ref, gt_ref, active_one, pre_one, active_two, pre_two, dw_ref):
    grad_pre = jnp.concatenate([pre_one[...], pre_two[...]], 1)
    active = jnp.concatenate([active_one[...], active_two[...]], 1)
    dw_ref[0, 0] = dot(xt_ref[...], grad_pre).astype(BF16)
    dw_ref[0, 1] = dot(gt_ref[...], active).astype(BF16)


def whole(shape):
    return pl.BlockSpec(shape, lambda *i: (0,) * len(shape), pipeline_mode=pl.Buffered(1))


EXPERT_PARAMS = pltpu.CompilerParams(vmem_limit_bytes=58 * 1024 * 1024)


def expert_cost(kind, rows, width, hidden, pieces):
    return pl.CostEstimate(
        flops=2 * kind * rows * width * hidden * pieces,
        bytes_accessed=6 * rows * width * 4,
        transcendentals=0,
    )


def expert_first(x, u, cent, w):
    rows, width = x.shape
    pieces, unused, hidden, unused_width = w.shape
    tile = min(ROWS, rows)
    tiles = rows // tile
    units = pieces * hidden

    def tiled(cols):
        return pl.BlockSpec((tile, cols), lambda i: (jnp.minimum(i, tiles - 1), 0))

    wide = jax.ShapeDtypeStruct((rows, width), F32)
    turned = jax.ShapeDtypeStruct((width, rows), BF16)
    return pl.pallas_call(
        functools.partial(expert_first_kernel, tiles),
        grid=(tiles + pieces,),
        in_specs=[tiled(width), tiled(width), whole((1, width)), whole(w.shape)],
        out_specs=[
            tiled(width), tiled(width),
            pl.BlockSpec((1, 2, width, hidden), lambda i: (jnp.maximum(i - tiles, 0), 0, 0, 0)),
            tiled(width), whole(turned.shape), whole(turned.shape), tiled(1),
        ],
        out_shape=[
            wide, wide, jax.ShapeDtypeStruct((pieces, 2, width, hidden), BF16),
            jax.ShapeDtypeStruct((rows, width), BF16), turned, turned,
            jax.ShapeDtypeStruct((rows, 1), F32),
        ],
        scratch_shapes=[
            pltpu.VMEM((rows, units), BF16), pltpu.VMEM((rows, units), BF16),
            pltpu.VMEM((2, units, width), BF16),
        ],
        compiler_params=EXPERT_PARAMS,
        cost_estimate=expert_cost(6, rows, width, hidden, pieces),
        name="expert_first",
    )(x, u, cent, w)


def expert_middle(x, g, out_sum, in_sum, w):
    rows, width = x.shape
    pieces, unused, hidden, unused_width = w.shape
    tile = min(ROWS, rows)
    units = pieces * hidden

    def tiled(cols):
        return pl.BlockSpec((tile, cols), lambda i: (i, 0))

    wide = jax.ShapeDtypeStruct((rows, width), F32)
    kept = jax.ShapeDtypeStruct((rows, units), BF16)
    return pl.pallas_call(
        expert_middle_kernel,
        grid=(rows // tile,),
        in_specs=[tiled(width)] * 4 + [whole(w.shape)],
        out_specs=[tiled(width), tiled(width), tiled(units), tiled(units)],
        out_shape=[wide, wide, kept, kept],
        scratch_shapes=[pltpu.VMEM((2, units, width), BF16)],
        compiler_params=EXPERT_PARAMS,
        cost_estimate=expert_cost(4, rows, width, hidden, pieces),
        name="expert_middle",
    )(x, g, out_sum, in_sum, w)


def expert_last(x, g, u, gate, cent, out_sum, in_sum, w):
    rows, width = x.shape
    pieces, unused, hidden, unused_width = w.shape
    tile = min(ROWS, rows)
    units = pieces * hidden

    def tiled(cols):
        return pl.BlockSpec((tile, cols), lambda i: (i, 0))

    low = jax.ShapeDtypeStruct((rows, width), BF16)
    kept = jax.ShapeDtypeStruct((rows, units), BF16)
    return pl.pallas_call(
        expert_last_kernel,
        grid=(rows // tile,),
        in_specs=[tiled(width)] * 3
        + [tiled(1), whole((1, width)), tiled(width), tiled(width), whole(w.shape)],
        out_specs=[tiled(width), tiled(width), whole((1, width)), tiled(units), tiled(units)],
        out_shape=[low, low, jax.ShapeDtypeStruct((1, width), F32), kept, kept],
        scratch_shapes=[pltpu.VMEM((2, units, width), BF16)],
        compiler_params=EXPERT_PARAMS,
        cost_estimate=expert_cost(4, rows, width, hidden, pieces),
        name="expert_last",
    )(x, g, u, gate, cent, out_sum, in_sum, w)


def expert_weights(xt, gt, one, two, pieces):
    width, rows = xt.shape
    cols = [pair[0].shape[1] // pieces for pair in (one, two)]
    specs = [pl.BlockSpec((rows, c), lambda i: (0, i)) for c in cols for _ in range(2)]
    shape = (pieces, 2, width, sum(cols))
    return pl.pallas_call(
        expert_weights_kernel,
        grid=(pieces,),
        in_specs=[whole(xt.shape), whole(xt.shape), *specs],
        out_specs=pl.BlockSpec((1, *shape[1:]), lambda i: (i, 0, 0, 0)),
        out_shape=jax.ShapeDtypeStruct(shape, BF16),
        compiler_params=EXPERT_PARAMS,
        cost_estimate=expert_cost(2, rows, width, sum(cols), pieces),
        name="expert_weights",
    )(xt, gt, *one, *two)


def norm_back(values, gain, grad):
    centre = jnp.mean(values, -1, keepdims=True)
    centered = values - centre
    spread = jnp.mean(centered * centered, -1, keepdims=True)
    rate = lax.rsqrt(spread + EPSILON)
    standard = centered * rate
    u = grad * gain
    back = rate * (
        u - jnp.mean(u, -1, keepdims=True) - standard * jnp.mean(u * standard, -1, keepdims=True)
    )
    return standard, back


def combine_back_kernel(
    back_ref, target_ref, resid_ref, cot_ref, gain_ref, weight_ref,
    resid_grad_ref, attn_ref, mixed_grad_ref, sums_ref,
):
    @pl.when(pl.program_id(0) == 0)
    def _():
        sums_ref[...] = jnp.zeros_like(sums_ref)

    target = target_ref[...]
    slots = lax.broadcasted_iota(jnp.int32, (1, back_ref.shape[0]), 1)
    grad = dot((target == slots).astype(BF16), back_ref[...])
    standard, back_norm = norm_back(resid_ref[...], gain_ref[...], grad)
    upstream = jnp.where(target >= 0, cot_ref[...].astype(F32), 0.0)
    grad_resid = upstream + back_norm
    resid_grad_ref[...] = grad_resid
    low = grad_resid.astype(BF16)
    attn_ref[...] = low
    mixed_grad_ref[...] = dot_nt(low, weight_ref[...]).astype(BF16)
    sums_ref[0:1, :] += jnp.sum(grad * standard, 0, keepdims=True)
    sums_ref[1:2, :] += jnp.sum(grad, 0, keepdims=True)


def combine_back(back, target, resid, cot, gain, weight):
    length, width = resid.shape
    tile = min(QTILE, length)
    tiled = pl.BlockSpec((tile, width), lambda i: (i, 0))
    low = jax.ShapeDtypeStruct(resid.shape, BF16)
    return pl.pallas_call(
        combine_back_kernel,
        grid=(length // tile,),
        in_specs=[
            whole(back.shape), pl.BlockSpec((tile, 1), lambda i: (i, 0)), tiled, tiled,
            whole((1, width)), whole(weight.shape),
        ],
        out_specs=[tiled, tiled, tiled, whole((8, width))],
        out_shape=[
            jax.ShapeDtypeStruct(resid.shape, F32), low, low, jax.ShapeDtypeStruct((8, width), F32),
        ],
        compiler_params=EXPERT_PARAMS,
        cost_estimate=pl.CostEstimate(
            flops=2 * length * width * (back.shape[0] + width),
            bytes_accessed=20 * length * width,
            transcendentals=0,
        ),
        name="combine_back",
    )(back, target, resid, cot, gain.reshape(1, width), weight)


def spread_kernel(count, flag_ref, *refs):
    sources, (query_ref, key_ref, value_ref, output_ref) = refs[:8], refs[8:]
    step = pl.program_id(0)
    half = query_ref.shape[0] // 2
    for part in range(2):
        mine, other, mine_more, other_more = sources[4 * part : 4 * part + 4]

        @pl.when((step >= part * count) & (step < (part + 1) * count))
        def _():
            for i, (at, left, right) in enumerate(
                [(query_ref, mine, other), (key_ref, mine, other), (value_ref, mine, other)]
                + [(output_ref, mine_more, other_more)]
            ):
                cols = slice(i * PAIR, (i + 1) * PAIR) if i < 3 else slice(None)
                low, high = left[:, cols].astype(F32), right[:, cols].astype(F32)
                at[:half, :] = jnp.where(flag_ref[0] == 0, low, high)
                at[half:, :] = jnp.where(flag_ref[0] == 0, high, low)


def spread(flag, halves, width):
    pairs = width // PAIR
    count = pairs // 2
    half = width // 2
    operands, specs = [], []
    for part, (mine, other) in enumerate(halves):

        def at(i, part=part):
            return jnp.clip(i - part * count, 0, count - 1)

        operands += [mine, other, mine, other]
        specs += [pl.BlockSpec((half, 3 * PAIR), lambda i, s, at=at: (0, at(i)))] * 2
        specs += [pl.BlockSpec((half, PAIR), lambda i, s, at=at: (0, 3 * count + at(i)))] * 2
    out = jax.ShapeDtypeStruct((width, width), F32)
    return pl.pallas_call(
        functools.partial(spread_kernel, count),
        grid_spec=pltpu.PrefetchScalarGridSpec(
            num_scalar_prefetch=1,
            grid=(pairs,),
            in_specs=specs,
            out_specs=[pl.BlockSpec((width, PAIR), lambda i, s: (0, i))] * 4,
        ),
        out_shape=[out] * 4,
        compiler_params=EXPERT_PARAMS,
        name="spread",
    )(flag, *operands)


def normalize(values, gain, shift):
    centre = jnp.mean(values, -1, keepdims=True)
    centered = values - centre
    spread = jnp.mean(centered * centered, -1, keepdims=True)
    return centered * lax.rsqrt(spread + EPSILON) * gain + shift


def xor_pairs(size, flip):
    return [(i, i ^ flip) for i in range(size)]


def exchange(rows, blocks):
    shape = rows.shape
    return lax.all_to_all(
        rows.reshape(blocks, -1, shape[1]), "wide", split_axis=0, concat_axis=0, tiled=True
    ).reshape(shape)


def reduce_halves(parts, sizes, bits):
    flags = []
    for axis, flip in bits:
        flag = (lax.axis_index(axis) // flip) % 2
        half = parts[0].shape[0] // 2
        mine = [lax.dynamic_slice_in_dim(p, flag * half, half, 0) for p in parts]
        theirs = [lax.dynamic_slice_in_dim(p, (1 - flag) * half, half, 0) for p in parts]
        if len(parts) > 1:
            mine, theirs = [jnp.concatenate(mine, 1)], [jnp.concatenate(theirs, 1)]
        came = lax.ppermute(theirs[0].astype(BF16), axis, xor_pairs(sizes[axis], flip))
        parts = [mine[0] + came.astype(F32)]
        flags.append(flag)
    return parts[0].astype(BF16), flags


def gather_halves(total, flags, sizes, bits, stop):
    for at in reversed(range(stop, len(bits))):
        axis, flip = bits[at]
        other = lax.ppermute(total, axis, xor_pairs(sizes[axis], flip))
        if at == 0:
            return total, other
        total = jnp.where(
            flags[at] == 0, jnp.concatenate([total, other], 0), jnp.concatenate([other, total], 0)
        )
    return total


def make_shards(n_wide, n_narrow):
    sizes = {"wide": n_wide, "narrow": n_narrow}
    wide_bits = [("wide", 1 << i) for i in range(n_wide.bit_length() - 1)]
    narrow_bits = [("narrow", 1 << i) for i in range(n_narrow.bit_length() - 1)]
    orders = [
        wide_bits + narrow_bits,
        wide_bits[:1] + wide_bits[2:] + wide_bits[1:2] + narrow_bits,
    ]

    def shards(
        block_in,
        seq_lengths,
        routes,
        first_gain,
        first_shift,
        query_weight,
        key_weight,
        value_weight,
        output_weight,
        second_gain,
        second_shift,
        centroids,
        hidden_weight,
        down_weight,
        cotangent,
    ):
        seqs_here, length, width = block_in.shape
        head_size = width // HEADS
        scale = head_size ** (-0.5)
        tokens = seqs_here * length
        experts_all = centroids.shape[1]
        capacity = 3 * tokens // (2 * experts_all)
        wide_here = lax.axis_index("wide")
        hidden_size = hidden_weight.shape[2]

        third = max(hidden_size // 6 // 128 * 128, 128)
        second = max(hidden_size // 3 // 128 * 128, 128)
        cuts = (0, hidden_size - second - third, hidden_size - third, hidden_size)
        hidden_t = hidden_weight[0].T
        packs = [
            jnp.stack([hidden_t[a:b], down_weight[0, a:b]], 0)[None]
            for a, b in zip(cuts, cuts[1:])
        ]
        weights = [lax.all_gather(pack, "narrow", axis=0, tiled=True) for pack in packs]

        live = lax.broadcasted_iota(jnp.int32, (tokens,), 0) < seq_lengths[0]
        route = routes.reshape(tokens)
        expert_ids = lax.broadcasted_iota(jnp.int32, (tokens, experts_all), 1)
        picked = route[:, None] == expert_ids
        ones_live = (picked & live[:, None]).astype(jnp.int32)
        earlier = jnp.cumsum(ones_live, 0, dtype=jnp.int32) - ones_live
        slot = jnp.sum(earlier * ones_live, 1, dtype=jnp.int32)
        target = route * capacity + slot
        slot_ids = lax.broadcasted_iota(jnp.int32, (tokens, experts_all * capacity), 1)
        target = jnp.where(live, target, -1)[:, None]
        table = (target == slot_ids).astype(BF16)
        cot = cotangent.reshape(tokens, width)

        def to_slots(rows):
            return dot_tn(table, rows).astype(BF16)

        upstream_slots, block_in, *packs = lax.optimization_barrier(
            (to_slots(cot), block_in, *packs)
        )
        upstream_rows = exchange(upstream_slots, experts_all)

        qkv_weight = jnp.concatenate([query_weight, key_weight, value_weight], 1)
        inputs_wide = block_in.reshape(tokens, width).astype(F32)
        normed_low = normalize(inputs_wide, first_gain, first_shift).astype(BF16)
        projected = dot(normed_low, qkv_weight).astype(BF16)
        mixed, logsum = attend(projected, seq_lengths, HEADS, scale)
        mixed, upstream_rows = lax.optimization_barrier((mixed, upstream_rows))
        resid = inputs_wide + dot(mixed, output_weight)
        normed_second = normalize(resid, second_gain, second_shift).astype(BF16)

        rows = exchange(to_slots(normed_second), experts_all)
        own_centroid = lax.dynamic_slice_in_dim(centroids.T, wide_here, 1, 0).astype(F32)
        out_sum, in_sum, weight_grads, grad_rows, rows_t, grad_rows_t, row_gate = expert_first(
            rows, upstream_rows, own_centroid, weights[0]
        )
        out_sum, in_sum, *kept_one = expert_middle(rows, grad_rows, out_sum, in_sum, weights[1])
        out_low, back_rows, own_centroid_grad, *kept_two = expert_last(
            rows, grad_rows, upstream_rows, row_gate, own_centroid, out_sum, in_sum, weights[2]
        )
        back = exchange(back_rows, experts_all)
        more_weight_grads = expert_weights(rows_t, grad_rows_t, kept_one, kept_two, n_narrow)
        grad_resid, grad_attn, grad_mixed, second_sums = combine_back(
            back, target, resid, cot, second_gain, output_weight
        )
        out_low, more_weight_grads, grad_mixed = lax.optimization_barrier(
            (out_low, more_weight_grads, grad_mixed)
        )
        returned = exchange(out_low, experts_all)

        qkv = (query_weight, key_weight, value_weight)
        count = width // PAIR // 2
        shared = (normed_low, qkv, mixed, grad_attn)
        part_one, grad_normed = attend_back(
            projected, grad_mixed, logsum, seq_lengths, scale, 0, count, *shared
        )
        grad_normed, returned = lax.optimization_barrier((grad_normed, returned))
        part_two, input_grad, first_sums = attend_back(
            projected, grad_mixed, logsum, seq_lengths, scale, 1, count, *shared,
            grad_normed, block_in, first_gain.reshape(1, width), grad_resid,
        )
        own_column = expert_ids[:1].reshape(experts_all, 1) == wide_here
        small = jnp.concatenate(
            [jnp.where(own_column, own_centroid_grad, 0.0), second_sums[:2], first_sums[:2]], 0
        )
        small = jnp.pad(small, ((0, -small.shape[0] % 128), (0, 0))).T
        expert_rows_here = dot(table, returned)
        logits = dot(normed_second, centroids)
        gate = jax.nn.sigmoid(jnp.sum(jnp.where(picked, logits, 0.0), 1, keepdims=True))
        block_out = (resid + gate * expert_rows_here).astype(BF16).reshape(block_in.shape)

        first_summed = lax.psum_scatter(weight_grads, "narrow", scatter_dimension=0, tiled=True)
        last_summed = lax.psum_scatter(more_weight_grads, "narrow", scatter_dimension=0, tiled=True)
        summed = [first_summed[0], last_summed[0]]
        hidden_grad = jnp.concatenate([s[0] for s in summed], 1).astype(F32)[None]
        down_grad = jnp.concatenate([s[1] for s in summed], 1).T.astype(F32)[None]

        totals = [
            reduce_halves(parts, sizes, order)
            for parts, order in zip(([part_one], [part_two, small]), orders)
        ]
        flag = totals[0][1][0]
        near = [
            gather_halves(total, flags, sizes, order, len(order) - len(narrow_bits))
            for (total, flags), order in zip(totals, orders)
        ]
        near[0], block_out = lax.optimization_barrier((near[0], block_out))
        near[1], hidden_grad, down_grad = lax.optimization_barrier((near[1], hidden_grad, down_grad))
        halves = [
            gather_halves(total, flags, sizes, order[: len(order) - len(narrow_bits)], 0)
            for total, (unused_total, flags), order in zip(near, totals, orders)
        ]
        query_grad, key_grad, value_grad, output_weight_grad = spread(
            flag.reshape(1), halves, width
        )
        low, high = [h[:, part_two.shape[1] :].astype(F32) for h in halves[1]]
        small = jnp.where(flag == 0, jnp.concatenate([low, high], 0), jnp.concatenate([high, low], 0))
        centroids_grad = small[:, :experts_all]
        second_gain_grad, second_shift_grad, first_gain_grad, first_shift_grad = [
            small[:, experts_all + i] for i in range(4)
        ]

        return (
            block_out,
            input_grad,
            first_gain_grad,
            first_shift_grad,
            query_grad,
            key_grad,
            value_grad,
            output_weight_grad,
            second_gain_grad,
            second_shift_grad,
            centroids_grad,
            hidden_grad,
            down_grad,
        )

    return shards


def solution(mesh):
    tokens_spec = P(("wide", "narrow"), None, None)
    in_specs = (
        tokens_spec,
        P(("wide", "narrow")),
        tokens_spec,
        *[P()] * 9,
        P("wide", None, "narrow"),
        P("wide", "narrow", None),
        tokens_spec,
    )
    out_specs = (
        tokens_spec,
        tokens_spec,
        *[P()] * 9,
        P("wide", None, "narrow"),
        P("wide", "narrow", None),
    )
    return jax.shard_map(
        make_shards(mesh.shape["wide"], mesh.shape["narrow"]),
        mesh=mesh,
        in_specs=in_specs,
        out_specs=out_specs,
        check_vma=False,
    )
```

time: 1420 us -> 470 us (0.33)
  waiting for transfers between devices: 800 us -> 164 us
  matrix products: 271 us -> 26.8 us
  Pallas kernels: 0 us -> 181 us
  blocking collectives: 109 us -> 0 us
  other arithmetic: 110 us -> 18.2 us
  local copies, waits for them, and re-layouts: 94.2 us -> 24.5 us
  starting transfers between devices: 9.2 us -> 35.1 us
    reduce_scatter x2, waiting for transfers between devices: 319 us -> 0.04 us  [the longest x1 0.02 us: shards(): lax.psum_scatter(weight_grads, 'narrow', scatter_dimension=0, tiled=True)]
    all_gather x2 -> x3, waiting for transfers between devices: 332 us -> 45.4 us  [shards(): lax.all_gather(pack, 'narrow', axis=0, tiled=True)]
    dot_general x31 -> x6, matrix products: 271 us -> 26.8 us  [the longest x4 15.9 us: dot(): return jnp.dot(left, right, preferred_element_type=F32)]
    pallas_call x0 -> x9, Pallas kernels: none -> 181 us  [the longest x2 56.2 us: attend_back(): pl.pallas_call(functools.partial(attend_back_kernel, scale, count, last),...]
    psum x1 -> x0, waiting for transfers between devices: 95 us -> none  [shards(): lax.psum((grad_gain_one, grad_shift_one, grad_qkv_weight, grad_output_wei...]
    ppermute x0 -> x20, waiting for transfers between devices: none -> 79.7 us  [the longest x10 48.7 us: reduce_halves(): lax.ppermute(theirs[0].astype(BF16), axis, xor_pairs(sizes[axis], flip))]
    all_to_all x2 -> x0, blocking collectives: 67.1 us -> none  [the longest x1 34.5 us: shards(): lax.all_to_all(dispatched, 'wide', split_axis=0, concat_axis=1, tiled=True)]
    unnamed x4 -> x2, other arithmetic: 49.7 us -> 0.08 us
  transfers between devices with their start and end apart: 7 -> 29, of which waited for: 7 -> 17; matrix products, arithmetic and copies ran while one was open for 4% -> 13% of each run, Pallas kernels for 0% -> 37%
where the time goes in v1:
time: 470 us; the launch traced here: 465 us
  Pallas kernels  181 us (39%)
  waiting for transfers between devices  164 us (35%)
  starting transfers between devices  35.1 us (7%)
  matrix products  26.8 us (6%)
  local copies, waits for them, and re-layouts  24.5 us (5%)
  other arithmetic  18.2 us (4%)
  between operations  15.7 us (3%)
    pallas_call x2, Pallas kernels, attend_back(): pl.pallas_call(functools.partial(attend_back_kernel, scale, count, last),...  56.2 us
    ppermute x10, waiting for transfers between devices, reduce_halves(): lax.ppermute(theirs[0].astype(BF16), axis, xor_pairs(sizes[axis], flip))  48.7 us
    all_gather x3, waiting for transfers between devices, shards(): lax.all_gather(pack, 'narrow', axis=0, tiled=True)  45.4 us
    all_to_all x4, waiting for transfers between devices, exchange(): lax.all_to_all(rows.reshape(blocks, -1, shape[1]), 'wide', split_axis=0,...  39 us
    pallas_call x1, Pallas kernels, expert_first(): pl.pallas_call(functools.partial(expert_first_kernel, tiles), grid=(tiles...  37.5 us
    ppermute x10, waiting for transfers between devices, gather_halves(): other = lax.ppermute(total, axis, xor_pairs(sizes[axis], flip))  30.9 us
    pallas_call x1, Pallas kernels, attend(): pl.pallas_call(functools.partial(attend_kernel, scale), grid_spec=pltpu.P...  22.1 us
    pallas_call x1, Pallas kernels, expert_middle(): pl.pallas_call(expert_middle_kernel, grid=(rows // tile,), in_specs=[tile...  18.6 us
  transfers between devices with their start and end apart: 29, of which 17 were waited for; matrix products, arithmetic and copies ran while one was open for 13% of the time, Pallas kernels for 37%

profile of v1, /device:TPU:0, one launch (start us, length us, event | category | flops | bytes accessed | tf_op | source)
XLA Modules:
  0.0 465.4 jit_solution(17746529111852036588)
XLA Ops:
  7.2 1.6 copy.43
  10.9 2.3 reduce-window.6
  13.8 6.1 %fusion.12 = bf16[1536,768]{1,0:T(8,128)(2,1)} fusion(s32[1024]{0:T(1024)S(1)} %add_select_fusion.1, bf16[1,1024,768]{2,1,0:T(8,128)(2,1)} %param.29), kind=kOutput, calls=%fused_computation.16 | convolution fusion | flops 2418671616 | bytes 3936256 | tf_op jit(solution)/shard_map/dot_general | solution.py:23
  19.9 5.3 %all-to-all-start = ((bf16[8,192,768]{2,1,0:T(8,128)(2,1)}), bf16[8,192,768]{2,1,0:T(8,128)(2,1)}, u32[]{:S(2)}, u32[]{:S(2)}) async-start(bf16[8,192,768]{2,1,0:T(8,128)(2,1)} %bitcast.117), calls=%async_computation | async-start | bytes 4718592 | tf_op jit(solution)/shard_map/all_to_all | solution.py:593
  29.3 6.2 %convolution_convert_fusion.q_ref.k_ref.v_ref = bf16[1024,2304]{1,0:T(8,128)(2,1)} fusion(bf16[1024,768]{1,0:T(8,128)(2,1)S(1)} %fusion.17.normed_ref, bf16[768,768]{1,0:T(8,128)(2,1)S(1)} %copy-done.13, bf16[768,768]{1,0:T(8,128)(2,1)S(1)} %copy-done.14, bf16[768,768]{1,0:T(8,128)(2,1)S(1)} %copy-done.15), kind=kOutput, calls=%fused_computation.4 | convolution fusion | flops 3636854784 | bytes 9830400 | tf_op jit(solution)/shard_map/dot_general | solution.py:19
  35.5 22.1 %attend.1 = (bf16[1024,768]{1,0:T(8,128)(2,1)S(1)}, f32[6,8,1024]{2,1,0:T(8,128)S(1)}) custom-call(s32[1]{0:T(128)} %copy.52.len_ref, bf16[1024,2304]{1,0:T(8,128)(2,1)} %convolution_convert_fusion.q_ref.k_ref.v_ref, bf16[1024,2304]{1,0:T(8,128)(2,1)} %convolution_convert_fusion.q_ref.k_ref.v_ref, bf16[1024,2304]{1,0:T(8,128)(2,1)} %convolution_convert_fusion.q_ref.k_ref.v_ref), custom_call_target="tpu_custom_call" | custom-call | flops 3221225472 | bytes 6291456 | tf_op jit(solution)/shard_map/attend/pallas_call | solution.py:70
  58.3 3.4 fusion.36
  63.4 4.8 %fusion.13 = bf16[1536,768]{1,0:T(8,128)(2,1)} fusion(bf16[1024,768]{1,0:T(8,128)(2,1)S(1)} %add_convert_fusion.1, s32[1024]{0:T(1024)S(1)} %add_select_fusion.1), kind=kOutput, calls=%fused_computation.17 | convolution fusion | flops 2418671616 | bytes 3936256 | tf_op jit(solution)/shard_map/dot_general | solution.py:23
  68.1 4.5 all-to-all-start.1
  75.6 26.5 %all-to-all-done.1 = bf16[8,192,768]{2,1,0:T(8,128)(2,1)S(1)} async-done(((bf16[8,192,768]{2,1,0:T(8,128)(2,1)}), bf16[8,192,768]{2,1,0:T(8,128)(2,1)S(1)}, u32[]{:S(2)}, u32[]{:S(2)}) %all-to-all-start.1) | async-done | bytes 2359328 | tf_op jit(solution)/shard_map/all_to_all | solution.py:593
  103.5 37.5 %expert_first.1 = (f32[1536,768]{1,0:T(8,128)}, f32[1536,768]{1,0:T(8,128)}, bf16[4,2,768,384]{3,2,1,0:T(8,128)(2,1)}, bf16[1536,768]{1,0:T(8,128)(2,1)}, bf16[7...) custom-call(bf16[1536,768]{1,0:T(8,128)(2,1)} %bitcast.105, bf16[1536,768]{1,0:T(8,128)(2,1)} %bitcast.7.u_ref, ...), custom_call_target="tpu_custom_call" | custom-call | flops 21743271936 | bytes 28311552 | tf_op jit(solution)/shard_map/expert_first/pallas_call | solution.py:382
  141.0 25.6 %all-gather.9.cloned.1.call-done = bf16[8,256,768]{2,1,0:T(8,128)(2,1)} async-done(((bf16[2,256,768]{2,1,0:T(8,128)(2,1)}), bf16[8,256,768]{2,1,0:T(8,128)(2,1)}) %all-gather.9.cloned.1.call-update) | async-done | bytes 3145744 | tf_op jit(solution)/shard_map/all_gather | solution.py:668
  166.6 18.6 %expert_middle.1 = (f32[1536,768]{1,0:T(8,128)}, f32[1536,768]{1,0:T(8,128)}, bf16[1536,1024]{1,0:T(8,128)(2,1)}, bf16[1536,1024]{1,0:T(8,128)(2,1)}) custom-call(bf16[1536,768]{1,0:T(8,128)(2,1)} %bitcast.106, bf16[1536,768]{1,0:T(8,128)(2,1)} %get-tuple-element.63.g_ref, f32[1536,768]{1,0:T(8,128)} %get-tuple-element.65.out_in, ...), custom_call_target="tpu_custom_call" | custom-call | flops 9663676416 | bytes 28311552 | tf_op jit(solution)/shard_map/expert_middle/pallas_call | solution.py:417
  185.2 19.4 %all-gather.11.cloned.1.call-done = bf16[8,128,768]{2,1,0:T(8,128)(2,1)} async-done(((bf16[2,128,768]{2,1,0:T(8,128)(2,1)}), bf16[8,128,768]{2,1,0:T(8,128)(2,1)}) %all-gather.11.cloned.1.call-update) | async-done | bytes 1572880 | tf_op jit(solution)/shard_map/all_gather | solution.py:668
  204.5 14.1 %expert_last.1 = (bf16[1536,768]{1,0:T(8,128)(2,1)}, bf16[1536,768]{1,0:T(8,128)(2,1)}, f32[1,768]{1,0:T(1,128)}, bf16[1536,512]{1,0:T(8,128)(2,1)}, bf16[1536,512]{1,0:T(8,128)(2,1)}) custom-call(bf16[1536,768]{1,0:T(8,128)(2,1)} %bitcast.107, bf16[1536,768]{1,0:T(8,128)(2,1)} %get-tuple-element.63.g_ref, bf16[1536,768]{1,0:T(8,128)(2,1)} %bitcast.7.u_ref, ...), custom_call_target="tpu_custom_call" | custom-call | flops 4831838208 | bytes 28311552 | tf_op jit(solution)/shard_map/expert_last/pallas_call | solution.py:441
  218.6 3.6 all-to-all-start.2
  224.2 14.9 %expert_weights.1 = bf16[4,2,768,384]{3,2,1,0:T(8,128)(2,1)} custom-call(bf16[768,1536]{1,0:T(8,128)(2,1)} %get-tuple-element.70.xt_ref, bf16[768,1536]{1,0:T(8,128)(2,1)} %get-tuple-element.71.gt_ref, bf16[1536,1024]{1,0:T(8,128)(2,1)} %get-tuple-element.72.active_one, bf16[1536,1024]{1,0:T(8,128)(2,1)} %get-tuple-element.73.pre_one, ...), custom_call_target="tpu_custom_call" | custom-call | flops 7247757312 | bytes 28311552 | tf_op jit(solution)/shard_map/expert_weights/pallas_call | solution.py:460
  239.2 12.5 %all-to-all-done.2 = bf16[8,192,768]{2,1,0:T(8,128)(2,1)S(1)} async-done(((bf16[8,192,768]{2,1,0:T(8,128)(2,1)}), bf16[8,192,768]{2,1,0:T(8,128)(2,1)S(1)}, u32[]{:S(2)}, u32[]{:S(2)}) %all-to-all-start.2) | async-done | bytes 2359328 | tf_op jit(solution)/shard_map/all_to_all | solution.py:593
  251.7 1.4 copy-done.12
  253.1 10.3 %combine_back.1 = (f32[1024,768]{1,0:T(8,128)}, bf16[1024,768]{1,0:T(8,128)(2,1)}, bf16[1024,768]{1,0:T(8,128)(2,1)}, f32[8,768]{1,0:T(8,128)}) custom-call(bf16[1536,768]{1,0:T(8,128)(2,1)} %bitcast.116, s32[1024,1]{1,0:T(8,128)} %add_select_fusion.target_ref, f32[1024,768]{1,0:T(8,128)} %copy-done.3, bf16[1024,768]{1,0:T(8,128)(2,1)} %bitcast.127, ...), custom_call_target="tpu_custom_call" | custom-call | flops 3623878656 | bytes 15728640 | tf_op jit(solution)/shard_map/combine_back/pallas_call | solution.py:512
  263.3 4.7 %all-to-all-start.3 = ((bf16[8,192,768]{2,1,0:T(8,128)(2,1)}), bf16[8,192,768]{2,1,0:T(8,128)(2,1)}, u32[]{:S(2)}, u32[]{:S(2)}) async-start(bf16[8,192,768]{2,1,0:T(8,128)(2,1)} %bitcast.113), calls=%async_computation.3 | async-start | bytes 4718592 | tf_op jit(solution)/shard_map/all_to_all | solution.py:593
  270.2 26.1 %attend_back.2 = (f32[768,1536]{1,0:T(8,128)}, f32[1024,768]{1,0:T(8,128)}) custom-call(s32[1]{0:T(128)} %copy.52.len_ref, bf16[1024,2304]{1,0:T(8,128)(2,1)} %convolution_convert_fusion.q_ref.k_ref.v_ref, bf16[1024,2304]{1,0:T(8,128)(2,1)} %convolution_convert_fusion.q_ref.k_ref.v_ref, bf16[1024,2304]{1,0:T(8,128)(2,1)} %convolution_convert_fusion.q_ref.k_ref.v_ref, ...), custom_call_target="tpu_custom_call" | custom-call | flops 8053063680 | bytes 5505024 | tf_op jit(solution)/shard_map/attend_back/pallas_call | solution.py:229
  296.3 1.8 dynamic-slice_convert_fusion.1
  298.3 30.1 %attend_back.3 = (f32[768,1536]{1,0:T(8,128)}, bf16[1,1024,768]{2,1,0:T(8,128)(2,1)}, f32[8,768]{1,0:T(8,128)}) custom-call(s32[1]{0:T(128)} %copy.52.len_ref, bf16[1024,2304]{1,0:T(8,128)(2,1)} %convolution_convert_fusion.q_ref.k_ref.v_ref, bf16[1024,2304]{1,0:T(8,128)(2,1)} %convolution_convert_fusion.q_ref.k_ref.v_ref, ...), custom_call_target="tpu_custom_call" | custom-call | flops 8053063680 | bytes 5505024 | tf_op jit(solution)/shard_map/attend_back/pallas_call | solution.py:229
  329.3 1.8 dynamic-slice_convert_fusion
  331.9 2.4 convert_add_fusion
  336.4 1.5 collective-permute-start.8
  337.9 11.6 %collective-permute-done.1 = bf16[192,1536]{1,0:T(8,128)(2,1)S(1)} collective-permute-done((bf16[192,1536]{1,0:T(8,128)(2,1)S(1)}, bf16[192,1536]{1,0:T(8,128)(2,1)S(1)}, u32[]{:S(2)}, u32[]{:S(2)}) %collective-permute-start.1) | collective-permute-done | bytes 589856 | tf_op jit(solution)/shard_map/ppermute | solution.py:607
  349.7 1.6 collective-permute-start.2
  351.2 2.2 collective-permute-done.8
  353.7 5.0 %collective-permute-done.2 = bf16[96,1536]{1,0:T(8,128)(2,1)S(1)} collective-permute-done((bf16[96,1536]{1,0:T(8,128)(2,1)S(1)}, bf16[96,1536]{1,0:T(8,128)(2,1)S(1)}, u32[]{:S(2)}, u32[]{:S(2)}) %collective-permute-start.2) | collective-permute-done | bytes 294944 | tf_op jit(solution)/shard_map/ppermute | solution.py:607
  358.8 2.2 collective-permute-done.9
  363.3 12.1 %collective-permute-done.10 = bf16[48,1664]{1,0:T(8,128)(2,1)S(1)} collective-permute-done((bf16[48,1664]{1,0:T(8,128)(2,1)S(1)}, bf16[48,1664]{1,0:T(8,128)(2,1)S(1)}, u32[]{:S(2)}, u32[]{:S(2)}) %collective-permute-start.10) | collective-permute-done | bytes 159776 | tf_op jit(solution)/shard_map/ppermute | solution.py:607
  375.6 14.4 %collective-permute-done.3 = bf16[48,1536]{1,0:T(8,128)(2,1)S(1)} collective-permute-done((bf16[48,1536]{1,0:T(8,128)(2,1)S(1)}, bf16[48,1536]{1,0:T(8,128)(2,1)S(1)}, u32[]{:S(2)}, u32[]{:S(2)}) %collective-permute-start.3) | collective-permute-done | bytes 147488 | tf_op jit(solution)/shard_map/ppermute | solution.py:607
  390.2 3.0 collective-permute-start.4
  393.1 3.5 collective-permute-done.12
  398.5 3.5 collective-permute-done.13
  404.9 1.6 convert_bitcast_fusion.1
  406.4 1.6 maximum_convert_fusion
  409.2 5.8 %fusion.21 = bf16[1,1024,768]{2,1,0:T(8,128)(2,1)} fusion(f32[1024,768]{1,0:T(8,128)S(1)} %copy-done.4, f32[1024]{0:T(1024)S(1)} %add_divide_fusion, bf16[1536,768]{1,0:T(8,128)(2,1)} %bitcast.25, s32[1024]{0:T(1024)S(1)} %add_select_fusion.1), kind=kOutput, calls=%fused_computation.33 | convolution fusion | flops 2419851264 | bytes 7086080 | tf_op jit(solution)/shard_map/dot_general | solution.py:19
  415.2 1.6 collective-permute-start.15
  416.9 3.4 collective-permute-done.6
  421.5 12.2 %collective-permute-done.17 = bf16[96,1536]{1,0:T(8,128)(2,1)S(1)} collective-permute-done((bf16[96,1536]{1,0:T(8,128)(2,1)S(1)}, bf16[96,1536]{1,0:T(8,128)(2,1)S(1)}, u32[]{:S(2)}, u32[]{:S(2)}) %collective-permute-start.17) | collective-permute-done | bytes 294944 | tf_op jit(solution)/shard_map/ppermute | solution.py:616
  433.8 1.5 collective-permute-start.18
  435.8 8.4 %collective-permute-done.18 = bf16[192,1536]{1,0:T(8,128)(2,1)S(1)} collective-permute-done((bf16[192,1536]{1,0:T(8,128)(2,1)S(1)}, bf16[192,1536]{1,0:T(8,128)(2,1)S(1)}, u32[]{:S(2)}, u32[]{:S(2)}) %collective-permute-start.18) | collective-permute-done | bytes 589856 | tf_op jit(solution)/shard_map/ppermute | solution.py:616
  444.6 3.4 copy.48
  449.7 1.5 slice_reduce_fusion
  451.2 7.4 %spread.1 = (f32[768,768]{1,0:T(8,128)}, f32[768,768]{1,0:T(8,128)}, f32[768,768]{1,0:T(8,128)}, f32[768,768]{1,0:T(8,128)}) custom-call(s32[1]{0:T(128)} %bitcast.36.flag_ref, bf16[384,1536]{1,0:T(8,128)(2,1)} %copy-done.6, bf16[384,1536]{1,0:T(8,128)(2,1)} %collective-permute-done.19.refs_1_.refs_3_, bf16[384,1536]{1,0:T(8,128)(2,1)} %copy-done.6, ...), custom_call_target="tpu_custom_call" | custom-call | tf_op jit(solution)/shard_map/spread/pallas_call | solution.py:566
  (169 shorter events, 33.4 us)
Async XLA Ops:
  7.2 1.8 slice-start.2
  7.2 95.3 %all-gather.7.cloned.1.call-start = ((), (), s32[]{:S(2)}) async-start(), calls=%async_computation.8 | async-start | bytes 5898240 | tf_op jit(solution)/shard_map/all_gather | solution.py:668
  8.9 16.7 %copy-start.11 = (bf16[1,768,768]{1,2,0:T(8,128)(2,1)}, bf16[1,768,768]{1,2,0:T(8,128)(2,1)S(1)}, u32[]{:S(2)}) copy-start(bf16[1,768,768]{1,2,0:T(8,128)(2,1)S(1)} %copy.43) | copy-start | bytes 3538948
  8.9 2.0 copy-start.16
  19.9 5.7 %slice-start.3 = ((bf16[1,768,768]{2,1,0:T(8,128)(2,1)}), bf16[1,256,768]{2,1,0:T(8,128)(2,1)S(1)}, s32[]{:S(2)}) async-start(bf16[1,768,768]{2,1,0:T(8,128)(2,1)} %param.28), calls=%async_computation.14 | async-start | bytes 786432 | tf_op jit(solution)/shard_map/slice | solution.py:665
  19.9 38.4 %all-to-all-start = ((bf16[8,192,768]{2,1,0:T(8,128)(2,1)}), bf16[8,192,768]{2,1,0:T(8,128)(2,1)}, u32[]{:S(2)}, u32[]{:S(2)}) async-start(bf16[8,192,768]{2,1,0:T(8,128)(2,1)} %bitcast.117), calls=%async_computation | async-start | bytes 4718592 | tf_op jit(solution)/shard_map/all_to_all | solution.py:593
  25.2 141.4 %all-gather.9.cloned.1.call-start = ((), (), s32[]{:S(2)}) async-start(), calls=%async_computation.9 | async-start | bytes 3932160 | tf_op jit(solution)/shard_map/all_gather | solution.py:668
  26.9 2.4 copy-start.13
  26.9 2.4 copy-start.14
  26.9 2.4 copy-start.15
  58.3 3.4 copy-start
  61.7 1.7 copy-start.3
  63.4 4.8 %copy-start.8 = (bf16[1024,768]{1,0:T(8,128)(2,1)}, bf16[1024,768]{1,0:T(8,128)(2,1)S(1)}, u32[]{:S(2)}) copy-start(bf16[1024,768]{1,0:T(8,128)(2,1)S(1)} %add_convert_fusion.1) | copy-start | bytes 4718596
  68.1 5.5 %slice-start.4 = ((bf16[1,768,768]{2,1,0:T(8,128)(2,1)}), bf16[1,128,768]{2,1,0:T(8,128)(2,1)S(1)}, s32[]{:S(2)}) async-start(bf16[1,768,768]{2,1,0:T(8,128)(2,1)} %param.28), calls=%async_computation.15 | async-start | bytes 393216 | tf_op jit(solution)/shard_map/slice | solution.py:665
  68.1 6.9 %copy-start.17 = (bf16[768,8]{0,1:T(8,128)(2,1)S(1)}, bf16[768,8]{0,1:T(8,128)(2,1)}, u32[]{:S(2)}) copy-start(bf16[768,8]{0,1:T(8,128)(2,1)} %param.26) | copy-start | bytes 36868
  68.1 34.0 %all-to-all-start.1 = ((bf16[8,192,768]{2,1,0:T(8,128)(2,1)}), bf16[8,192,768]{2,1,0:T(8,128)(2,1)S(1)}, u32[]{:S(2)}, u32[]{:S(2)}) async-start(bf16[8,192,768]{2,1,0:T(8,128)(2,1)} %bitcast.114), calls=%async_computation.1 | async-start | bytes 4718592 | tf_op jit(solution)/shard_map/all_to_all | solution.py:593
  72.6 131.9 %all-gather.11.cloned.1.call-start = ((), (), s32[]{:S(2)}) async-start(), calls=%async_computation.10 | async-start | bytes 1966080 | tf_op jit(solution)/shard_map/all_gather | solution.py:668
  74.5 327.6 %reduce-scatter.3.cloned.1.call-start = ((), (), s32[]{:S(2)}) async-start(), calls=%async_computation.6 | async-start | bytes 5898240 | tf_op jit(solution)/shard_map/reduce_scatter | solution.py:740
  218.6 33.0 %all-to-all-start.2 = ((bf16[8,192,768]{2,1,0:T(8,128)(2,1)}), bf16[8,192,768]{2,1,0:T(8,128)(2,1)S(1)}, u32[]{:S(2)}, u32[]{:S(2)}) async-start(bf16[8,192,768]{2,1,0:T(8,128)(2,1)} %bitcast.115), calls=%async_computation.2 | async-start | bytes 4718592 | tf_op jit(solution)/shard_map/all_to_all | solution.py:593
  263.3 5.5 %copy-start.9 = (bf16[1024,768]{1,0:T(8,128)(2,1)S(1)}, bf16[1024,768]{1,0:T(8,128)(2,1)}, u32[]{:S(2)}) copy-start(bf16[1024,768]{1,0:T(8,128)(2,1)} %copy-done.8) | copy-start | bytes 4718596
  263.3 6.0 %copy-start.22 = (f32[1,768]{1,0:T(1,128)S(1)}, f32[1,768]{1,0:T(1,128)}, u32[]{:S(2)}) copy-start(f32[1,768]{1,0:T(1,128)} %get-tuple-element.90) | copy-start | bytes 9220
  263.3 34.9 %all-to-all-start.3 = ((bf16[8,192,768]{2,1,0:T(8,128)(2,1)}), bf16[8,192,768]{2,1,0:T(8,128)(2,1)}, u32[]{:S(2)}, u32[]{:S(2)}) async-start(bf16[8,192,768]{2,1,0:T(8,128)(2,1)} %bitcast.113), calls=%async_computation.3 | async-start | bytes 4718592 | tf_op jit(solution)/shard_map/all_to_all | solution.py:593
  268.0 135.4 %reduce-scatter.5.cloned.1.call-start = ((), (), s32[]{:S(2)}) async-start(), calls=%async_computation.7 | async-start | bytes 5898240 | tf_op jit(solution)/shard_map/reduce_scatter | solution.py:741
  298.1 33.8 %collective-permute-start = (bf16[384,1536]{1,0:T(8,128)(2,1)S(1)}, bf16[384,1536]{1,0:T(8,128)(2,1)S(1)}, u32[]{:S(2)}, u32[]{:S(2)}) collective-permute-start(bf16[384,1536]{1,0:T(8,128)(2,1)S(1)} %dynamic-slice_convert_fusion.1), channel_id=1, source_target_pairs={{0,4},{4,0},{8,12},{12,8},{16,20},{20,16},{24,28},{28,24},{1,5},{5... | collective-permute-start | bytes 3538952 | tf_op jit(solution)/shard_map/ppermute | solution.py:607
  331.1 4.6 slice-start
  331.3 4.7 %collective-permute-start.7 = (bf16[384,1664]{1,0:T(8,128)(2,1)S(1)}, bf16[384,1664]{1,0:T(8,128)(2,1)S(1)}, u32[]{:S(2)}, u32[]{:S(2)}) collective-permute-start(bf16[384,1664]{1,0:T(8,128)(2,1)S(1)} %pad_maximum_fusion), channel_id=1, source_target_pairs={{0,4},{4,0},{8,12},{12,8},{16,20},{20,16},{24,28},{28,24},{1,5},{5... | collective-permute-start | bytes 3833864 | tf_op jit(solution)/shard_map/ppermute | solution.py:607
  331.9 3.9 slice-start.1
  334.4 15.1 %collective-permute-start.1 = (bf16[192,1536]{1,0:T(8,128)(2,1)S(1)}, bf16[192,1536]{1,0:T(8,128)(2,1)S(1)}, u32[]{:S(2)}, u32[]{:S(2)}) collective-permute-start(bf16[192,1536]{1,0:T(8,128)(2,1)S(1)} %dynamic-slice_convert_fusion.3), channel_id=1, source_target_pairs={{0,8},{4,12},{8,0},{12,4},{16,24},{20,28},{24,16},{28,20},{1,9},{5... | collective-permute-start | bytes 1769480 | tf_op jit(solution)/shard_map/ppermute | solution.py:607
  336.4 17.1 %collective-permute-start.8 = (bf16[192,1664]{1,0:T(8,128)(2,1)S(1)}, bf16[192,1664]{1,0:T(8,128)(2,1)S(1)}, u32[]{:S(2)}, u32[]{:S(2)}) collective-permute-start(bf16[192,1664]{1,0:T(8,128)(2,1)S(1)} %dynamic-slice_convert_fusion.2), channel_id=1, source_target_pairs={{0,16},{4,20},{8,24},{12,28},{16,0},{20,4},{24,8},{28,12},{1,17},{... | collective-permute-start | bytes 1916936 | tf_op jit(solution)/shard_map/ppermute | solution.py:607
  349.7 9.1 %collective-permute-start.2 = (bf16[96,1536]{1,0:T(8,128)(2,1)S(1)}, bf16[96,1536]{1,0:T(8,128)(2,1)S(1)}, u32[]{:S(2)}, u32[]{:S(2)}) collective-permute-start(bf16[96,1536]{1,0:T(8,128)(2,1)S(1)} %dynamic-slice_convert_fusion.5), channel_id=1, source_target_pairs={{0,16},{4,20},{8,24},{12,28},{16,0},{20,4},{24,8},{28,12},{1,17},{... | collective-permute-start | bytes 884744 | tf_op jit(solution)/shard_map/ppermute | solution.py:607
  353.6 7.4 %collective-permute-start.9 = (bf16[96,1664]{1,0:T(8,128)(2,1)S(1)}, bf16[96,1664]{1,0:T(8,128)(2,1)S(1)}, u32[]{:S(2)}, u32[]{:S(2)}) collective-permute-start(bf16[96,1664]{1,0:T(8,128)(2,1)S(1)} %dynamic-slice_convert_fusion.4), channel_id=1, source_target_pairs={{0,8},{4,12},{8,0},{12,4},{16,24},{20,28},{24,16},{28,20},{1,9},{5... | collective-permute-start | bytes 958472 | tf_op jit(solution)/shard_map/ppermute | solution.py:607
  361.2 14.3 %collective-permute-start.10 = (bf16[48,1664]{1,0:T(8,128)(2,1)S(1)}, bf16[48,1664]{1,0:T(8,128)(2,1)S(1)}, u32[]{:S(2)}, u32[]{:S(2)}) collective-permute-start(bf16[48,1664]{1,0:T(8,128)(2,1)S(1)} %dynamic-slice_convert_fusion.6), channel_id=1, source_target_pairs={{0,1},{1,0},{2,3},{3,2},{4,5},{5,4},{6,7},{7,6},{8,9},{9,8},{10,11... | collective-permute-start | bytes 479240 | tf_op jit(solution)/shard_map/ppermute | solution.py:607
  362.2 27.7 %collective-permute-start.3 = (bf16[48,1536]{1,0:T(8,128)(2,1)S(1)}, bf16[48,1536]{1,0:T(8,128)(2,1)S(1)}, u32[]{:S(2)}, u32[]{:S(2)}) collective-permute-start(bf16[48,1536]{1,0:T(8,128)(2,1)S(1)} %dynamic-slice_convert_fusion.7), channel_id=1, source_target_pairs={{0,1},{1,0},{2,3},{3,2},{4,5},{5,4},{6,7},{7,6},{8,9},{9,8},{10,11... | collective-permute-start | bytes 442376 | tf_op jit(solution)/shard_map/ppermute | solution.py:607
  375.5 14.5 %collective-permute-start.11 = (bf16[24,1664]{1,0:T(8,128)(2,1)S(1)}, bf16[24,1664]{1,0:T(8,128)(2,1)S(1)}, u32[]{:S(2)}, u32[]{:S(2)}) collective-permute-start(bf16[24,1664]{1,0:T(8,128)(2,1)S(1)} %dynamic-slice_convert_fusion.8), channel_id=1, source_target_pairs={{0,2},{1,3},{2,0},{3,1},{4,6},{5,7},{6,4},{7,5},{8,10},{9,11},{10,... | collective-permute-start | bytes 239624 | tf_op jit(solution)/shard_map/ppermute | solution.py:607
  390.1 6.6 %collective-permute-start.12 = (bf16[24,1664]{1,0:T(8,128)(2,1)S(1)}, bf16[24,1664]{1,0:T(8,128)(2,1)S(1)}, u32[]{:S(2)}, u32[]{:S(2)}) collective-permute-start(bf16[24,1664]{1,0:T(8,128)(2,1)S(1)} %add_convert_fusion.2), channel_id=1, source_target_pairs={{0,2},{1,3},{2,0},{3,1},{4,6},{5,7},{6,4},{7,5},{8,10},{9,11},{10,... | collective-permute-start | bytes 239624 | tf_op jit(solution)/shard_map/ppermute | solution.py:616
  390.2 7.7 %collective-permute-start.4 = (bf16[24,1536]{1,0:T(8,128)(2,1)S(1)}, bf16[24,1536]{1,0:T(8,128)(2,1)S(1)}, u32[]{:S(2)}, u32[]{:S(2)}) collective-permute-start(bf16[24,1536]{1,0:T(8,128)(2,1)S(1)} %dynamic-slice_convert_fusion.9), channel_id=1, source_target_pairs={{0,2},{1,3},{2,0},{3,1},{4,6},{5,7},{6,4},{7,5},{8,10},{9,11},{10,... | collective-permute-start | bytes 221192 | tf_op jit(solution)/shard_map/ppermute | solution.py:607
  396.7 5.3 %collective-permute-start.13 = (bf16[48,1664]{1,0:T(8,128)(2,1)S(1)}, bf16[48,1664]{1,0:T(8,128)(2,1)S(1)}, u32[]{:S(2)}, u32[]{:S(2)}) collective-permute-start(bf16[48,1664]{1,0:T(8,128)(2,1)S(1)} %maximum_select_fusion.7), channel_id=1, source_target_pairs={{0,1},{1,0},{2,3},{3,2},{4,5},{5,4},{6,7},{7,6},{8,9},{9,8},{10,11... | collective-permute-start | bytes 479240 | tf_op jit(solution)/shard_map/ppermute | solution.py:616
  397.9 17.0 %collective-permute-start.5 = (bf16[24,1536]{1,0:T(8,128)(2,1)S(1)}, bf16[24,1536]{1,0:T(8,128)(2,1)S(1)}, u32[]{:S(2)}, u32[]{:S(2)}) collective-permute-start(bf16[24,1536]{1,0:T(8,128)(2,1)S(1)} %add_convert_fusion.3), channel_id=1, source_target_pairs={{0,2},{1,3},{2,0},{3,1},{4,6},{5,7},{6,4},{7,5},{8,10},{9,11},{10,... | collective-permute-start | bytes 221192 | tf_op jit(solution)/shard_map/ppermute | solution.py:616
  406.4 2.7 copy-start.4
  408.0 7.1 %collective-permute-start.14 = (bf16[96,1664]{1,0:T(8,128)(2,1)S(1)}, bf16[96,1664]{1,0:T(8,128)(2,1)S(1)}, u32[]{:S(2)}, u32[]{:S(2)}) collective-permute-start(bf16[96,1664]{1,0:T(8,128)(2,1)S(1)} %maximum_select_fusion.5), channel_id=1, source_target_pairs={{0,8},{4,12},{8,0},{12,4},{16,24},{20,28},{24,16},{28,20},{1,9},{5... | collective-permute-start | bytes 958472 | tf_op jit(solution)/shard_map/ppermute | solution.py:616
  415.0 5.2 %collective-permute-start.6 = (bf16[48,1536]{1,0:T(8,128)(2,1)S(1)}, bf16[48,1536]{1,0:T(8,128)(2,1)S(1)}, u32[]{:S(2)}, u32[]{:S(2)}) collective-permute-start(bf16[48,1536]{1,0:T(8,128)(2,1)S(1)} %maximum_select_fusion.8), channel_id=1, source_target_pairs={{0,1},{1,0},{2,3},{3,2},{4,5},{5,4},{6,7},{7,6},{8,9},{9,8},{10,11... | collective-permute-start | bytes 442376 | tf_op jit(solution)/shard_map/ppermute | solution.py:616
  415.2 20.1 %collective-permute-start.15 = (bf16[192,1664]{1,0:T(8,128)(2,1)S(1)}, bf16[192,1664]{1,0:T(8,128)(2,1)S(1)}, u32[]{:S(2)}, u32[]{:S(2)}) collective-permute-start(bf16[192,1664]{1,0:T(8,128)(2,1)S(1)} %maximum_select_fusion.2), channel_id=1, source_target_pairs={{0,16},{4,20},{8,24},{12,28},{16,0},{20,4},{24,8},{28,12},{1,17},{... | collective-permute-start | bytes 1916936 | tf_op jit(solution)/shard_map/ppermute | solution.py:616
  420.3 13.4 %collective-permute-start.17 = (bf16[96,1536]{1,0:T(8,128)(2,1)S(1)}, bf16[96,1536]{1,0:T(8,128)(2,1)S(1)}, u32[]{:S(2)}, u32[]{:S(2)}) collective-permute-start(bf16[96,1536]{1,0:T(8,128)(2,1)S(1)} %maximum_select_fusion.6), channel_id=1, source_target_pairs={{0,16},{4,20},{8,24},{12,28},{16,0},{20,4},{24,8},{28,12},{1,17},{... | collective-permute-start | bytes 884744 | tf_op jit(solution)/shard_map/ppermute | solution.py:616
  433.8 10.4 %collective-permute-start.18 = (bf16[192,1536]{1,0:T(8,128)(2,1)S(1)}, bf16[192,1536]{1,0:T(8,128)(2,1)S(1)}, u32[]{:S(2)}, u32[]{:S(2)}) collective-permute-start(bf16[192,1536]{1,0:T(8,128)(2,1)S(1)} %maximum_select_fusion.3), channel_id=1, source_target_pairs={{0,8},{4,12},{8,0},{12,4},{16,24},{20,28},{24,16},{28,20},{1,9},{5... | collective-permute-start | bytes 1769480 | tf_op jit(solution)/shard_map/ppermute | solution.py:616
  435.7 12.3 %copy-start.5 = (bf16[384,1664]{1,0:T(8,128)(2,1)}, bf16[384,1664]{1,0:T(8,128)(2,1)S(1)}, u32[]{:S(2)}) copy-start(bf16[384,1664]{1,0:T(8,128)(2,1)S(1)} %maximum_select_fusion.refs_4_.refs_6_) | copy-start | bytes 3833860
  435.7 12.3 %collective-permute-start.16 = (bf16[384,1664]{1,0:T(8,128)(2,1)S(1)}, bf16[384,1664]{1,0:T(8,128)(2,1)}, u32[]{:S(2)}, u32[]{:S(2)}) collective-permute-start(bf16[384,1664]{1,0:T(8,128)(2,1)S(1)} %maximum_select_fusion.refs_4_.refs_6_), channel_id=1, source_target_pairs={{0,4},{4,0},{8,12},{12,8},{16,20},{20,16},{24,28},{28,24},{1,5},{5... | collective-permute-start | bytes 3833864 | tf_op jit(solution)/shard_map/ppermute | solution.py:616
  444.5 3.5 copy-start.6
  444.5 6.7 %collective-permute-start.19 = (bf16[384,1536]{1,0:T(8,128)(2,1)S(1)}, bf16[384,1536]{1,0:T(8,128)(2,1)}, u32[]{:S(2)}, u32[]{:S(2)}) collective-permute-start(bf16[384,1536]{1,0:T(8,128)(2,1)S(1)} %maximum_select_fusion.1.refs_0_.refs_2_), channel_id=1, source_target_pairs={{0,4},{4,0},{8,12},{12,8},{16,20},{20,16},{24,28},{28,24},{1,5},{5... | collective-permute-start | bytes 3538952 | tf_op jit(solution)/shard_map/ppermute | solution.py:616
  (9 other events, 9.5 us)
Sparse Core Ops, SparseCore 0:
  10.3 92.0 all-gather.6
  104.6 61.9 all-gather.8
  168.8 35.7 all-gather.10
  206.7 84.1 reduce-scatter.2
  298.4 94.5 reduce-scatter.4

commit v2 on v1

v2 whole, which is shorter than its diff:
```python
import functools
import jax
import jax.numpy as jnp
from jax import lax
from jax.experimental import pallas as pl
from jax.experimental.pallas import tpu as pltpu
from jax.sharding import PartitionSpec as P

F32 = jnp.float32
BF16 = jnp.bfloat16
HEADS = 12
EPSILON = 1e-05
MASKED_SCORE = -1000000000.0
PAIR = 128
QTILE = 256


def dot(left, right):
    return jnp.dot(left, right, preferred_element_type=F32)


def dot_tn(left, right):
    return lax.dot_general(left, right, (((0,), (0,)), ((), ())), preferred_element_type=F32)


def dot_nt(left, right):
    return lax.dot_general(left, right, (((1,), (1,)), ((), ())), preferred_element_type=F32)


def lanes_of(head, shape):
    lane = lax.broadcasted_iota(jnp.int32, shape, 1)
    return (lane >= head * (PAIR // 2)) & (lane < (head + 1) * (PAIR // 2))


def packed_rows(length, tile):
    return [sum(range(1, at + 1)) * tile for at in range(length // tile + 1)]


def attend_kernel(scale, len_ref, q_ref, k_ref, v_ref, mixed_ref, probs_ref):
    length = q_ref.shape[0]
    tile = min(QTILE, length)
    seq_len = len_ref[0]
    starts = packed_rows(length, tile)
    for at in range(length // tile):
        start, finish = at * tile, (at + 1) * tile
        query = q_ref[start:finish, :] * scale
        keys = k_ref[:finish, :]
        values = v_ref[:finish, :]
        key_pos = lax.broadcasted_iota(jnp.int32, (finish, 1), 0)
        bias = jnp.where(key_pos < seq_len, 0.0, MASKED_SCORE)
        row = lax.broadcasted_iota(jnp.int32, (tile, tile), 0)
        col = lax.broadcasted_iota(jnp.int32, (tile, tile), 1)
        mixed = None
        for head in range(2):
            zero = jnp.zeros((), BF16)
            q_head = jnp.where(lanes_of(head, query.shape), query, zero)
            scores = dot_nt(keys, q_head) + bias
            diagonal = jnp.where(row <= col, scores[start:], MASKED_SCORE)
            scores = diagonal if start == 0 else jnp.concatenate([scores[:start], diagonal], 0)
            expo = jnp.exp(scores - jnp.max(scores, 0, keepdims=True))
            probs = (expo * (1.0 / jnp.sum(expo, 0, keepdims=True))).astype(BF16)
            probs_ref[0, head, starts[at] : starts[at + 1], :] = probs
            v_head = jnp.where(lanes_of(head, values.shape), values, zero)
            part = dot_tn(probs, v_head)
            mixed = part if mixed is None else mixed + part
        mixed_ref[start:finish, :] = mixed.astype(BF16)


def attend(projected, seq_lengths, scale):
    length, width3 = projected.shape
    width = width3 // 3
    pairs = width // PAIR
    tile = min(QTILE, length)
    rows = packed_rows(length, tile)[-1]
    return pl.pallas_call(
        functools.partial(attend_kernel, scale),
        grid_spec=pltpu.PrefetchScalarGridSpec(
            num_scalar_prefetch=1,
            grid=(pairs,),
            in_specs=[
                pl.BlockSpec((length, PAIR), lambda i, s: (0, i)),
                pl.BlockSpec((length, PAIR), lambda i, s: (0, pairs + i)),
                pl.BlockSpec((length, PAIR), lambda i, s: (0, 2 * pairs + i)),
            ],
            out_specs=[
                pl.BlockSpec((length, PAIR), lambda i, s: (0, i)),
                pl.BlockSpec((1, 2, rows, tile), lambda i, s: (i, 0, 0, 0)),
            ],
        ),
        out_shape=[
            jax.ShapeDtypeStruct((length, width), BF16),
            jax.ShapeDtypeStruct((pairs, 2, rows, tile), BF16),
        ],
        compiler_params=pltpu.CompilerParams(vmem_limit_bytes=48 * 1024 * 1024),
        cost_estimate=pl.CostEstimate(
            flops=4 * length * length * width, bytes_accessed=8 * length * width, transcendentals=0
        ),
        name="attend",
    )(seq_lengths, projected, projected, projected)


def attend_back_kernel(
    scale, counts, part, flag_ref, q_ref, k_ref, v_ref, g_ref, probs_ref, normed_t, *refs
):
    parts = len(counts)
    count = counts[part]
    last = part == parts - 1
    if part == 0:
        mixed_t, attn_ref, mine_ref, theirs_ref, grads = refs
    elif last:
        befores, refs = refs[: parts - 1], refs[parts - 1 :]
        qkv, (in_ref, gain_ref, resid_ref, cent_ref, sums_ref) = refs[:3], refs[3:8]
        mine_ref, theirs_ref, out_ref, grads, sums_scratch = refs[10:]
    else:
        mine_ref, theirs_ref, grads = refs
    length = q_ref.shape[0]
    tile = min(QTILE, length)
    starts = packed_rows(length, tile)
    step = pl.program_id(0)
    half = mine_ref.shape[0]
    columns = 3 * PAIR

    def give(product):
        low, high = product[:half], product[half:]
        mine_ref[...] = jnp.where(flag_ref[0] == 0, low, high)
        theirs_ref[...] = jnp.where(flag_ref[0] == 0, high, low).astype(BF16)

    def pair():
        dk_sum = [None] * (length // tile)
        dv_sum = [None] * (length // tile)
        dq = []
        for at in range(length // tile):
            start, finish = at * tile, (at + 1) * tile
            query = q_ref[start:finish, :] * scale
            grad = g_ref[start:finish, :]
            keys = k_ref[:finish, :]
            values = v_ref[:finish, :]
            grad_query = None
            for head in range(2):
                zero = jnp.zeros((), BF16)
                q_head = jnp.where(lanes_of(head, query.shape), query, zero)
                g_head = jnp.where(lanes_of(head, query.shape), grad, zero)
                k_head = jnp.where(lanes_of(head, keys.shape), keys, zero)
                low = probs_ref[0, head, starts[at] : starts[at + 1], :]
                probs = low.astype(F32)
                product = probs * dot_nt(values, g_head)
                centre = jnp.sum(product, 0, keepdims=True)
                grad_scores = (product - probs * centre).astype(BF16)
                dv = dot(low, g_head)
                dk = dot(grad_scores, q_head)
                for j in range(at + 1):
                    here = slice(j * tile, (j + 1) * tile)
                    dk_sum[j] = dk[here] if dk_sum[j] is None else dk_sum[j] + dk[here]
                    dv_sum[j] = dv[here] if dv_sum[j] is None else dv_sum[j] + dv[here]
                share = dot_tn(grad_scores, k_head)
                grad_query = share if grad_query is None else grad_query + share
            dq.append((grad_query * scale).astype(BF16))
        sides = [dq, [x.astype(BF16) for x in dk_sum], [x.astype(BF16) for x in dv_sum]]
        return jnp.concatenate([jnp.concatenate(side, 0) for side in sides], 1)

    @pl.when(step < count)
    def _():
        found = pair()
        for k in range(3):
            cols = pl.ds(pl.multiple_of(step * PAIR, PAIR), PAIR) if last else slice(None)
            grads[k, :, cols] = found[:, k * PAIR : (k + 1) * PAIR]
        give(dot(normed_t[...], found))

    if part == 0:

        @pl.when(step >= count)
        def _():
            give(dot(mixed_t[...], attn_ref[...]))

    if last:

        @pl.when(step == count)
        def _():
            sums_scratch[...] = jnp.zeros_like(sums_scratch)

        @pl.when(step >= count)
        def _():
            here = pl.ds(pl.multiple_of((step - count) * tile, tile), tile)
            grad = None
            for j in range(parts):
                before = sum(counts[:j])
                cols = slice(before * PAIR, (before + counts[j]) * PAIR)
                for k, weight in enumerate(qkv):
                    side = grads[k, here, :] if j == parts - 1 else befores[j][k]
                    share = dot_nt(side, weight[:, cols])
                    grad = share if grad is None else grad + share
            standard, back_norm = norm_back(in_ref[0].astype(F32), gain_ref[...], grad)
            out_ref[0] = (resid_ref[...] + back_norm).astype(BF16)
            sums_scratch[0:1, :] += jnp.sum(grad * standard, 0, keepdims=True)
            sums_scratch[1:2, :] += jnp.sum(grad, 0, keepdims=True)

        @pl.when(step == count + length // tile - 1)
        def _():
            sums = cent_ref[...]
            rows, width = sums.shape
            place = lax.broadcasted_iota(jnp.int32, (rows, 1), 0)
            for row, ref, k in (
                (rows - 4, sums_ref, 0), (rows - 3, sums_ref, 1),
                (rows - 2, sums_scratch, 0), (rows - 1, sums_scratch, 1),
            ):
                sums = jnp.where(place == row, ref[k : k + 1, :], sums)
            turned = jnp.concatenate([sums, jnp.zeros((PAIR - rows, width), F32)], 0).T
            low, high = turned[:half], turned[half:]
            mine_ref[:, :PAIR] = jnp.where(flag_ref[0] == 0, low, high)
            theirs_ref[:, :PAIR] = jnp.where(flag_ref[0] == 0, high, low).astype(BF16)


def attend_back(flag, projected, grad_mixed, probs, scale, counts, part, normed_t, *more):
    width, length = normed_t.shape
    pairs = width // PAIR
    count = counts[part]
    first = sum(counts[:part])
    last = part == len(counts) - 1
    block = (length, PAIR)
    columns = 3 * PAIR
    extra = width // columns if part == 0 else 0

    def at(i):
        return first + jnp.minimum(i, count - 1)

    own = (count + extra) * columns
    held = own if part == 0 else sum(counts[1:]) * columns + PAIR
    offset = sum(counts[1:part])
    steps = count + (1 if last else extra)
    half_spec = pl.BlockSpec(
        (width // 2, columns), lambda i, s: (0, offset + jnp.minimum(i, steps - 1))
    )
    half_shape = (width // 2, held)
    in_specs = [
        pl.BlockSpec(block, lambda i, s: (0, at(i))),
        pl.BlockSpec(block, lambda i, s: (0, pairs + at(i))),
        pl.BlockSpec(block, lambda i, s: (0, 2 * pairs + at(i))),
        pl.BlockSpec(block, lambda i, s: (0, at(i))),
        pl.BlockSpec((1, *probs.shape[1:]), lambda i, s: (at(i), 0, 0, 0)),
        whole(normed_t.shape),
    ]
    out_specs = [half_spec, half_spec]
    out_shape = [jax.ShapeDtypeStruct(half_shape, F32), jax.ShapeDtypeStruct(half_shape, BF16)]
    scratch = []
    aliases = {}
    if last:
        tile = min(QTILE, length)

        def row(i):
            return jnp.maximum(i - count, 0)

        in_specs += [
            pl.BlockSpec((3, tile, c * PAIR), lambda i, s: (0, row(i), 0)) for c in counts[:-1]
        ]
        in_specs += [whole((width, width))] * 3
        in_specs += [
            pl.BlockSpec((1, tile, width), lambda i, s: (0, row(i), 0)), whole((1, width)),
            pl.BlockSpec((tile, width), lambda i, s: (row(i), 0)), whole(more[-4].shape),
            whole(more[-3].shape),
        ]
        in_specs += [pl.BlockSpec(memory_space=pl.ANY)] * 2
        aliases = {5 + len(more): 0, 6 + len(more): 1}
        extra = length // tile
        out_specs += [pl.BlockSpec((1, tile, width), lambda i, s: (0, row(i), 0))]
        out_shape += [jax.ShapeDtypeStruct((1, length, width), BF16)]
        scratch += [pltpu.VMEM((3, length, count * PAIR), BF16), pltpu.VMEM((8, width), F32)]
    else:
        if part == 0:
            in_specs += [
                whole((width, length)),
                pl.BlockSpec((length, columns), lambda i, s: (0, jnp.maximum(i - count, 0))),
            ]
        out_specs += [
            pl.BlockSpec((3, length, PAIR), lambda i, s: (0, 0, jnp.minimum(i, count - 1)))
        ]
        out_shape += [jax.ShapeDtypeStruct((3, length, count * PAIR), BF16)]
    return pl.pallas_call(
        functools.partial(attend_back_kernel, scale, counts, part),
        grid_spec=pltpu.PrefetchScalarGridSpec(
            num_scalar_prefetch=1,
            grid=(count + extra,),
            in_specs=in_specs,
            out_specs=out_specs,
            scratch_shapes=scratch,
        ),
        out_shape=out_shape,
        input_output_aliases=aliases,
        compiler_params=pltpu.CompilerParams(vmem_limit_bytes=58 * 1024 * 1024),
        cost_estimate=pl.CostEstimate(
            flops=20 * length * length * count * PAIR,
            bytes_accessed=14 * length * count * PAIR,
            transcendentals=0,
        ),
        name="attend_back",
    )(flag, projected, projected, projected, grad_mixed, probs, normed_t, *more)


ERFC = (0.254829592, -0.284496736, 1.421413741, -1.453152027, 1.061405429)
ERFC_RATE = 0.3275911 * 0.5**0.5
ROWS = 256


def gelu_pair(value):
    size = jnp.abs(value)
    t = 1.0 / (1.0 + ERFC_RATE * size)
    poly = t * (
        ERFC[0] + t * (ERFC[1] + t * (ERFC[2] + t * (ERFC[3] + t * ERFC[4])))
    )
    bell = jnp.exp(-0.5 * value * value)
    tail = 0.5 * poly * bell
    below = jnp.where(value < 0, tail, 1.0 - tail)
    return value * below, below + value * (bell * 0.3989422804014327)


def join_pieces(w_ref, w_all):
    pieces, unused, hidden, unused_width = w_ref.shape
    for p in range(pieces):
        for k in range(2):
            w_all[k, p * hidden : (p + 1) * hidden, :] = w_ref[p, k]


def expert_tile(x, g, w_all, active_ref, pre_ref, at):
    units = w_all.shape[1]
    chunk = units if units <= 512 else 512 if units % 512 == 0 else 384
    for start in range(0, units, chunk):
        cols = slice(start, start + chunk)
        active, slope = gelu_pair(dot_nt(x, w_all[0, cols, :]))
        active_ref[at, cols] = active.astype(BF16)
        pre_ref[at, cols] = (dot_nt(g, w_all[1, cols, :]) * slope).astype(BF16)
    return dot(active_ref[at, :], w_all[1]), dot(pre_ref[at, :], w_all[0])


def expert_first_kernel(
    tiles, x_ref, u_ref, cent_ref, w_ref, out_ref, in_ref, dw_ref, g_ref, xt_ref, gt_ref, gate_ref,
    active, grad_pre, w_all,
):
    rows = x_ref.shape[0]
    step = pl.program_id(0)

    @pl.when(step == 0)
    def _():
        join_pieces(w_ref, w_all)

    @pl.when(step < tiles)
    def _():
        at = pl.ds(pl.multiple_of(step * rows, rows), rows)
        x = x_ref[...]
        chosen = jnp.sum(x.astype(F32) * cent_ref[...], 1, keepdims=True)
        gate = 1.0 / (1.0 + jnp.exp(-chosen))
        gate_ref[...] = gate
        g = (gate * u_ref[...].astype(F32)).astype(BF16)
        g_ref[...] = g
        xt_ref[:, at] = x.T
        gt_ref[:, at] = g.T
        out_ref[...], in_ref[...] = expert_tile(x, g, w_all, active, grad_pre, at)

    @pl.when(step >= tiles)
    def _():
        hidden = dw_ref.shape[3]
        cols = pl.ds(pl.multiple_of((step - tiles) * hidden, hidden), hidden)
        dw_ref[0, 0] = dot(xt_ref[...], grad_pre[:, cols]).astype(BF16)
        dw_ref[0, 1] = dot(gt_ref[...], active[:, cols]).astype(BF16)


def expert_last_kernel(
    x_ref, g_ref, u_ref, gate_ref, cent_ref, out_in, in_in, w_ref,
    low_ref, back_ref, cent_grad_ref, active_ref, pre_ref, w_all,
):
    @pl.when(pl.program_id(0) == 0)
    def _():
        join_pieces(w_ref, w_all)
        cent_grad_ref[...] = jnp.zeros_like(cent_grad_ref)

    x = x_ref[...]
    out, grad_in = expert_tile(x, g_ref[...], w_all, active_ref, pre_ref, slice(None))
    low = (out_in[...] + out).astype(BF16)
    low_ref[...] = low
    gate = gate_ref[...]
    chosen = jnp.sum(u_ref[...].astype(F32) * low.astype(F32), 1, keepdims=True)
    chosen = chosen * gate * (1.0 - gate)
    back_ref[...] = (in_in[...] + grad_in + chosen * cent_ref[...]).astype(BF16)
    cent_grad_ref[...] += jnp.sum(chosen * x.astype(F32), 0, keepdims=True)


def expert_weights_kernel(xt_ref, gt_ref, active_ref, pre_ref, dw_ref):
    dw_ref[0, 0] = dot(xt_ref[...], pre_ref[...]).astype(BF16)
    dw_ref[0, 1] = dot(gt_ref[...], active_ref[...]).astype(BF16)


def whole(shape):
    return pl.BlockSpec(shape, lambda *i: (0,) * len(shape), pipeline_mode=pl.Buffered(1))


EXPERT_PARAMS = pltpu.CompilerParams(vmem_limit_bytes=58 * 1024 * 1024)


def expert_cost(kind, rows, width, hidden, pieces):
    return pl.CostEstimate(
        flops=2 * kind * rows * width * hidden * pieces,
        bytes_accessed=6 * rows * width * 4,
        transcendentals=0,
    )


def expert_first(x, u, cent, w):
    rows, width = x.shape
    pieces, unused, hidden, unused_width = w.shape
    tile = min(ROWS, rows)
    tiles = rows // tile
    units = pieces * hidden

    def tiled(cols):
        return pl.BlockSpec((tile, cols), lambda i: (jnp.minimum(i, tiles - 1), 0))

    wide = jax.ShapeDtypeStruct((rows, width), F32)
    turned = jax.ShapeDtypeStruct((width, rows), BF16)
    return pl.pallas_call(
        functools.partial(expert_first_kernel, tiles),
        grid=(tiles + pieces,),
        in_specs=[tiled(width), tiled(width), whole((1, width)), whole(w.shape)],
        out_specs=[
            tiled(width), tiled(width),
            pl.BlockSpec((1, 2, width, hidden), lambda i: (jnp.maximum(i - tiles, 0), 0, 0, 0)),
            tiled(width), whole(turned.shape), whole(turned.shape), tiled(1),
        ],
        out_shape=[
            wide, wide, jax.ShapeDtypeStruct((pieces, 2, width, hidden), BF16),
            jax.ShapeDtypeStruct((rows, width), BF16), turned, turned,
            jax.ShapeDtypeStruct((rows, 1), F32),
        ],
        scratch_shapes=[
            pltpu.VMEM((rows, units), BF16), pltpu.VMEM((rows, units), BF16),
            pltpu.VMEM((2, units, width), BF16),
        ],
        compiler_params=EXPERT_PARAMS,
        cost_estimate=expert_cost(6, rows, width, hidden, pieces),
        name="expert_first",
    )(x, u, cent, w)


def expert_last(x, g, u, gate, cent, out_sum, in_sum, w):
    rows, width = x.shape
    pieces, unused, hidden, unused_width = w.shape
    tile = min(ROWS, rows)
    units = pieces * hidden

    def tiled(cols):
        return pl.BlockSpec((tile, cols), lambda i: (i, 0))

    low = jax.ShapeDtypeStruct((rows, width), BF16)
    kept = jax.ShapeDtypeStruct((rows, units), BF16)
    return pl.pallas_call(
        expert_last_kernel,
        grid=(rows // tile,),
        in_specs=[tiled(width)] * 3
        + [tiled(1), whole((1, width)), tiled(width), tiled(width), whole(w.shape)],
        out_specs=[tiled(width), tiled(width), whole((1, width)), tiled(units), tiled(units)],
        out_shape=[low, low, jax.ShapeDtypeStruct((1, width), F32), kept, kept],
        scratch_shapes=[pltpu.VMEM((2, units, width), BF16)],
        compiler_params=EXPERT_PARAMS,
        cost_estimate=expert_cost(4, rows, width, hidden, pieces),
        name="expert_last",
    )(x, g, u, gate, cent, out_sum, in_sum, w)


def expert_weights(xt, gt, active, grad_pre, pieces):
    width, rows = xt.shape
    hidden = active.shape[1] // pieces
    kept_spec = pl.BlockSpec((rows, hidden), lambda i: (0, i))
    shape = (pieces, 2, width, hidden)
    return pl.pallas_call(
        expert_weights_kernel,
        grid=(pieces,),
        in_specs=[whole(xt.shape), whole(xt.shape), kept_spec, kept_spec],
        out_specs=pl.BlockSpec((1, *shape[1:]), lambda i: (i, 0, 0, 0)),
        out_shape=jax.ShapeDtypeStruct(shape, BF16),
        compiler_params=EXPERT_PARAMS,
        cost_estimate=expert_cost(2, rows, width, hidden, pieces),
        name="expert_weights",
    )(xt, gt, active, grad_pre)


def norm_back(values, gain, grad):
    centre = jnp.mean(values, -1, keepdims=True)
    centered = values - centre
    spread = jnp.mean(centered * centered, -1, keepdims=True)
    rate = lax.rsqrt(spread + EPSILON)
    standard = centered * rate
    u = grad * gain
    back = rate * (
        u - jnp.mean(u, -1, keepdims=True) - standard * jnp.mean(u * standard, -1, keepdims=True)
    )
    return standard, back


def combine_back_kernel(
    back_ref, target_ref, resid_ref, cot_ref, gain_ref, weight_ref,
    resid_grad_ref, attn_ref, mixed_grad_ref, sums_ref,
):
    @pl.when(pl.program_id(0) == 0)
    def _():
        sums_ref[...] = jnp.zeros_like(sums_ref)

    target = target_ref[...]
    slots = lax.broadcasted_iota(jnp.int32, (1, back_ref.shape[0]), 1)
    grad = dot((target == slots).astype(BF16), back_ref[...])
    standard, back_norm = norm_back(resid_ref[...], gain_ref[...], grad)
    upstream = jnp.where(target >= 0, cot_ref[...].astype(F32), 0.0)
    grad_resid = upstream + back_norm
    resid_grad_ref[...] = grad_resid
    low = grad_resid.astype(BF16)
    attn_ref[...] = low
    mixed_grad_ref[...] = dot_nt(low, weight_ref[...]).astype(BF16)
    sums_ref[0:1, :] += jnp.sum(grad * standard, 0, keepdims=True)
    sums_ref[1:2, :] += jnp.sum(grad, 0, keepdims=True)


def combine_back(back, target, resid, cot, gain, weight):
    length, width = resid.shape
    tile = min(QTILE, length)
    tiled = pl.BlockSpec((tile, width), lambda i: (i, 0))
    low = jax.ShapeDtypeStruct(resid.shape, BF16)
    return pl.pallas_call(
        combine_back_kernel,
        grid=(length // tile,),
        in_specs=[
            whole(back.shape), pl.BlockSpec((tile, 1), lambda i: (i, 0)), tiled, tiled,
            whole((1, width)), whole(weight.shape),
        ],
        out_specs=[tiled, tiled, tiled, whole((8, width))],
        out_shape=[
            jax.ShapeDtypeStruct(resid.shape, F32), low, low, jax.ShapeDtypeStruct((8, width), F32),
        ],
        compiler_params=EXPERT_PARAMS,
        cost_estimate=pl.CostEstimate(
            flops=2 * length * width * (back.shape[0] + width),
            bytes_accessed=20 * length * width,
            transcendentals=0,
        ),
        name="combine_back",
    )(back, target, resid, cot, gain.reshape(1, width), weight)


def combine_out_kernel(rows_ref, target_ref, gate_ref, resid_ref, out_ref):
    slots = lax.broadcasted_iota(jnp.int32, (1, rows_ref.shape[0]), 1)
    rows = dot((target_ref[...] == slots).astype(BF16), rows_ref[...])
    out_ref[0] = (resid_ref[...] + gate_ref[...] * rows).astype(BF16)


def combine_out(rows, target, gate, resid):
    length, width = resid.shape
    tile = min(QTILE, length)
    column = pl.BlockSpec((tile, 1), lambda i: (i, 0))
    return pl.pallas_call(
        combine_out_kernel,
        grid=(length // tile,),
        in_specs=[
            whole(rows.shape), column, column, pl.BlockSpec((tile, width), lambda i: (i, 0)),
        ],
        out_specs=pl.BlockSpec((1, tile, width), lambda i: (0, i, 0)),
        out_shape=jax.ShapeDtypeStruct((1, length, width), BF16),
        compiler_params=EXPERT_PARAMS,
        cost_estimate=pl.CostEstimate(
            flops=2 * length * width * rows.shape[0],
            bytes_accessed=8 * length * width,
            transcendentals=0,
        ),
        name="combine_out",
    )(rows, target, gate, resid)


def finish_experts_kernel(blocks, first_ref, second_ref, hidden_ref, down_ref):
    step = pl.program_id(0)
    for source, here in ((first_ref, step < blocks), (second_ref, step >= blocks)):

        @pl.when(here)
        def _():
            hidden_ref[0] = source[0, 0].astype(F32)
            down_ref[0] = source[0, 1].T.astype(F32)


def finish_experts(first, second):
    unused, two, width, size = second.shape
    blocks = first.shape[3] // size
    hidden = first.shape[3] + size
    return pl.pallas_call(
        functools.partial(finish_experts_kernel, blocks),
        grid=(blocks + 1,),
        in_specs=[
            pl.BlockSpec((1, 2, width, size), lambda i: (0, 0, 0, jnp.minimum(i, blocks - 1))),
            whole(second.shape),
        ],
        out_specs=[
            pl.BlockSpec((1, width, size), lambda i: (0, 0, i)),
            pl.BlockSpec((1, size, width), lambda i: (0, i, 0)),
        ],
        out_shape=[
            jax.ShapeDtypeStruct((1, width, hidden), F32),
            jax.ShapeDtypeStruct((1, hidden, width), F32),
        ],
        compiler_params=EXPERT_PARAMS,
        name="finish_experts",
    )(first, second)


def spread_kernel(
    near, moved, flag_ref, one_ref, one_other, two_ref, two_other,
    query_ref, key_ref, value_ref, output_ref, cent_ref, *vectors,
):
    step = pl.program_id(0)
    steps = pl.num_programs(0)
    half = query_ref.shape[0] // 2
    chains = ((one_ref, one_other), (two_ref, two_other))

    def halves(chain, block):
        cols = pl.ds(pl.multiple_of(block * PAIR, PAIR), PAIR)
        low, high = [side[:, cols].astype(F32) for side in chains[chain]]
        return jnp.where(flag_ref[0] == 0, low, high), jnp.where(flag_ref[0] == 0, high, low)

    for k, here in enumerate((step < near, step >= near)):

        @pl.when(here)
        def _():
            for i, at in enumerate((query_ref, key_ref, value_ref)):
                at[:half, :], at[half:, :] = halves(k, 3 * (step - near * k) + i)

    kept = steps - moved
    sums_at = 3 * (steps - near)
    for k, here in enumerate((step < kept, step >= kept)):

        @pl.when(here)
        def _():
            block = sums_at + 1 + step - kept if k else 3 * near + step
            output_ref[:half, :], output_ref[half:, :] = halves(k, block)

    @pl.when(step == 0)
    def _():
        side = jnp.concatenate([x.T for x in halves(1, sums_at)], 1)
        experts = cent_ref.shape[0]
        cent_ref[...] = side[:experts]
        for ref, row in vectors_of(vectors, experts):
            ref[...] = side[row]


def vectors_of(refs, experts):
    last = experts + 4 + -(experts + 4) % 8
    return zip(refs, range(last - 4, last))


def spread(flag, halves, width, near, moved, experts):
    pairs = width // PAIR
    out = jax.ShapeDtypeStruct((width, width), F32)
    vector = jax.ShapeDtypeStruct((width,), F32)
    return pl.pallas_call(
        functools.partial(spread_kernel, near, moved),
        grid=(pairs,),
        in_specs=[pl.BlockSpec(memory_space=pltpu.SMEM)]
        + [pl.BlockSpec(memory_space=pltpu.VMEM)] * 4,
        out_specs=[pl.BlockSpec((width, PAIR), lambda i: (0, i))] * 4
        + [whole((experts, width))]
        + [whole((width,))] * 4,
        out_shape=[out] * 4 + [jax.ShapeDtypeStruct((experts, width), F32)] + [vector] * 4,
        compiler_params=pltpu.CompilerParams(vmem_limit_bytes=32 * 1024 * 1024),
        name="spread",
    )(flag, *halves[0], *halves[1])


def normalize(values, gain, shift):
    centre = jnp.mean(values, -1, keepdims=True)
    centered = values - centre
    spread = jnp.mean(centered * centered, -1, keepdims=True)
    return centered * lax.rsqrt(spread + EPSILON) * gain + shift


def xor_pairs(size, flip):
    return [(i, i ^ flip) for i in range(size)]


def exchange(rows, blocks):
    shape = rows.shape
    return lax.all_to_all(
        rows.reshape(blocks, -1, shape[1]), "wide", split_axis=0, concat_axis=0, tiled=True
    ).reshape(shape)


def add_up(terms):
    return functools.reduce(lambda a, b: a + b, [t.astype(F32) for t in terms])


def reduce_halves(terms, flags, sizes, bits, beside=None):
    for i, (axis, flip) in enumerate(bits):
        flag = (lax.axis_index(axis) // flip) % 2
        half = terms[0].shape[0] // 2
        mine, theirs = [
            [lax.dynamic_slice_in_dim(t, f * half, half, 0) for t in terms] for f in (flag, 1 - flag)
        ]
        came = lax.ppermute(add_up(theirs).astype(BF16), axis, xor_pairs(sizes[axis], flip))
        if beside is not None and i == len(bits) - 1:
            came, *beside = lax.optimization_barrier((came, *beside))
        terms = [add_up([*mine, came])]
        flags.append(flag)
    return terms[0] if beside is None else (terms[0], *beside)


def gather_halves(total, flags, sizes, bits):
    for at in reversed(range(len(bits))):
        axis, flip = bits[at]
        other = lax.ppermute(total, axis, xor_pairs(sizes[axis], flip))
        total = jnp.where(
            flags[at] == 0, jnp.concatenate([total, other], 0), jnp.concatenate([other, total], 0)
        )
    return total


def gather_plane(one, two, flags, sizes, bits, work, operands):
    columns = two.shape[1]
    for at, (axis, flip) in enumerate(bits):
        back = len(bits) - 1 - at
        came = [
            lax.ppermute(one, bits[back][0], xor_pairs(sizes[bits[back][0]], bits[back][1])),
            lax.ppermute(two, axis, xor_pairs(sizes[axis], flip)),
        ]
        if at == 0:
            came, operands = lax.optimization_barrier((came, operands))
            done = work(*operands)
        if at == len(bits) - 1:
            came, done = lax.optimization_barrier((came, done))
        came_one, came_two = lax.optimization_barrier(came)
        one = jnp.where(
            flags[back] == 0, jnp.concatenate([one, came_one], 0), jnp.concatenate([came_one, one], 0)
        )
        two = jnp.where(
            flags[at] == 0, jnp.stack([two, came_two], at), jnp.stack([came_two, two], at)
        )
    return one, two.reshape(-1, columns), done


def make_shards(n_wide, n_narrow):
    sizes = {"wide": n_wide, "narrow": n_narrow}
    wide_bits = [("wide", 1 << i) for i in range(n_wide.bit_length() - 1)]
    narrow_bits = [("narrow", 1 << i) for i in range(n_narrow.bit_length() - 1)]

    def shards(
        block_in,
        seq_lengths,
        routes,
        first_gain,
        first_shift,
        query_weight,
        key_weight,
        value_weight,
        output_weight,
        second_gain,
        second_shift,
        centroids,
        hidden_weight,
        down_weight,
        cotangent,
    ):
        seqs_here, length, width = block_in.shape
        head_size = width // HEADS
        scale = head_size ** (-0.5)
        tokens = seqs_here * length
        experts_all = centroids.shape[1]
        capacity = 3 * tokens // (2 * experts_all)
        wide_here = lax.axis_index("wide")
        hidden_size = hidden_weight.shape[2]

        second = max(hidden_size // 3 // 128 * 128, 128)
        cuts = (0, hidden_size - second, hidden_size)
        hidden_t = hidden_weight[0].T
        packs = [
            jnp.stack([hidden_t[a:b], down_weight[0, a:b]], 0)[None]
            for a, b in zip(cuts, cuts[1:])
        ]
        packs[0], block_in, seq_lengths, routes, cotangent = lax.optimization_barrier(
            (packs[0], block_in, seq_lengths, routes, cotangent)
        )
        weights = [lax.all_gather(pack, "narrow", axis=0, tiled=True) for pack in packs]

        live = lax.broadcasted_iota(jnp.int32, (tokens,), 0) < seq_lengths[0]
        route = routes.reshape(tokens)
        expert_ids = lax.broadcasted_iota(jnp.int32, (tokens, experts_all), 1)
        picked = route[:, None] == expert_ids
        ones_live = (picked & live[:, None]).astype(jnp.int32)
        earlier = jnp.cumsum(ones_live, 0, dtype=jnp.int32) - ones_live
        slot = jnp.sum(earlier * ones_live, 1, dtype=jnp.int32)
        target = route * capacity + slot
        slot_ids = lax.broadcasted_iota(jnp.int32, (tokens, experts_all * capacity), 1)
        target = jnp.where(live, target, -1)[:, None]
        table = (target == slot_ids).astype(BF16)
        cot = cotangent.reshape(tokens, width)

        def to_slots(rows):
            return dot_tn(table, rows).astype(BF16)

        upstream_slots, block_in, *packs = lax.optimization_barrier(
            (to_slots(cot), block_in, *packs)
        )
        upstream_rows = exchange(upstream_slots, experts_all)

        qkv_weight = jnp.concatenate([query_weight, key_weight, value_weight], 1)
        inputs_wide = block_in.reshape(tokens, width).astype(F32)
        normed_low = normalize(inputs_wide, first_gain, first_shift).astype(BF16)
        projected = dot(normed_low, qkv_weight).astype(BF16)
        mixed, probs = attend(projected, seq_lengths, scale)
        mixed, upstream_rows = lax.optimization_barrier((mixed, upstream_rows))
        resid = inputs_wide + dot(mixed, output_weight)
        normed_second = normalize(resid, second_gain, second_shift).astype(BF16)

        pairs = width // PAIR
        counts = (pairs // 2, pairs // 3, pairs - pairs // 2 - pairs // 3)
        logits = dot(normed_second, centroids)
        gate = jax.nn.sigmoid(jnp.sum(jnp.where(picked, logits, 0.0), 1, keepdims=True))
        slots, normed_t, mixed_t, gate, target = lax.optimization_barrier(
            (to_slots(normed_second), normed_low.T, mixed.T, gate, target)
        )
        rows = exchange(slots, experts_all)
        own_centroid = lax.dynamic_slice_in_dim(centroids.T, wide_here, 1, 0).astype(F32)
        out_sum, in_sum, weight_grads, grad_rows, rows_t, grad_rows_t, row_gate = expert_first(
            rows, upstream_rows, own_centroid, weights[0]
        )
        out_low, back_rows, own_centroid_grad, *kept = expert_last(
            rows, grad_rows, upstream_rows, row_gate, own_centroid, out_sum, in_sum, weights[1]
        )
        back = exchange(back_rows, experts_all)
        more_weight_grads = expert_weights(rows_t, grad_rows_t, *kept, n_narrow)
        own_row = lax.broadcasted_iota(jnp.int32, (experts_all + 4 + -(experts_all + 4) % 8, 1), 0)
        sums = jnp.where(own_row == wide_here, own_centroid_grad, 0.0)
        sums, back = lax.optimization_barrier((sums, back))
        grad_resid, grad_attn, grad_mixed, second_sums = combine_back(
            back, target, resid, cot, second_gain, output_weight
        )
        out_low, more_weight_grads, grad_mixed = lax.optimization_barrier(
            (out_low, more_weight_grads, grad_mixed)
        )
        returned = exchange(out_low, experts_all)

        flag = wide_here % 2
        shared = (flag.reshape(1), projected, grad_mixed, probs, scale)
        core, plane, line = wide_bits[:1], wide_bits[1:], narrow_bits
        flags = [[flag], [flag]]

        def swap(half):
            return lax.ppermute(half, "wide", xor_pairs(n_wide, 1))

        first_summed = lax.psum_scatter(weight_grads, "narrow", scatter_dimension=0, tiled=True)
        mine_one, theirs_one, grads_one = attend_back(
            *shared, counts, 0, normed_t, mixed_t, grad_attn
        )
        came_one = swap(theirs_one)
        mine_two, theirs_two, grads_two = attend_back(*shared, counts, 1, normed_t)
        block_out = combine_out(returned, target, gate, resid)
        grads_two, block_out, came_one, more_weight_grads = lax.optimization_barrier(
            (grads_two, block_out, came_one, more_weight_grads)
        )
        last_summed = lax.psum_scatter(more_weight_grads, "narrow", scatter_dimension=0, tiled=True)
        mine_two, theirs_two, input_grad = attend_back(
            *shared, counts, 2, normed_t, grads_one, grads_two, query_weight, key_weight, value_weight, block_in,
            first_gain.reshape(1, width), grad_resid, sums, second_sums, mine_two, theirs_two,
        )
        chain_one, mine_two, theirs_two, first_summed = reduce_halves(
            [mine_one, came_one], flags[0], sizes, plane[:1], (mine_two, theirs_two, first_summed)
        )
        chain_two = [mine_two, swap(theirs_two)]
        chain_one = reduce_halves([chain_one], flags[0], sizes, plane[1:] + line)
        chain_two = reduce_halves(chain_two, flags[1], sizes, plane[:1])
        chain_two, last_summed = reduce_halves(
            [chain_two], flags[1], sizes, plane[1:] + line, (last_summed,)
        )
        near = [
            gather_halves(total.astype(BF16), kept[len(wide_bits) :], sizes, line)
            for total, kept in zip((chain_one, chain_two), flags)
        ]
        inner = [kept[1 : len(wide_bits)] for kept in flags]
        moved = pairs // 3
        near_cols = near[0].shape[1] - moved * PAIR
        near = [near[0][:, :near_cols], jnp.concatenate([near[1], near[0][:, near_cols:]], 1)]
        *near, (hidden_grad, down_grad) = gather_plane(
            *near, inner[0], sizes, plane, finish_experts, (first_summed, last_summed)
        )
        halves = [(half, swap(half)) for half in near]
        query_grad, key_grad, value_grad, output_weight_grad, centroids_grad, *vectors = spread(
            flag.reshape(1), halves, width, counts[0], moved, experts_all
        )
        centroids_grad = centroids_grad.T
        second_gain_grad, second_shift_grad, first_gain_grad, first_shift_grad = vectors
        return (
            block_out,
            input_grad,
            first_gain_grad,
            first_shift_grad,
            query_grad,
            key_grad,
            value_grad,
            output_weight_grad,
            second_gain_grad,
            second_shift_grad,
            centroids_grad,
            hidden_grad,
            down_grad,
        )

    return shards


def solution(mesh):
    tokens_spec = P(("wide", "narrow"), None, None)
    in_specs = (
        tokens_spec,
        P(("wide", "narrow")),
        tokens_spec,
        *[P()] * 9,
        P("wide", None, "narrow"),
        P("wide", "narrow", None),
        tokens_spec,
    )
    out_specs = (
        tokens_spec,
        tokens_spec,
        *[P()] * 9,
        P("wide", None, "narrow"),
        P("wide", "narrow", None),
    )
    return jax.shard_map(
        make_shards(mesh.shape["wide"], mesh.shape["narrow"]),
        mesh=mesh,
        in_specs=in_specs,
        out_specs=out_specs,
        check_vma=False,
    )
```

time: 470 us -> 435 us (0.926)
  waiting for transfers between devices: 164 us -> 143 us
  matrix products: 26.8 us -> 20.5 us
  Pallas kernels: 181 us -> 175 us
    ppermute x10 -> x4, waiting for transfers between devices: 30.9 us -> 10.1 us  [gather_halves(): other = lax.ppermute(total, axis, xor_pairs(sizes[axis], flip))]
    optimization_barrier x0 -> x3, local copies, waits for them, and re-layouts: none -> 14.5 us  [the longest x1 12.7 us: shards(): mixed, upstream_rows = lax.optimization_barrier((mixed, upstream_rows))]
    all_gather x3 -> x2, waiting for transfers between devices: 45.4 us -> 31.5 us  [shards(): lax.all_gather(pack, 'narrow', axis=0, tiled=True)]
    pallas_call x4 -> x6, Pallas kernels: 82.1 us -> 68.8 us  [the longest x3 53.2 us: attend_back(): pl.pallas_call(functools.partial(attend_back_kernel, scale, counts, part)...]
    ppermute x10 -> x16, waiting for transfers between devices: 48.7 us -> 56.2 us  [the longest x8 37.2 us: reduce_halves(): lax.ppermute(add_up(theirs).astype(BF16), axis, xor_pairs(sizes[axis], fl...]
    pallas_call x1, Pallas kernels: 37.5 us -> 44.6 us  [expert_first(): pl.pallas_call(functools.partial(expert_first_kernel, tiles), grid=(tiles...]
    unnamed x53 -> x43, local copies, waits for them, and re-layouts: 11.6 us -> 5.48 us
    pallas_call x1, Pallas kernels: 14.1 us -> 19.3 us  [expert_last(): pl.pallas_call(expert_last_kernel, grid=(rows // tile,), in_specs=[tiled(...]
  transfers between devices with their start and end apart: 29 -> 28, of which waited for: 17 -> 19; matrix products, arithmetic and copies ran while one was open for 13% -> 13% of each run, Pallas kernels for 37% -> 40%
where the time goes in v2:
time: 435 us; the launch traced here: 431 us
  Pallas kernels  175 us (40%)
  waiting for transfers between devices  143 us (33%)
  starting transfers between devices  32 us (7%)
  local copies, waits for them, and re-layouts  27.8 us (6%)
  matrix products  20.5 us (5%)
  other arithmetic  18.3 us (4%)
  between operations  15.2 us (3%)
    pallas_call x3, Pallas kernels, attend_back(): pl.pallas_call(functools.partial(attend_back_kernel, scale, counts, part)...  53.2 us
    pallas_call x1, Pallas kernels, expert_first(): pl.pallas_call(functools.partial(expert_first_kernel, tiles), grid=(tiles...  44.6 us
    all_to_all x4, waiting for transfers between devices, exchange(): lax.all_to_all(rows.reshape(blocks, -1, shape[1]), 'wide', split_axis=0,...  43.9 us
    ppermute x8, waiting for transfers between devices, reduce_halves(): lax.ppermute(add_up(theirs).astype(BF16), axis, xor_pairs(sizes[axis], fl...  37.2 us
    all_gather x2, waiting for transfers between devices, shards(): lax.all_gather(pack, 'narrow', axis=0, tiled=True)  31.5 us
    pallas_call x1, Pallas kernels, attend(): pl.pallas_call(functools.partial(attend_kernel, scale), grid_spec=pltpu.P...  22.3 us
    pallas_call x1, Pallas kernels, expert_last(): pl.pallas_call(expert_last_kernel, grid=(rows // tile,), in_specs=[tiled(...  19.3 us
    all_to_all x4, starting transfers between devices, exchange(): lax.all_to_all(rows.reshape(blocks, -1, shape[1]), 'wide', split_axis=0,...  18.4 us
  transfers between devices with their start and end apart: 28, of which 19 were waited for; matrix products, arithmetic and copies ran while one was open for 13% of the time, Pallas kernels for 40%

profile of v2, /device:TPU:0, one launch (start us, length us, event | category | flops | bytes accessed | tf_op | source)
XLA Modules:
  0.0 431.4 jit_solution(5919975989817183485)
XLA Ops:
  7.2 1.6 copy.43
  8.9 1.5 slice-done
  12.4 2.3 reduce-window.6
  15.2 4.7 %fusion.11 = bf16[1536,768]{1,0:T(8,128)(2,1)} fusion(s32[1024]{0:T(1024)S(1)} %add_select_fusion.1, bf16[1,1024,768]{2,1,0:T(8,128)(2,1)S(1)} %copy-done.20), kind=kOutput, calls=%fused_computation.16 | convolution fusion | flops 2418671616 | bytes 3936256 | tf_op jit(solution)/shard_map/dot_general | solution.py:23
  20.0 5.7 %all-to-all-start = ((bf16[8,192,768]{2,1,0:T(8,128)(2,1)}), bf16[8,192,768]{2,1,0:T(8,128)(2,1)}, u32[]{:S(2)}, u32[]{:S(2)}) async-start(bf16[8,192,768]{2,1,0:T(8,128)(2,1)} %bitcast.105), calls=%async_computation | async-start | bytes 4718592 | tf_op jit(solution)/shard_map/all_to_all | solution.py:681
  29.7 8.3 %convolution_convert_fusion.q_ref.k_ref.v_ref = bf16[1024,2304]{1,0:T(8,128)(2,1)} fusion(bf16[768,768]{1,0:T(8,128)(2,1)} %refs_4_.1, bf16[768,768]{1,0:T(8,128)(2,1)} %refs_3_.1, bf16[768,768]{1,0:T(8,128)(2,1)} %refs_2_.1, bf16[1,1024,768]{1,2,0:T(8,128)(2,1)S(1)} %copy.44, f32[768]{0:T(1024)S(1)} %copy-done.14, f32[768]{0:T(1024)S(1)} %copy-done.11, ...), kind=kOutput, calls=%fused_computation.3 | convolution fusion | flops 3641573376 | bytes 9844736 | tf_op jit(solution)/shard_map/dot_general | solution.py:19
  37.9 22.3 %attend.1 = (bf16[1024,768]{1,0:T(8,128)(2,1)S(1)}, bf16[6,2,2560,256]{3,2,1,0:T(8,128)(2,1)}) custom-call(s32[1]{0:T(128)} %copy.55.len_ref, bf16[1024,2304]{1,0:T(8,128)(2,1)} %convolution_convert_fusion.q_ref.k_ref.v_ref, bf16[1024,2304]{1,0:T(8,128)(2,1)} %convolution_convert_fusion.q_ref.k_ref.v_ref, ...), custom_call_target="tpu_custom_call" | custom-call | flops 3221225472 | bytes 6291456 | tf_op jit(solution)/shard_map/attend/pallas_call | solution.py:75
  60.2 1.8 fusion.32.normed_t
  62.0 12.7 %copy.45 = bf16[1024,768]{0,1:T(8,128)(2,1)} copy(bf16[1024,768]{1,0:T(8,128)(2,1)S(1)} %get-tuple-element.100) | data formatting | bytes 3145728 | tf_op jit(solution)/shard_map/optimization_barrier | solution.py:807
  74.7 2.8 fusion.34
  79.5 4.3 %convolution_convert_fusion.1 = bf16[1536,768]{1,0:T(8,128)(2,1)} fusion(bf16[1024,768]{0,1:T(8,128)(2,1)S(1)} %add_convert_fusion, s32[1024]{0:T(1024)S(1)} %copy-done.18), kind=kOutput, calls=%fused_computation.15 | convolution fusion | flops 2420244480 | bytes 3936256 | tf_op jit(solution)/shard_map/dot_general | solution.py:23
  83.8 4.4 %all-to-all-start.1 = ((bf16[8,192,768]{2,1,0:T(8,128)(2,1)}), bf16[8,192,768]{2,1,0:T(8,128)(2,1)S(1)}, u32[]{:S(2)}, u32[]{:S(2)}) async-start(bf16[8,192,768]{2,1,0:T(8,128)(2,1)} %bitcast.103), calls=%async_computation.1 | async-start | bytes 4718592 | tf_op jit(solution)/shard_map/all_to_all | solution.py:681
  89.9 27.8 %all-to-all-done.1 = bf16[8,192,768]{2,1,0:T(8,128)(2,1)S(1)} async-done(((bf16[8,192,768]{2,1,0:T(8,128)(2,1)}), bf16[8,192,768]{2,1,0:T(8,128)(2,1)S(1)}, u32[]{:S(2)}, u32[]{:S(2)}) %all-to-all-start.1) | async-done | bytes 2359328 | tf_op jit(solution)/shard_map/all_to_all | solution.py:681
  117.7 12.2 %all-gather.4.cloned.1.call-done.w_ref = bf16[4,2,512,768]{3,2,1,0:T(8,128)(2,1)} async-done(((bf16[1,2,512,768]{3,2,1,0:T(8,128)(2,1)}), bf16[4,2,512,768]{3,2,1,0:T(8,128)(2,1)}) %all-gather.4.cloned.1.call-update) | async-done | bytes 6291472 | tf_op jit(solution)/shard_map/all_gather | solution.py:779
  129.9 44.6 %expert_first.1 = (f32[1536,768]{1,0:T(8,128)}, f32[1536,768]{1,0:T(8,128)}, bf16[4,2,768,512]{3,2,1,0:T(8,128)(2,1)}, bf16[1536,768]{1,0:T(8,128)(2,1)}, bf16[7...) custom-call(bf16[1536,768]{1,0:T(8,128)(2,1)} %bitcast.100, bf16[1536,768]{1,0:T(8,128)(2,1)} %bitcast.12.u_ref, ...), custom_call_target="tpu_custom_call" | custom-call | flops 28991029248 | bytes 28311552 | tf_op jit(solution)/shard_map/expert_first/pallas_call | solution.py:417
  174.5 19.3 %all-gather.6.cloned.1.call-done = bf16[8,256,768]{2,1,0:T(8,128)(2,1)} async-done(((bf16[2,256,768]{2,1,0:T(8,128)(2,1)}), bf16[8,256,768]{2,1,0:T(8,128)(2,1)}) %all-gather.6.cloned.1.call-update) | async-done | bytes 3145744 | tf_op jit(solution)/shard_map/all_gather | solution.py:779
  193.8 19.3 %expert_last.1 = (bf16[1536,768]{1,0:T(8,128)(2,1)}, bf16[1536,768]{1,0:T(8,128)(2,1)}, f32[1,768]{1,0:T(1,128)}, bf16[1536,1024]{1,0:T(8,128)(2,1)}, bf16[1536,1024]{1,0:T(8,128)(2,1)}) custom-call(bf16[1536,768]{1,0:T(8,128)(2,1)} %bitcast.101, bf16[1536,768]{1,0:T(8,128)(2,1)} %get-tuple-element.103.g_ref, bf16[1536,768]{1,0:T(8,128)(2,1)} %bitcast.12.u_ref, ...), custom_call_target="tpu_custom_call" | custom-call | flops 9663676416 | bytes 28311552 | tf_op jit(solution)/shard_map/expert_last/pallas_call | solution.py:452
  213.1 4.7 %all-to-all-start.2 = ((bf16[8,192,768]{2,1,0:T(8,128)(2,1)}), bf16[8,192,768]{2,1,0:T(8,128)(2,1)}, u32[]{:S(2)}, u32[]{:S(2)}) async-start(bf16[8,192,768]{2,1,0:T(8,128)(2,1)} %bitcast.104), calls=%async_computation.2 | async-start | bytes 4718592 | tf_op jit(solution)/shard_map/all_to_all | solution.py:681
  218.4 2.4 copy.48.resid_ref
  221.5 9.7 %expert_weights.1 = bf16[4,2,768,256]{3,2,1,0:T(8,128)(2,1)} custom-call(bf16[768,1536]{1,0:T(8,128)(2,1)} %get-tuple-element.108.xt_ref, bf16[768,1536]{1,0:T(8,128)(2,1)} %get-tuple-element.109.gt_ref, bf16[1536,1024]{1,0:T(8,128)(2,1)} %get-tuple-element.110.active_ref, bf16[1536,1024]{1,0:T(8,128)(2,1)} %get-tuple-element.111.pre_ref), custom_call_target="tpu_custom_call" | custom-call | flops 4831838208 | bytes 28311552 | tf_op jit(solution)/shard_map/expert_weights/pallas_call | solution.py:471
  231.2 16.1 %all-to-all-done.2 = bf16[8,192,768]{2,1,0:T(8,128)(2,1)} async-done(((bf16[8,192,768]{2,1,0:T(8,128)(2,1)}), bf16[8,192,768]{2,1,0:T(8,128)(2,1)}, u32[]{:S(2)}, u32[]{:S(2)}) %all-to-all-start.2) | async-done | bytes 2359328 | tf_op jit(solution)/shard_map/all_to_all | solution.py:681
  247.3 10.3 %combine_back.1 = (f32[1024,768]{1,0:T(8,128)}, bf16[1024,768]{1,0:T(8,128)(2,1)}, bf16[1024,768]{1,0:T(8,128)(2,1)}, f32[8,768]{1,0:T(8,128)}) custom-call(bf16[1536,768]{1,0:T(8,128)(2,1)} %bitcast.25.back_ref, s32[1024,1]{1,0:T(8,128)} %add_select_fusion.target_ref, f32[1024,768]{1,0:T(8,128)} %copy.48.resid_ref, bf16[1024,768]{1,0:T(8,128)(2,1)} %bitcast.117, ...), custom_call_target="tpu_custom_call" | custom-call | flops 3623878656 | bytes 15728640 | tf_op jit(solution)/shard_map/combine_back/pallas_call | solution.py:523
  257.5 3.6 all-to-all-start.3
  261.2 21.6 %attend_back.4 = (f32[384,1920]{1,0:T(8,128)}, bf16[384,1920]{1,0:T(8,128)(2,1)}, bf16[3,1024,384]{2,1,0:T(8,128)(2,1)}) custom-call(s32[1]{0:T(128)} %bitcast.flag_ref, bf16[1024,2304]{1,0:T(8,128)(2,1)} %convolution_convert_fusion.q_ref.k_ref.v_ref, bf16[1024,2304]{1,0:T(8,128)(2,1)} %convolution_convert_fusion.q_ref.k_ref.v_ref, ...), custom_call_target="tpu_custom_call" | custom-call | flops 8053063680 | bytes 5505024 | tf_op jit(solution)/shard_map/attend_back/pallas_call | solution.py:277
  284.2 13.3 %attend_back.3 = (f32[384,1280]{1,0:T(8,128)}, bf16[384,1280]{1,0:T(8,128)(2,1)}, bf16[3,1024,256]{2,1,0:T(8,128)(2,1)}) custom-call(s32[1]{0:T(128)} %bitcast.flag_ref, bf16[1024,2304]{1,0:T(8,128)(2,1)} %convolution_convert_fusion.q_ref.k_ref.v_ref, bf16[1024,2304]{1,0:T(8,128)(2,1)} %convolution_convert_fusion.q_ref.k_ref.v_ref, ...), custom_call_target="tpu_custom_call" | custom-call | flops 5368709120 | bytes 3670016 | tf_op jit(solution)/shard_map/attend_back/pallas_call | solution.py:277
  297.5 1.4 copy-done.7
  298.9 7.1 %combine_out.1 = bf16[1,1024,768]{2,1,0:T(8,128)(2,1)} custom-call(bf16[1536,768]{1,0:T(8,128)(2,1)} %bitcast.102, s32[1024,1]{1,0:T(8,128)} %add_select_fusion.target_ref, f32[1024,1]{1,0:T(8,128)} %copy.49.gate_ref, f32[1024,768]{1,0:T(8,128)} %copy.48.resid_ref), custom_call_target="tpu_custom_call" | custom-call | flops 2415919104 | bytes 6291456 | tf_op jit(solution)/shard_map/combine_out/pallas_call | solution.py:554
  306.1 1.8 copy-done.5
  309.1 1.8 collective-permute-start.1
  311.4 18.3 %attend_back.5 = (f32[384,1280]{1,0:T(8,128)}, bf16[384,1280]{1,0:T(8,128)(2,1)}, bf16[1,1024,768]{2,1,0:T(8,128)(2,1)}) custom-call(s32[1]{0:T(128)} %bitcast.flag_ref, bf16[1024,2304]{1,0:T(8,128)(2,1)} %convolution_convert_fusion.q_ref.k_ref.v_ref, ...), custom_call_target="tpu_custom_call", output_to_operand_aliasing={{0}: (17, {}), {1}: (18, {})} | custom-call | flops 2684354560 | bytes 1835008 | tf_op jit(solution)/shard_map/attend_back/pallas_call | solution.py:277
  329.9 2.2 convert_add_fusion
  332.8 1.5 collective-permute-start.2
  335.7 8.3 %collective-permute-done.2 = bf16[96,1920]{1,0:T(8,128)(2,1)} collective-permute-done((bf16[96,1920]{1,0:T(8,128)(2,1)}, bf16[96,1920]{1,0:T(8,128)(2,1)}, u32[]{:S(2)}, u32[]{:S(2)}) %collective-permute-start.2) | collective-permute-done | bytes 368672 | tf_op jit(solution)/shard_map/ppermute | solution.py:697
  345.2 3.5 collective-permute-done.9
  350.5 9.6 %collective-permute-done.3 = bf16[48,1920]{1,0:T(8,128)(2,1)S(1)} collective-permute-done((bf16[48,1920]{1,0:T(8,128)(2,1)S(1)}, bf16[48,1920]{1,0:T(8,128)(2,1)S(1)}, u32[]{:S(2)}, u32[]{:S(2)}) %collective-permute-start.3) | collective-permute-done | bytes 184352 | tf_op jit(solution)/shard_map/ppermute | solution.py:697
  361.6 11.4 %collective-permute-done.11 = bf16[48,1280]{1,0:T(8,128)(2,1)S(1)} collective-permute-done((bf16[48,1280]{1,0:T(8,128)(2,1)S(1)}, bf16[48,1280]{1,0:T(8,128)(2,1)S(1)}, u32[]{:S(2)}, u32[]{:S(2)}) %collective-permute-start.11) | collective-permute-done | bytes 122912 | tf_op jit(solution)/shard_map/ppermute | solution.py:697
  373.1 3.0 collective-permute-start.5
  376.9 4.4 %collective-permute-done.12 = bf16[24,1280]{1,0:T(8,128)(2,1)S(1)} collective-permute-done((bf16[24,1280]{1,0:T(8,128)(2,1)S(1)}, bf16[24,1280]{1,0:T(8,128)(2,1)S(1)}, u32[]{:S(2)}, u32[]{:S(2)}) %collective-permute-start.12) | collective-permute-done | bytes 61472 | tf_op jit(solution)/shard_map/ppermute | solution.py:697
  381.4 2.5 collective-permute-done.5
  384.1 2.6 collective-permute-done.13
  386.7 4.8 %collective-permute-done.6 = bf16[48,1920]{1,0:T(8,128)(2,1)S(1)} collective-permute-done((bf16[48,1920]{1,0:T(8,128)(2,1)S(1)}, bf16[48,1920]{1,0:T(8,128)(2,1)S(1)}, u32[]{:S(2)}, u32[]{:S(2)}) %collective-permute-start.6) | collective-permute-done | bytes 184352 | tf_op jit(solution)/shard_map/ppermute | solution.py:708
  393.6 5.2 %collective-permute-done.7 = bf16[96,1664]{1,0:T(8,128)(2,1)S(1)} collective-permute-done((bf16[96,1664]{1,0:T(8,128)(2,1)S(1)}, bf16[96,1664]{1,0:T(8,128)(2,1)S(1)}, u32[]{:S(2)}, u32[]{:S(2)}) %collective-permute-start.7) | collective-permute-done | bytes 319520 | tf_op jit(solution)/shard_map/ppermute | solution.py:720
  398.7 2.0 collective-permute-done.15
  401.4 1.5 collective-permute-start.17
  402.9 4.0 finish_experts.1
  407.0 7.1 %collective-permute-done.17 = bf16[2,96,1536]{2,1,0:T(8,128)(2,1)S(1)} collective-permute-done((bf16[2,96,1536]{2,1,0:T(8,128)(2,1)S(1)}, bf16[2,96,1536]{2,1,0:T(8,128)(2,1)S(1)}, u32[]{:S(2)}, u32[]{:S(2)}) %collective-permute-start.17) | collective-permute-done | bytes 589856 | tf_op jit(solution)/shard_map/ppermute | solution.py:721
  416.2 3.9 collective-permute-done.19.two_other
  420.1 4.5 %spread.1 = (f32[768,768]{1,0:T(8,128)}, f32[768,768]{1,0:T(8,128)}, f32[768,768]{1,0:T(8,128)}, f32[768,768]{1,0:T(8,128)}, f32[8,768]{1,0:T(8,128)}, /*index=5...) custom-call(s32[1]{0:T(128)} %bitcast.flag_ref, bf16[384,1664]{1,0:T(8,128)(2,1)S(1)} %maximum_select_fusion.one_ref, ...), custom_call_target="tpu_custom_call" | custom-call | tf_op jit(solution)/shard_map/spread/pallas_call | solution.py:654
  (140 shorter events, 26.7 us)
Async XLA Ops:
  7.2 122.7 %all-gather.4.cloned.1.call-start = ((), (), s32[]{:S(2)}) async-start(), calls=%async_computation.6 | async-start | bytes 7864320 | tf_op jit(solution)/shard_map/all_gather | solution.py:779
  8.8 2.9 copy-start.4
  8.8 1.6 slice-start
  10.4 2.0 copy-start.8
  10.4 4.8 %copy-start.20 = (bf16[1,1024,768]{2,1,0:T(8,128)(2,1)S(1)}, bf16[1,1024,768]{2,1,0:T(8,128)(2,1)}, u32[]{:S(2)}) copy-start(bf16[1,1024,768]{2,1,0:T(8,128)(2,1)} %param.29) | copy-start | bytes 4718596
  15.2 4.7 %copy-start.17 = (s32[1024]{0:T(1024)}, s32[1024]{0:T(1024)S(1)}, u32[]{:S(2)}) copy-start(s32[1024]{0:T(1024)S(1)} %add_select_fusion.1) | copy-start | bytes 12292
  20.0 5.7 %copy-start.3 = (bf16[1,1024,768]{2,1,0:T(8,128)(2,1)S(1)}, bf16[1,1024,768]{2,1,0:T(8,128)(2,1)}, u32[]{:S(2)}) copy-start(bf16[1,1024,768]{2,1,0:T(8,128)(2,1)} %refs_5_) | copy-start | bytes 4718596
  20.0 42.0 %all-to-all-start = ((bf16[8,192,768]{2,1,0:T(8,128)(2,1)}), bf16[8,192,768]{2,1,0:T(8,128)(2,1)}, u32[]{:S(2)}, u32[]{:S(2)}) async-start(bf16[8,192,768]{2,1,0:T(8,128)(2,1)} %bitcast.105), calls=%async_computation | async-start | bytes 4718592 | tf_op jit(solution)/shard_map/all_to_all | solution.py:681
  27.2 2.4 copy-start.11
  27.2 2.4 copy-start.14
  28.3 1.4 copy-start.12
  37.9 22.3 %copy-start.13 = (f32[1024]{0:T(1024)S(1)}, f32[1024]{0:T(1024)}, u32[]{:S(2)}) copy-start(f32[1024]{0:T(1024)} %copy-done.12) | copy-start | bytes 12292
  37.9 22.3 %copy-start.15 = (f32[768]{0:T(1024)S(1)}, f32[768]{0:T(1024)}, u32[]{:S(2)}) copy-start(f32[768]{0:T(1024)} %param.19) | copy-start | bytes 9220
  77.5 1.6 copy-start
  78.3 1.2 copy-start.18
  83.8 4.4 %slice-start.1 = ((bf16[1,768,768]{2,1,0:T(8,128)(2,1)}), bf16[1,256,768]{2,1,0:T(8,128)(2,1)S(1)}, s32[]{:S(2)}) async-start(bf16[1,768,768]{2,1,0:T(8,128)(2,1)} %param.28), calls=%async_computation.11 | async-start | bytes 786432 | tf_op jit(solution)/shard_map/slice | solution.py:773
  83.8 33.8 %all-to-all-start.1 = ((bf16[8,192,768]{2,1,0:T(8,128)(2,1)}), bf16[8,192,768]{2,1,0:T(8,128)(2,1)S(1)}, u32[]{:S(2)}, u32[]{:S(2)}) async-start(bf16[8,192,768]{2,1,0:T(8,128)(2,1)} %bitcast.103), calls=%async_computation.1 | async-start | bytes 4718592 | tf_op jit(solution)/shard_map/all_to_all | solution.py:681
  88.2 105.6 %all-gather.6.cloned.1.call-start = ((), (), s32[]{:S(2)}) async-start(), calls=%async_computation.9 | async-start | bytes 3932160 | tf_op jit(solution)/shard_map/all_gather | solution.py:779
  89.3 240.5 %reduce-scatter.3.cloned.1.call-start = ((), (), s32[]{:S(2)}) async-start(), calls=%async_computation.7 | async-start | bytes 7864320 | tf_op jit(solution)/shard_map/reduce_scatter | solution.py:847
  117.7 12.2 %copy-start.6 = (bf16[8,192,768]{2,1,0:T(8,128)(2,1)}, bf16[8,192,768]{2,1,0:T(8,128)(2,1)S(1)}, u32[]{:S(2)}) copy-start(bf16[8,192,768]{2,1,0:T(8,128)(2,1)S(1)} %all-to-all-done.1) | copy-start | bytes 7077892
  213.1 5.3 %copy-start.1 = (f32[1024,768]{0,1:T(8,128)S(1)}, f32[1024,768]{0,1:T(8,128)}, u32[]{:S(2)}) copy-start(f32[1024,768]{0,1:T(8,128)} %copy-done) | copy-start | bytes 9437188
  213.1 34.1 %all-to-all-start.2 = ((bf16[8,192,768]{2,1,0:T(8,128)(2,1)}), bf16[8,192,768]{2,1,0:T(8,128)(2,1)}, u32[]{:S(2)}, u32[]{:S(2)}) async-start(bf16[8,192,768]{2,1,0:T(8,128)(2,1)} %bitcast.104), calls=%async_computation.2 | async-start | bytes 4718592 | tf_op jit(solution)/shard_map/all_to_all | solution.py:681
  218.4 2.4 copy-start.19
  257.5 40.0 %all-to-all-start.3 = ((bf16[8,192,768]{2,1,0:T(8,128)(2,1)}), bf16[8,192,768]{2,1,0:T(8,128)(2,1)S(1)}, u32[]{:S(2)}, u32[]{:S(2)}) async-start(bf16[8,192,768]{2,1,0:T(8,128)(2,1)} %bitcast.26), calls=%async_computation.3 | async-start | bytes 4718592 | tf_op jit(solution)/shard_map/all_to_all | solution.py:681
  261.2 115.7 %reduce-scatter.5.cloned.1.call-start = ((), (), s32[]{:S(2)}) async-start(), calls=%async_computation.8 | async-start | bytes 3932160 | tf_op jit(solution)/shard_map/reduce_scatter | solution.py:857
  282.9 23.1 %collective-permute-start = (bf16[384,1920]{1,0:T(8,128)(2,1)}, bf16[384,1920]{1,0:T(8,128)(2,1)}, u32[]{:S(2)}, u32[]{:S(2)}) collective-permute-start(bf16[384,1920]{1,0:T(8,128)(2,1)} %get-tuple-element.125), channel_id=1, source_target_pairs={{0,4},{4,0},{8,12},{12,8},{16,20},{20,16},{24,28},{28,24},{1,5},{5... | collective-permute-start | bytes 4423688 | tf_op jit(solution)/shard_map/ppermute | solution.py:845
  297.5 1.4 copy-start.7
  306.0 1.8 copy-start.5
  309.1 20.6 %collective-permute-start.1 = (bf16[192,1920]{1,0:T(8,128)(2,1)S(1)}, bf16[192,1920]{1,0:T(8,128)(2,1)}, u32[]{:S(2)}, u32[]{:S(2)}) collective-permute-start(bf16[192,1920]{1,0:T(8,128)(2,1)S(1)} %add_convert_fusion.1), channel_id=1, source_target_pairs={{0,8},{4,12},{8,0},{12,4},{16,24},{20,28},{24,16},{28,20},{1,9},{5... | collective-permute-start | bytes 2211848 | tf_op jit(solution)/shard_map/ppermute | solution.py:697
  329.7 4.6 %collective-permute-start.8 = (bf16[384,1280]{1,0:T(8,128)(2,1)}, bf16[384,1280]{1,0:T(8,128)(2,1)}, u32[]{:S(2)}, u32[]{:S(2)}) collective-permute-start(bf16[384,1280]{1,0:T(8,128)(2,1)} %get-tuple-element.143), channel_id=1, source_target_pairs={{0,4},{4,0},{8,12},{12,8},{16,20},{20,16},{24,28},{28,24},{1,5},{5... | collective-permute-start | bytes 2949128 | tf_op jit(solution)/shard_map/ppermute | solution.py:845
  329.9 4.5 %copy-start.2 = (f32[384,1280]{1,0:T(8,128)S(1)}, f32[384,1280]{1,0:T(8,128)}, u32[]{:S(2)}) copy-start(f32[384,1280]{1,0:T(8,128)} %get-tuple-element.142) | copy-start | bytes 5898244
  332.8 11.2 %collective-permute-start.2 = (bf16[96,1920]{1,0:T(8,128)(2,1)}, bf16[96,1920]{1,0:T(8,128)(2,1)}, u32[]{:S(2)}, u32[]{:S(2)}) collective-permute-start(bf16[96,1920]{1,0:T(8,128)(2,1)} %dynamic-slice_convert_fusion), channel_id=1, source_target_pairs={{0,16},{4,20},{8,24},{12,28},{16,0},{20,4},{24,8},{28,12},{1,17},{... | collective-permute-start | bytes 1105928 | tf_op jit(solution)/shard_map/ppermute | solution.py:697
  335.5 13.3 %collective-permute-start.9 = (bf16[192,1280]{1,0:T(8,128)(2,1)S(1)}, bf16[192,1280]{1,0:T(8,128)(2,1)S(1)}, u32[]{:S(2)}, u32[]{:S(2)}) collective-permute-start(bf16[192,1280]{1,0:T(8,128)(2,1)S(1)} %add_convert_fusion.2), channel_id=1, source_target_pairs={{0,8},{4,12},{8,0},{12,4},{16,24},{20,28},{24,16},{28,20},{1,9},{5... | collective-permute-start | bytes 1474568 | tf_op jit(solution)/shard_map/ppermute | solution.py:697
  345.1 15.0 %collective-permute-start.3 = (bf16[48,1920]{1,0:T(8,128)(2,1)S(1)}, bf16[48,1920]{1,0:T(8,128)(2,1)S(1)}, u32[]{:S(2)}, u32[]{:S(2)}) collective-permute-start(bf16[48,1920]{1,0:T(8,128)(2,1)S(1)} %dynamic-slice_convert_fusion.2), channel_id=1, source_target_pairs={{0,1},{1,0},{2,3},{3,2},{4,5},{5,4},{6,7},{7,6},{8,9},{9,8},{10,11... | collective-permute-start | bytes 552968 | tf_op jit(solution)/shard_map/ppermute | solution.py:697
  349.9 10.2 %collective-permute-start.10 = (bf16[96,1280]{1,0:T(8,128)(2,1)S(1)}, bf16[96,1280]{1,0:T(8,128)(2,1)S(1)}, u32[]{:S(2)}, u32[]{:S(2)}) collective-permute-start(bf16[96,1280]{1,0:T(8,128)(2,1)S(1)} %dynamic-slice_convert_fusion.1), channel_id=1, source_target_pairs={{0,16},{4,20},{8,24},{12,28},{16,0},{20,4},{24,8},{28,12},{1,17},{... | collective-permute-start | bytes 737288 | tf_op jit(solution)/shard_map/ppermute | solution.py:697
  360.2 12.7 %collective-permute-start.11 = (bf16[48,1280]{1,0:T(8,128)(2,1)S(1)}, bf16[48,1280]{1,0:T(8,128)(2,1)S(1)}, u32[]{:S(2)}, u32[]{:S(2)}) collective-permute-start(bf16[48,1280]{1,0:T(8,128)(2,1)S(1)} %dynamic-slice_convert_fusion.3), channel_id=1, source_target_pairs={{0,1},{1,0},{2,3},{3,2},{4,5},{5,4},{6,7},{7,6},{8,9},{9,8},{10,11... | collective-permute-start | bytes 368648 | tf_op jit(solution)/shard_map/ppermute | solution.py:697
  360.4 12.8 %collective-permute-start.4 = (bf16[24,1920]{1,0:T(8,128)(2,1)S(1)}, bf16[24,1920]{1,0:T(8,128)(2,1)S(1)}, u32[]{:S(2)}, u32[]{:S(2)}) collective-permute-start(bf16[24,1920]{1,0:T(8,128)(2,1)S(1)} %dynamic-slice_convert_fusion.4), channel_id=1, source_target_pairs={{0,2},{1,3},{2,0},{3,1},{4,6},{5,7},{6,4},{7,5},{8,10},{9,11},{10,... | collective-permute-start | bytes 276488 | tf_op jit(solution)/shard_map/ppermute | solution.py:697
  373.0 8.3 %collective-permute-start.12 = (bf16[24,1280]{1,0:T(8,128)(2,1)S(1)}, bf16[24,1280]{1,0:T(8,128)(2,1)S(1)}, u32[]{:S(2)}, u32[]{:S(2)}) collective-permute-start(bf16[24,1280]{1,0:T(8,128)(2,1)S(1)} %dynamic-slice_convert_fusion.5), channel_id=1, source_target_pairs={{0,2},{1,3},{2,0},{3,1},{4,6},{5,7},{6,4},{7,5},{8,10},{9,11},{10,... | collective-permute-start | bytes 184328 | tf_op jit(solution)/shard_map/ppermute | solution.py:697
  373.1 10.8 %collective-permute-start.5 = (bf16[24,1920]{1,0:T(8,128)(2,1)S(1)}, bf16[24,1920]{1,0:T(8,128)(2,1)S(1)}, u32[]{:S(2)}, u32[]{:S(2)}) collective-permute-start(bf16[24,1920]{1,0:T(8,128)(2,1)S(1)} %add_convert_fusion.3), channel_id=1, source_target_pairs={{0,2},{1,3},{2,0},{3,1},{4,6},{5,7},{6,4},{7,5},{8,10},{9,11},{10,... | collective-permute-start | bytes 276488 | tf_op jit(solution)/shard_map/ppermute | solution.py:708
  381.3 5.3 %collective-permute-start.13 = (bf16[24,1280]{1,0:T(8,128)(2,1)S(1)}, bf16[24,1280]{1,0:T(8,128)(2,1)S(1)}, u32[]{:S(2)}, u32[]{:S(2)}) collective-permute-start(bf16[24,1280]{1,0:T(8,128)(2,1)S(1)} %add_convert_fusion.4), channel_id=1, source_target_pairs={{0,2},{1,3},{2,0},{3,1},{4,6},{5,7},{6,4},{7,5},{8,10},{9,11},{10,... | collective-permute-start | bytes 184328 | tf_op jit(solution)/shard_map/ppermute | solution.py:708
  384.0 7.6 %collective-permute-start.6 = (bf16[48,1920]{1,0:T(8,128)(2,1)S(1)}, bf16[48,1920]{1,0:T(8,128)(2,1)S(1)}, u32[]{:S(2)}, u32[]{:S(2)}) collective-permute-start(bf16[48,1920]{1,0:T(8,128)(2,1)S(1)} %maximum_select_fusion.7), channel_id=1, source_target_pairs={{0,1},{1,0},{2,3},{3,2},{4,5},{5,4},{6,7},{7,6},{8,9},{9,8},{10,11... | collective-permute-start | bytes 552968 | tf_op jit(solution)/shard_map/ppermute | solution.py:708
  386.7 6.2 %collective-permute-start.14 = (bf16[48,1280]{1,0:T(8,128)(2,1)S(1)}, bf16[48,1280]{1,0:T(8,128)(2,1)S(1)}, u32[]{:S(2)}, u32[]{:S(2)}) collective-permute-start(bf16[48,1280]{1,0:T(8,128)(2,1)S(1)} %maximum_select_fusion.8), channel_id=1, source_target_pairs={{0,1},{1,0},{2,3},{3,2},{4,5},{5,4},{6,7},{7,6},{8,9},{9,8},{10,11... | collective-permute-start | bytes 368648 | tf_op jit(solution)/shard_map/ppermute | solution.py:708
  391.7 7.1 %collective-permute-start.7 = (bf16[96,1664]{1,0:T(8,128)(2,1)S(1)}, bf16[96,1664]{1,0:T(8,128)(2,1)S(1)}, u32[]{:S(2)}, u32[]{:S(2)}) collective-permute-start(bf16[96,1664]{1,0:T(8,128)(2,1)S(1)} %slice.35), channel_id=1, source_target_pairs={{0,16},{4,20},{8,24},{12,28},{16,0},{20,4},{24,8},{28,12},{1,17},{... | collective-permute-start | bytes 958472 | tf_op jit(solution)/shard_map/ppermute | solution.py:720
  393.0 7.7 %collective-permute-start.15 = (bf16[96,1536]{1,0:T(8,128)(2,1)S(1)}, bf16[96,1536]{1,0:T(8,128)(2,1)S(1)}, u32[]{:S(2)}, u32[]{:S(2)}) collective-permute-start(bf16[96,1536]{1,0:T(8,128)(2,1)S(1)} %get-tuple-element.173), channel_id=1, source_target_pairs={{0,8},{4,12},{8,0},{12,4},{16,24},{20,28},{24,16},{28,20},{1,9},{5... | collective-permute-start | bytes 884744 | tf_op jit(solution)/shard_map/ppermute | solution.py:721
  400.8 14.2 %collective-permute-start.16 = (bf16[192,1664]{1,0:T(8,128)(2,1)S(1)}, bf16[192,1664]{1,0:T(8,128)(2,1)S(1)}, u32[]{:S(2)}, u32[]{:S(2)}) collective-permute-start(bf16[192,1664]{1,0:T(8,128)(2,1)S(1)} %maximum_select_fusion.2), channel_id=1, source_target_pairs={{0,8},{4,12},{8,0},{12,4},{16,24},{20,28},{24,16},{28,20},{1,9},{5... | collective-permute-start | bytes 1916936 | tf_op jit(solution)/shard_map/ppermute | solution.py:720
  401.4 12.7 %collective-permute-start.17 = (bf16[2,96,1536]{2,1,0:T(8,128)(2,1)S(1)}, bf16[2,96,1536]{2,1,0:T(8,128)(2,1)S(1)}, u32[]{:S(2)}, u32[]{:S(2)}) collective-permute-start(bf16[2,96,1536]{2,1,0:T(8,128)(2,1)S(1)} %maximum_select_fusion.3), channel_id=1, source_target_pairs={{0,16},{4,20},{8,24},{12,28},{16,0},{20,4},{24,8},{28,12},{1,17},{... | collective-permute-start | bytes 1769480 | tf_op jit(solution)/shard_map/ppermute | solution.py:721
  415.4 4.7 %collective-permute-start.18 = (bf16[384,1664]{1,0:T(8,128)(2,1)S(1)}, bf16[384,1664]{1,0:T(8,128)(2,1)S(1)}, u32[]{:S(2)}, u32[]{:S(2)}) collective-permute-start(bf16[384,1664]{1,0:T(8,128)(2,1)S(1)} %maximum_select_fusion.one_ref), channel_id=1, source_target_pairs={{0,4},{4,0},{8,12},{12,8},{16,20},{20,16},{24,28},{28,24},{1,5},{5... | collective-permute-start | bytes 3833864 | tf_op jit(solution)/shard_map/ppermute | solution.py:845
  415.6 4.5 %collective-permute-start.19 = (bf16[384,1536]{1,0:T(8,128)(2,1)S(1)}, bf16[384,1536]{1,0:T(8,128)(2,1)S(1)}, u32[]{:S(2)}, u32[]{:S(2)}) collective-permute-start(bf16[384,1536]{1,0:T(8,128)(2,1)S(1)} %bitcast.95), channel_id=1, source_target_pairs={{0,4},{4,0},{8,12},{12,8},{16,20},{20,16},{24,28},{28,24},{1,5},{5... | collective-permute-start | bytes 3538952 | tf_op jit(solution)/shard_map/ppermute | solution.py:845
  (3 other events, 2.3 us)
Sparse Core Ops, SparseCore 0:
  11.8 118.0 all-gather.3
  132.0 61.7 all-gather.5
  196.1 109.3 reduce-scatter.2
  307.7 69.1 reduce-scatter.4

commit v3 on v2

--- a/solution.py
+++ b/solution.py
@@ -382,9 +382,9 @@
     cent_grad_ref[...] += jnp.sum(chosen * x.astype(F32), 0, keepdims=True)
 
 
-def expert_weights_kernel(xt_ref, gt_ref, active_ref, pre_ref, dw_ref):
-    dw_ref[0, 0] = dot(xt_ref[...], pre_ref[...]).astype(BF16)
-    dw_ref[0, 1] = dot(gt_ref[...], active_ref[...]).astype(BF16)
+def expert_weights_kernel(xt_ref, gt_ref, active_ref, pre_ref, hidden_ref, down_ref):
+    hidden_ref[0] = dot(xt_ref[...], pre_ref[...]).astype(BF16)
+    down_ref[0] = dot(gt_ref[...], active_ref[...]).astype(BF16)
 
 
 def whole(shape):
@@ -467,13 +467,14 @@
     width, rows = xt.shape
     hidden = active.shape[1] // pieces
     kept_spec = pl.BlockSpec((rows, hidden), lambda i: (0, i))
-    shape = (pieces, 2, width, hidden)
+    shape = (pieces, width, hidden)
+    piece = pl.BlockSpec((1, width, hidden), lambda i: (i, 0, 0))
     return pl.pallas_call(
         expert_weights_kernel,
         grid=(pieces,),
         in_specs=[whole(xt.shape), whole(xt.shape), kept_spec, kept_spec],
-        out_specs=pl.BlockSpec((1, *shape[1:]), lambda i: (i, 0, 0, 0)),
-        out_shape=jax.ShapeDtypeStruct(shape, BF16),
+        out_specs=[piece, piece],
+        out_shape=[jax.ShapeDtypeStruct(shape, BF16)] * 2,
         compiler_params=EXPERT_PARAMS,
         cost_estimate=expert_cost(2, rows, width, hidden, pieces),
         name="expert_weights",
@@ -569,35 +570,38 @@
     )(rows, target, gate, resid)
 
 
-def finish_experts_kernel(blocks, first_ref, second_ref, hidden_ref, down_ref):
+def finish_experts_kernel(blocks, turned, first_ref, second_ref, out_ref):
     step = pl.program_id(0)
-    for source, here in ((first_ref, step < blocks), (second_ref, step >= blocks)):
-
-        @pl.when(here)
-        def _():
-            hidden_ref[0] = source[0, 0].astype(F32)
-            down_ref[0] = source[0, 1].T.astype(F32)
-
-
-def finish_experts(first, second):
-    unused, two, width, size = second.shape
+
+    def put(rows):
+        out_ref[0] = (rows.T if turned else rows).astype(F32)
+
+    @pl.when(step < blocks)
+    def _():
+        put(first_ref[0, 0])
+
+    @pl.when(step >= blocks)
+    def _():
+        put(second_ref[0])
+
+
+def finish_experts(first, second, index):
+    unused, width, size = second.shape
     blocks = first.shape[3] // size
     hidden = first.shape[3] + size
+    turned = index == 1
+    block, shape = (1, width, size), (1, width, hidden)
+    if turned:
+        block, shape = (1, size, width), (1, hidden, width)
     return pl.pallas_call(
-        functools.partial(finish_experts_kernel, blocks),
+        functools.partial(finish_experts_kernel, blocks, turned),
         grid=(blocks + 1,),
         in_specs=[
-            pl.BlockSpec((1, 2, width, size), lambda i: (0, 0, 0, jnp.minimum(i, blocks - 1))),
+            pl.BlockSpec((1, 1, width, size), lambda i: (0, index, 0, jnp.minimum(i, blocks - 1))),
             whole(second.shape),
         ],
-        out_specs=[
-            pl.BlockSpec((1, width, size), lambda i: (0, 0, i)),
-            pl.BlockSpec((1, size, width), lambda i: (0, i, 0)),
-        ],
-        out_shape=[
-            jax.ShapeDtypeStruct((1, width, hidden), F32),
-            jax.ShapeDtypeStruct((1, hidden, width), F32),
-        ],
+        out_specs=pl.BlockSpec(block, lambda i: (0, i, 0) if turned else (0, 0, i)),
+        out_shape=jax.ShapeDtypeStruct(shape, F32),
         compiler_params=EXPERT_PARAMS,
         name="finish_experts",
     )(first, second)
@@ -824,15 +828,15 @@
             rows, grad_rows, upstream_rows, row_gate, own_centroid, out_sum, in_sum, weights[1]
         )
         back = exchange(back_rows, experts_all)
-        more_weight_grads = expert_weights(rows_t, grad_rows_t, *kept, n_narrow)
+        more_hidden, more_down = expert_weights(rows_t, grad_rows_t, *kept, n_narrow)
         own_row = lax.broadcasted_iota(jnp.int32, (experts_all + 4 + -(experts_all + 4) % 8, 1), 0)
         sums = jnp.where(own_row == wide_here, own_centroid_grad, 0.0)
         sums, back = lax.optimization_barrier((sums, back))
         grad_resid, grad_attn, grad_mixed, second_sums = combine_back(
             back, target, resid, cot, second_gain, output_weight
         )
-        out_low, more_weight_grads, grad_mixed = lax.optimization_barrier(
-            (out_low, more_weight_grads, grad_mixed)
+        out_low, more_hidden, more_down, grad_mixed = lax.optimization_barrier(
+            (out_low, more_hidden, more_down, grad_mixed)
         )
         returned = exchange(out_low, experts_all)
 
@@ -850,11 +854,10 @@
         )
         came_one = swap(theirs_one)
         mine_two, theirs_two, grads_two = attend_back(*shared, counts, 1, normed_t)
-        block_out = combine_out(returned, target, gate, resid)
-        grads_two, block_out, came_one, more_weight_grads = lax.optimization_barrier(
-            (grads_two, block_out, came_one, more_weight_grads)
-        )
-        last_summed = lax.psum_scatter(more_weight_grads, "narrow", scatter_dimension=0, tiled=True)
+        grads_two, returned, came_one, more_hidden = lax.optimization_barrier(
+            (grads_two, returned, came_one, more_hidden)
+        )
+        hidden_summed = lax.psum_scatter(more_hidden, "narrow", scatter_dimension=0, tiled=True)
         mine_two, theirs_two, input_grad = attend_back(
             *shared, counts, 2, normed_t, grads_one, grads_two, query_weight, key_weight, value_weight, block_in,
             first_gain.reshape(1, width), grad_resid, sums, second_sums, mine_two, theirs_two,
@@ -865,20 +868,33 @@
         chain_two = [mine_two, swap(theirs_two)]
         chain_one = reduce_halves([chain_one], flags[0], sizes, plane[1:] + line)
         chain_two = reduce_halves(chain_two, flags[1], sizes, plane[:1])
-        chain_two, last_summed = reduce_halves(
-            [chain_two], flags[1], sizes, plane[1:] + line, (last_summed,)
-        )
+        chain_two, hidden_summed = reduce_halves(
+            [chain_two], flags[1], sizes, plane[1:], (hidden_summed,)
+        )
+        chain_two = reduce_halves([chain_two], flags[1], sizes, line)
         near = [
-            gather_halves(total.astype(BF16), kept[len(wide_bits) :], sizes, line)
-            for total, kept in zip((chain_one, chain_two), flags)
+            gather_halves(total.astype(BF16), kept[-len(line) :], sizes, line)
+            for total, kept in ((chain_one, flags[0]),)
         ]
+        kept = flags[1][-len(line) :]
+        far = gather_halves(chain_two.astype(BF16), kept[1:], sizes, line[1:])
+        far, more_down = lax.optimization_barrier((far, more_down))
+        down_summed = lax.psum_scatter(more_down, "narrow", scatter_dimension=0, tiled=True)
+        near.append(gather_halves(far, kept[:1], sizes, line[:1]))
         inner = [kept[1 : len(wide_bits)] for kept in flags]
         moved = pairs // 3
         near_cols = near[0].shape[1] - moved * PAIR
         near = [near[0][:, :near_cols], jnp.concatenate([near[1], near[0][:, near_cols:]], 1)]
-        *near, (hidden_grad, down_grad) = gather_plane(
-            *near, inner[0], sizes, plane, finish_experts, (first_summed, last_summed)
-        )
+        def finish(first_summed, hidden_summed, returned):
+            return (
+                finish_experts(first_summed, hidden_summed, 0),
+                combine_out(returned, target, gate, resid),
+            )
+
+        *near, (hidden_grad, block_out) = gather_plane(
+            *near, inner[0], sizes, plane, finish, (first_summed, hidden_summed, returned)
+        )
+        down_grad = finish_experts(first_summed, down_summed, 1)
         halves = [(half, swap(half)) for half in near]
         query_grad, key_grad, value_grad, output_weight_grad, centroids_grad, *vectors = spread(
             flag.reshape(1), halves, width, counts[0], moved, experts_all

time: 435 us -> 420 us (0.966)
  local copies, waits for them, and re-layouts: 27.8 us -> 14.2 us
  waiting for transfers between devices: 143 us -> 133 us
  starting transfers between devices: 32 us -> 36.6 us
    ppermute x8, waiting for transfers between devices: 37.2 us -> 23.1 us  [reduce_halves(): lax.ppermute(add_up(theirs).astype(BF16), axis, xor_pairs(sizes[axis], fl...]
    optimization_barrier x1, local copies, waits for them, and re-layouts: 12.7 us -> 1.65 us  [shards(): mixed, upstream_rows = lax.optimization_barrier((mixed, upstream_rows))]
    all_gather x2, waiting for transfers between devices: 31.5 us -> 41.6 us  [shards(): lax.all_gather(pack, 'narrow', axis=0, tiled=True)]
    ppermute x2, waiting for transfers between devices: 9.11 us -> 2.75 us  [gather_plane(): lax.ppermute(two, axis, xor_pairs(sizes[axis], flip))]
    reduce_scatter x1 -> x2, waiting for transfers between devices: 0.78 us -> 5.37 us  [the longest x1 2.72 us: shards(): lax.psum_scatter(more_hidden, 'narrow', scatter_dimension=0, tiled=True)]
  transfers between devices with their start and end apart: 28 -> 29, of which waited for: 19 -> 17; matrix products, arithmetic and copies ran while one was open for 13% -> 11% of each run, Pallas kernels for 40% -> 42%
where the time goes in v3:
time: 420 us; the launch traced here: 416 us
  Pallas kernels  176 us (42%)
  waiting for transfers between devices  133 us (32%)
  starting transfers between devices  36.6 us (9%)
  other arithmetic  20.3 us (5%)
  matrix products  20 us (5%)
  between operations  15.4 us (4%)
  local copies, waits for them, and re-layouts  14.2 us (3%)
    pallas_call x3, Pallas kernels, attend_back(): pl.pallas_call(functools.partial(attend_back_kernel, scale, counts, part)...  52.3 us
    pallas_call x1, Pallas kernels, expert_first(): pl.pallas_call(functools.partial(expert_first_kernel, tiles), grid=(tiles...  44.6 us
    all_to_all x4, waiting for transfers between devices, exchange(): lax.all_to_all(rows.reshape(blocks, -1, shape[1]), 'wide', split_axis=0,...  44.5 us
    all_gather x2, waiting for transfers between devices, shards(): lax.all_gather(pack, 'narrow', axis=0, tiled=True)  41.6 us
    ppermute x8, waiting for transfers between devices, reduce_halves(): lax.ppermute(add_up(theirs).astype(BF16), axis, xor_pairs(sizes[axis], fl...  23.1 us
    pallas_call x1, Pallas kernels, attend(): pl.pallas_call(functools.partial(attend_kernel, scale), grid_spec=pltpu.P...  22.2 us
    pallas_call x1, Pallas kernels, expert_last(): pl.pallas_call(expert_last_kernel, grid=(rows // tile,), in_specs=[tiled(...  19.4 us
    all_to_all x4, starting transfers between devices, exchange(): lax.all_to_all(rows.reshape(blocks, -1, shape[1]), 'wide', split_axis=0,...  19 us
  transfers between devices with their start and end apart: 29, of which 17 were waited for; matrix products, arithmetic and copies ran while one was open for 11% of the time, Pallas kernels for 42%

profile of v3, /device:TPU:0, one launch (start us, length us, event | category | flops | bytes accessed | tf_op | source)
XLA Modules:
  0.0 416.1 jit_solution(14718260541081859929)
XLA Ops:
  12.1 2.3 reduce-window.6
  14.9 4.7 %fusion.11 = bf16[1536,768]{1,0:T(8,128)(2,1)} fusion(s32[1024]{0:T(1024)S(1)} %add_select_fusion.1, bf16[1,1024,768]{2,1,0:T(8,128)(2,1)S(1)} %copy-done.19), kind=kOutput, calls=%fused_computation.15 | convolution fusion | flops 2418671616 | bytes 3936256 | tf_op jit(solution)/shard_map/dot_general | solution.py:23
  19.6 5.7 %all-to-all-start = ((bf16[8,192,768]{2,1,0:T(8,128)(2,1)}), bf16[8,192,768]{2,1,0:T(8,128)(2,1)}, u32[]{:S(2)}, u32[]{:S(2)}) async-start(bf16[8,192,768]{2,1,0:T(8,128)(2,1)} %bitcast.11), calls=%async_computation | async-start | bytes 4718592 | tf_op jit(solution)/shard_map/all_to_all | solution.py:685
  30.0 7.2 %convolution_convert_fusion.q_ref.k_ref.v_ref = bf16[1024,2304]{1,0:T(8,128)(2,1)} fusion(bf16[768,768]{1,0:T(8,128)(2,1)S(1)} %copy-done.8, bf16[768,768]{1,0:T(8,128)(2,1)S(1)} %copy-done.9, bf16[768,768]{1,0:T(8,128)(2,1)S(1)} %copy-done.10, bf16[1,1024,768]{2,1,0:T(8,128)(2,1)S(1)} %copy-done, f32[768]{0:T(1024)S(1)} %copy-done.16, ...), kind=kOutput, calls=%fused_computation.3 | convolution fusion | flops 3641573376 | bytes 9844736 | tf_op jit(solution)/shard_map/dot_general | solution.py:19
  37.2 22.2 %attend.1 = (bf16[1024,768]{1,0:T(8,128)(2,1)S(1)}, bf16[6,2,2560,256]{3,2,1,0:T(8,128)(2,1)}) custom-call(s32[1]{0:T(128)} %copy.59.len_ref, bf16[1024,2304]{1,0:T(8,128)(2,1)} %convolution_convert_fusion.q_ref.k_ref.v_ref, bf16[1024,2304]{1,0:T(8,128)(2,1)} %convolution_convert_fusion.q_ref.k_ref.v_ref, ...), custom_call_target="tpu_custom_call" | custom-call | flops 3221225472 | bytes 6291456 | tf_op jit(solution)/shard_map/attend/pallas_call | solution.py:75
  59.4 1.8 fusion.32
  61.2 1.7 copy.47
  62.8 2.8 fusion.34
  68.5 4.8 %fusion.12 = bf16[1536,768]{1,0:T(8,128)(2,1)} fusion(bf16[1024,768]{1,0:T(8,128)(2,1)S(1)} %add_convert_fusion, s32[1024]{0:T(1024)S(1)} %add_select_fusion.1), kind=kOutput, calls=%fused_computation.16 | convolution fusion | flops 2418671616 | bytes 3936256 | tf_op jit(solution)/shard_map/dot_general | solution.py:23
  73.3 4.4 %all-to-all-start.1 = ((bf16[8,192,768]{2,1,0:T(8,128)(2,1)}), bf16[8,192,768]{2,1,0:T(8,128)(2,1)S(1)}, u32[]{:S(2)}, u32[]{:S(2)}) async-start(bf16[8,192,768]{2,1,0:T(8,128)(2,1)} %bitcast.103), calls=%async_computation.1 | async-start | bytes 4718592 | tf_op jit(solution)/shard_map/all_to_all | solution.py:685
  79.4 27.8 %all-to-all-done.1 = bf16[8,192,768]{2,1,0:T(8,128)(2,1)S(1)} async-done(((bf16[8,192,768]{2,1,0:T(8,128)(2,1)}), bf16[8,192,768]{2,1,0:T(8,128)(2,1)S(1)}, u32[]{:S(2)}, u32[]{:S(2)}) %all-to-all-start.1) | async-done | bytes 2359328 | tf_op jit(solution)/shard_map/all_to_all | solution.py:685
  107.2 22.3 %all-gather.4.cloned.1.call-done.w_ref = bf16[4,2,512,768]{3,2,1,0:T(8,128)(2,1)} async-done(((bf16[1,2,512,768]{3,2,1,0:T(8,128)(2,1)}), bf16[4,2,512,768]{3,2,1,0:T(8,128)(2,1)}) %all-gather.4.cloned.1.call-update) | async-done | bytes 6291472 | tf_op jit(solution)/shard_map/all_gather | solution.py:783
  129.5 44.6 %expert_first.1 = (f32[1536,768]{1,0:T(8,128)}, f32[1536,768]{1,0:T(8,128)}, bf16[4,2,768,512]{3,2,1,0:T(8,128)(2,1)}, bf16[1536,768]{1,0:T(8,128)(2,1)}, bf16[7...) custom-call(bf16[1536,768]{1,0:T(8,128)(2,1)} %bitcast.100, bf16[1536,768]{1,0:T(8,128)(2,1)} %bitcast.12.u_ref, ...), custom_call_target="tpu_custom_call" | custom-call | flops 28991029248 | bytes 28311552 | tf_op jit(solution)/shard_map/expert_first/pallas_call | solution.py:417
  174.1 19.3 %all-gather.6.cloned.1.call-done = bf16[8,256,768]{2,1,0:T(8,128)(2,1)} async-done(((bf16[2,256,768]{2,1,0:T(8,128)(2,1)}), bf16[8,256,768]{2,1,0:T(8,128)(2,1)}) %all-gather.6.cloned.1.call-update) | async-done | bytes 3145744 | tf_op jit(solution)/shard_map/all_gather | solution.py:783
  193.4 19.4 %expert_last.1 = (bf16[1536,768]{1,0:T(8,128)(2,1)}, bf16[1536,768]{1,0:T(8,128)(2,1)}, f32[1,768]{1,0:T(1,128)}, bf16[1536,1024]{1,0:T(8,128)(2,1)}, bf16[1536,1024]{1,0:T(8,128)(2,1)}) custom-call(bf16[1536,768]{1,0:T(8,128)(2,1)} %bitcast.101, bf16[1536,768]{1,0:T(8,128)(2,1)} %get-tuple-element.107.g_ref, bf16[1536,768]{1,0:T(8,128)(2,1)} %bitcast.12.u_ref, ...), custom_call_target="tpu_custom_call" | custom-call | flops 9663676416 | bytes 28311552 | tf_op jit(solution)/shard_map/expert_last/pallas_call | solution.py:452
  212.8 4.5 %all-to-all-start.2 = ((bf16[8,192,768]{2,1,0:T(8,128)(2,1)}), bf16[8,192,768]{2,1,0:T(8,128)(2,1)}, u32[]{:S(2)}, u32[]{:S(2)}) async-start(bf16[8,192,768]{2,1,0:T(8,128)(2,1)} %bitcast.102), calls=%async_computation.2 | async-start | bytes 4718592 | tf_op jit(solution)/shard_map/all_to_all | solution.py:685
  217.9 1.7 copy.50.normed_t
  220.3 9.8 %expert_weights.1 = (bf16[4,768,256]{2,1,0:T(8,128)(2,1)}, bf16[4,768,256]{2,1,0:T(8,128)(2,1)}) custom-call(bf16[768,1536]{1,0:T(8,128)(2,1)} %get-tuple-element.112.xt_ref, bf16[768,1536]{1,0:T(8,128)(2,1)} %get-tuple-element.113.gt_ref, bf16[1536,1024]{1,0:T(8,128)(2,1)} %get-tuple-element.114.active_ref, bf16[1536,1024]{1,0:T(8,128)(2,1)} %get-tuple-element.115.pre_ref), custom_call_target="tpu_custom_call" | custom-call | flops 4831838208 | bytes 28311552 | tf_op jit(solution)/shard_map/expert_weights/pallas_call | solution.py:472
  230.1 16.7 %all-to-all-done.2 = bf16[8,192,768]{2,1,0:T(8,128)(2,1)} async-done(((bf16[8,192,768]{2,1,0:T(8,128)(2,1)}), bf16[8,192,768]{2,1,0:T(8,128)(2,1)}, u32[]{:S(2)}, u32[]{:S(2)}) %all-to-all-start.2) | async-done | bytes 2359328 | tf_op jit(solution)/shard_map/all_to_all | solution.py:685
  246.8 10.3 %combine_back.1 = (f32[1024,768]{1,0:T(8,128)}, bf16[1024,768]{1,0:T(8,128)(2,1)}, bf16[1024,768]{1,0:T(8,128)(2,1)}, f32[8,768]{1,0:T(8,128)}) custom-call(bf16[1536,768]{1,0:T(8,128)(2,1)} %bitcast.25.back_ref, s32[1024,1]{1,0:T(8,128)} %add_select_fusion.target_ref, f32[1024,768]{1,0:T(8,128)} %copy-done.1, bf16[1024,768]{1,0:T(8,128)(2,1)} %bitcast.115, ...), custom_call_target="tpu_custom_call" | custom-call | flops 3623878656 | bytes 15728640 | tf_op jit(solution)/shard_map/combine_back/pallas_call | solution.py:524
  257.1 4.4 %all-to-all-start.3 = ((bf16[8,192,768]{2,1,0:T(8,128)(2,1)}), bf16[8,192,768]{2,1,0:T(8,128)(2,1)}, u32[]{:S(2)}, u32[]{:S(2)}) async-start(bf16[8,192,768]{2,1,0:T(8,128)(2,1)} %bitcast.26), calls=%async_computation.3 | async-start | bytes 4718592 | tf_op jit(solution)/shard_map/all_to_all | solution.py:685
  261.7 21.2 %attend_back.3 = (f32[384,1920]{1,0:T(8,128)}, bf16[384,1920]{1,0:T(8,128)(2,1)}, bf16[3,1024,384]{2,1,0:T(8,128)(2,1)}) custom-call(s32[1]{0:T(128)} %bitcast.flag_ref, bf16[1024,2304]{1,0:T(8,128)(2,1)} %convolution_convert_fusion.q_ref.k_ref.v_ref, bf16[1024,2304]{1,0:T(8,128)(2,1)} %convolution_convert_fusion.q_ref.k_ref.v_ref, ...), custom_call_target="tpu_custom_call" | custom-call | flops 8053063680 | bytes 5505024 | tf_op jit(solution)/shard_map/attend_back/pallas_call | solution.py:277
  283.3 13.4 %attend_back.4 = (f32[384,1280]{1,0:T(8,128)}, bf16[384,1280]{1,0:T(8,128)(2,1)}, bf16[3,1024,256]{2,1,0:T(8,128)(2,1)}) custom-call(s32[1]{0:T(128)} %bitcast.flag_ref, bf16[1024,2304]{1,0:T(8,128)(2,1)} %convolution_convert_fusion.q_ref.k_ref.v_ref, bf16[1024,2304]{1,0:T(8,128)(2,1)} %convolution_convert_fusion.q_ref.k_ref.v_ref, ...), custom_call_target="tpu_custom_call" | custom-call | flops 5368709120 | bytes 3670016 | tf_op jit(solution)/shard_map/attend_back/pallas_call | solution.py:277
  296.7 2.1 add_convert_fusion.1
  298.9 1.7 collective-permute-start.1
  301.4 17.6 %attend_back.5 = (f32[384,1280]{1,0:T(8,128)}, bf16[384,1280]{1,0:T(8,128)(2,1)}, bf16[1,1024,768]{2,1,0:T(8,128)(2,1)}) custom-call(s32[1]{0:T(128)} %bitcast.flag_ref, bf16[1024,2304]{1,0:T(8,128)(2,1)} %convolution_convert_fusion.q_ref.k_ref.v_ref, ...), custom_call_target="tpu_custom_call", output_to_operand_aliasing={{0}: (17, {}), {1}: (18, {})} | custom-call | flops 2684354560 | bytes 1835008 | tf_op jit(solution)/shard_map/attend_back/pallas_call | solution.py:277
  320.0 2.1 convert_add_fusion
  326.0 7.8 %collective-permute-done.2 = bf16[96,1920]{1,0:T(8,128)(2,1)} collective-permute-done((bf16[96,1920]{1,0:T(8,128)(2,1)}, bf16[96,1920]{1,0:T(8,128)(2,1)}, u32[]{:S(2)}, u32[]{:S(2)}) %collective-permute-start.2) | collective-permute-done | bytes 368672 | tf_op jit(solution)/shard_map/ppermute | solution.py:701
  334.9 3.5 collective-permute-done.9
  340.3 3.9 collective-permute-done.3
  344.3 2.7 reduce-scatter.6.cloned.1.call-done.second_ref
  347.2 1.6 collective-permute-start.4
  348.8 5.0 %collective-permute-done.11 = bf16[48,1280]{1,0:T(8,128)(2,1)S(1)} collective-permute-done((bf16[48,1280]{1,0:T(8,128)(2,1)S(1)}, bf16[48,1280]{1,0:T(8,128)(2,1)S(1)}, u32[]{:S(2)}, u32[]{:S(2)}) %collective-permute-start.11) | collective-permute-done | bytes 122912 | tf_op jit(solution)/shard_map/ppermute | solution.py:701
  355.0 1.9 collective-permute-start.5
  356.9 2.9 collective-permute-done.12
  360.2 3.0 collective-permute-done.5
  363.3 1.7 collective-permute-done.13
  365.4 3.6 collective-permute-done.6
  370.8 1.8 collective-permute-start.15
  372.6 3.6 collective-permute-done.7
  376.2 2.7 collective-permute-done.15
  379.1 1.9 collective-permute-start.16
  383.6 3.0 finish_experts.2
  386.6 7.1 %combine_out.1 = bf16[1,1024,768]{2,1,0:T(8,128)(2,1)} custom-call(bf16[1536,768]{1,0:T(8,128)(2,1)} %bitcast.27.rows_ref, s32[1024,1]{1,0:T(8,128)} %add_select_fusion.target_ref, f32[1024,1]{1,0:T(8,128)} %copy.53.gate_ref, f32[1024,768]{1,0:T(8,128)} %copy-done.1), custom_call_target="tpu_custom_call" | custom-call | flops 2415919104 | bytes 6291456 | tf_op jit(solution)/shard_map/combine_out/pallas_call | solution.py:555
  395.1 3.9 collective-permute-done.19.two_other
  399.0 4.5 %spread.1 = (f32[768,768]{1,0:T(8,128)}, f32[768,768]{1,0:T(8,128)}, f32[768,768]{1,0:T(8,128)}, f32[768,768]{1,0:T(8,128)}, f32[8,768]{1,0:T(8,128)}, /*index=5...) custom-call(s32[1]{0:T(128)} %bitcast.flag_ref, bf16[384,1664]{1,0:T(8,128)(2,1)S(1)} %maximum_select_fusion.one_ref, ...), custom_call_target="tpu_custom_call" | custom-call | tf_op jit(solution)/shard_map/spread/pallas_call | solution.py:658
  403.5 2.6 reduce-scatter.8.cloned.1.call-done.second_ref
  406.2 3.2 finish_experts.3
  (141 shorter events, 32.3 us)
Async XLA Ops:
  7.2 122.3 %all-gather.4.cloned.1.call-start = ((), (), s32[]{:S(2)}) async-start(), calls=%async_computation.7 | async-start | bytes 7864320 | tf_op jit(solution)/shard_map/all_gather | solution.py:783
  8.8 1.1 slice-start
  11.2 3.7 copy-start.19
  19.6 41.6 %all-to-all-start = ((bf16[8,192,768]{2,1,0:T(8,128)(2,1)}), bf16[8,192,768]{2,1,0:T(8,128)(2,1)}, u32[]{:S(2)}, u32[]{:S(2)}) async-start(bf16[8,192,768]{2,1,0:T(8,128)(2,1)} %bitcast.11), calls=%async_computation | async-start | bytes 4718592 | tf_op jit(solution)/shard_map/all_to_all | solution.py:685
  25.3 2.1 copy-start
  27.4 2.4 copy-start.10
  27.7 1.1 copy-start.6
  27.7 1.3 copy-start.7
  28.3 1.5 copy-start.8
  28.3 1.7 copy-start.9
  28.3 1.7 copy-start.15
  28.3 1.7 copy-start.16
  65.6 1.6 copy-start.1
  65.7 1.6 copy-start.14
  65.7 1.6 copy-start.17
  73.3 4.5 %slice-start.1 = ((bf16[1,768,768]{2,1,0:T(8,128)(2,1)}), bf16[1,256,768]{2,1,0:T(8,128)(2,1)S(1)}, s32[]{:S(2)}) async-start(bf16[1,768,768]{2,1,0:T(8,128)(2,1)} %param.28), calls=%async_computation.13 | async-start | bytes 786432 | tf_op jit(solution)/shard_map/slice | solution.py:777
  73.3 33.9 %all-to-all-start.1 = ((bf16[8,192,768]{2,1,0:T(8,128)(2,1)}), bf16[8,192,768]{2,1,0:T(8,128)(2,1)S(1)}, u32[]{:S(2)}, u32[]{:S(2)}) async-start(bf16[8,192,768]{2,1,0:T(8,128)(2,1)} %bitcast.103), calls=%async_computation.1 | async-start | bytes 4718592 | tf_op jit(solution)/shard_map/all_to_all | solution.py:685
  77.7 115.7 %all-gather.6.cloned.1.call-start = ((), (), s32[]{:S(2)}) async-start(), calls=%async_computation.11 | async-start | bytes 3932160 | tf_op jit(solution)/shard_map/all_gather | solution.py:783
  78.8 240.4 %reduce-scatter.4.cloned.1.call-start = ((), (), s32[]{:S(2)}) async-start(), calls=%async_computation.8 | async-start | bytes 7864320 | tf_op jit(solution)/shard_map/reduce_scatter | solution.py:851
  107.2 22.3 %copy-start.5 = (bf16[8,192,768]{2,1,0:T(8,128)(2,1)}, bf16[8,192,768]{2,1,0:T(8,128)(2,1)S(1)}, u32[]{:S(2)}) copy-start(bf16[8,192,768]{2,1,0:T(8,128)(2,1)S(1)} %all-to-all-done.1) | copy-start | bytes 7077892
  212.8 5.1 %copy-start.3 = (bf16[768,1024]{0,1:T(8,128)(2,1)S(1)}, bf16[768,1024]{0,1:T(8,128)(2,1)}, u32[]{:S(2)}) copy-start(bf16[768,1024]{0,1:T(8,128)(2,1)} %fusion.32) | copy-start | bytes 4718596
  212.8 34.0 %all-to-all-start.2 = ((bf16[8,192,768]{2,1,0:T(8,128)(2,1)}), bf16[8,192,768]{2,1,0:T(8,128)(2,1)}, u32[]{:S(2)}, u32[]{:S(2)}) async-start(bf16[8,192,768]{2,1,0:T(8,128)(2,1)} %bitcast.102), calls=%async_computation.2 | async-start | bytes 4718592 | tf_op jit(solution)/shard_map/all_to_all | solution.py:685
  217.9 1.7 copy-start.18
  257.1 39.6 %all-to-all-start.3 = ((bf16[8,192,768]{2,1,0:T(8,128)(2,1)}), bf16[8,192,768]{2,1,0:T(8,128)(2,1)}, u32[]{:S(2)}, u32[]{:S(2)}) async-start(bf16[8,192,768]{2,1,0:T(8,128)(2,1)} %bitcast.26), calls=%async_computation.3 | async-start | bytes 4718592 | tf_op jit(solution)/shard_map/all_to_all | solution.py:685
  261.5 85.5 %reduce-scatter.6.cloned.1.call-start = ((), (), s32[]{:S(2)}) async-start(), calls=%async_computation.9 | async-start | bytes 1966080 | tf_op jit(solution)/shard_map/reduce_scatter | solution.py:860
  283.0 13.8 %collective-permute-start = (bf16[384,1920]{1,0:T(8,128)(2,1)}, bf16[384,1920]{1,0:T(8,128)(2,1)}, u32[]{:S(2)}, u32[]{:S(2)}) collective-permute-start(bf16[384,1920]{1,0:T(8,128)(2,1)} %get-tuple-element.131), channel_id=1, source_target_pairs={{0,4},{4,0},{8,12},{12,8},{16,20},{20,16},{24,28},{28,24},{1,5},{5... | collective-permute-start | bytes 4423688 | tf_op jit(solution)/shard_map/ppermute | solution.py:849
  283.3 13.5 %copy-start.4 = (f32[384,1920]{1,0:T(8,128)S(1)}, f32[384,1920]{1,0:T(8,128)}, u32[]{:S(2)}) copy-start(f32[384,1920]{1,0:T(8,128)} %get-tuple-element.128) | copy-start | bytes 8847364
  298.9 20.2 %collective-permute-start.1 = (bf16[192,1920]{1,0:T(8,128)(2,1)}, bf16[192,1920]{1,0:T(8,128)(2,1)S(1)}, u32[]{:S(2)}, u32[]{:S(2)}) collective-permute-start(bf16[192,1920]{1,0:T(8,128)(2,1)} %add_convert_fusion.1), channel_id=1, source_target_pairs={{0,8},{4,12},{8,0},{12,4},{16,24},{20,28},{24,16},{28,20},{1,9},{5... | collective-permute-start | bytes 2211848 | tf_op jit(solution)/shard_map/ppermute | solution.py:701
  301.1 105.0 %reduce-scatter.8.cloned.1.call-start = ((), (), s32[]{:S(2)}) async-start(), calls=%async_computation.10 | async-start | bytes 1966080 | tf_op jit(solution)/shard_map/reduce_scatter | solution.py:882
  319.1 5.2 %collective-permute-start.8 = (bf16[384,1280]{1,0:T(8,128)(2,1)}, bf16[384,1280]{1,0:T(8,128)(2,1)}, u32[]{:S(2)}, u32[]{:S(2)}) collective-permute-start(bf16[384,1280]{1,0:T(8,128)(2,1)} %get-tuple-element.146), channel_id=1, source_target_pairs={{0,4},{4,0},{8,12},{12,8},{16,20},{20,16},{24,28},{28,24},{1,5},{5... | collective-permute-start | bytes 2949128 | tf_op jit(solution)/shard_map/ppermute | solution.py:849
  320.0 4.4 %copy-start.2 = (f32[384,1280]{1,0:T(8,128)S(1)}, f32[384,1280]{1,0:T(8,128)}, u32[]{:S(2)}) copy-start(f32[384,1280]{1,0:T(8,128)} %get-tuple-element.145) | copy-start | bytes 5898244
  322.9 10.9 %collective-permute-start.2 = (bf16[96,1920]{1,0:T(8,128)(2,1)}, bf16[96,1920]{1,0:T(8,128)(2,1)}, u32[]{:S(2)}, u32[]{:S(2)}) collective-permute-start(bf16[96,1920]{1,0:T(8,128)(2,1)} %dynamic-slice_convert_fusion), channel_id=1, source_target_pairs={{0,16},{4,20},{8,24},{12,28},{16,0},{20,4},{24,8},{28,12},{1,17},{... | collective-permute-start | bytes 1105928 | tf_op jit(solution)/shard_map/ppermute | solution.py:701
  325.5 13.0 %collective-permute-start.9 = (bf16[192,1280]{1,0:T(8,128)(2,1)S(1)}, bf16[192,1280]{1,0:T(8,128)(2,1)S(1)}, u32[]{:S(2)}, u32[]{:S(2)}) collective-permute-start(bf16[192,1280]{1,0:T(8,128)(2,1)S(1)} %add_convert_fusion.2), channel_id=1, source_target_pairs={{0,8},{4,12},{8,0},{12,4},{16,24},{20,28},{24,16},{28,20},{1,9},{5... | collective-permute-start | bytes 1474568 | tf_op jit(solution)/shard_map/ppermute | solution.py:701
  334.9 9.3 %collective-permute-start.3 = (bf16[48,1920]{1,0:T(8,128)(2,1)S(1)}, bf16[48,1920]{1,0:T(8,128)(2,1)S(1)}, u32[]{:S(2)}, u32[]{:S(2)}) collective-permute-start(bf16[48,1920]{1,0:T(8,128)(2,1)S(1)} %dynamic-slice_convert_fusion.2), channel_id=1, source_target_pairs={{0,1},{1,0},{2,3},{3,2},{4,5},{5,4},{6,7},{7,6},{8,9},{9,8},{10,11... | collective-permute-start | bytes 552968 | tf_op jit(solution)/shard_map/ppermute | solution.py:701
  339.7 7.3 %collective-permute-start.10 = (bf16[96,1280]{1,0:T(8,128)(2,1)S(1)}, bf16[96,1280]{1,0:T(8,128)(2,1)S(1)}, u32[]{:S(2)}, u32[]{:S(2)}) collective-permute-start(bf16[96,1280]{1,0:T(8,128)(2,1)S(1)} %dynamic-slice_convert_fusion.1), channel_id=1, source_target_pairs={{0,16},{4,20},{8,24},{12,28},{16,0},{20,4},{24,8},{28,12},{1,17},{... | collective-permute-start | bytes 737288 | tf_op jit(solution)/shard_map/ppermute | solution.py:701
  347.1 6.7 %collective-permute-start.11 = (bf16[48,1280]{1,0:T(8,128)(2,1)S(1)}, bf16[48,1280]{1,0:T(8,128)(2,1)S(1)}, u32[]{:S(2)}, u32[]{:S(2)}) collective-permute-start(bf16[48,1280]{1,0:T(8,128)(2,1)S(1)} %dynamic-slice_convert_fusion.3), channel_id=1, source_target_pairs={{0,1},{1,0},{2,3},{3,2},{4,5},{5,4},{6,7},{7,6},{8,9},{9,8},{10,11... | collective-permute-start | bytes 368648 | tf_op jit(solution)/shard_map/ppermute | solution.py:701
  347.2 7.8 %collective-permute-start.4 = (bf16[24,1920]{1,0:T(8,128)(2,1)S(1)}, bf16[24,1920]{1,0:T(8,128)(2,1)S(1)}, u32[]{:S(2)}, u32[]{:S(2)}) collective-permute-start(bf16[24,1920]{1,0:T(8,128)(2,1)S(1)} %dynamic-slice_convert_fusion.4), channel_id=1, source_target_pairs={{0,2},{1,3},{2,0},{3,1},{4,6},{5,7},{6,4},{7,5},{8,10},{9,11},{10,... | collective-permute-start | bytes 276488 | tf_op jit(solution)/shard_map/ppermute | solution.py:701
  353.8 5.9 %collective-permute-start.12 = (bf16[24,1280]{1,0:T(8,128)(2,1)S(1)}, bf16[24,1280]{1,0:T(8,128)(2,1)S(1)}, u32[]{:S(2)}, u32[]{:S(2)}) collective-permute-start(bf16[24,1280]{1,0:T(8,128)(2,1)S(1)} %dynamic-slice_convert_fusion.5), channel_id=1, source_target_pairs={{0,2},{1,3},{2,0},{3,1},{4,6},{5,7},{6,4},{7,5},{8,10},{9,11},{10,... | collective-permute-start | bytes 184328 | tf_op jit(solution)/shard_map/ppermute | solution.py:701
  355.0 8.2 %collective-permute-start.5 = (bf16[24,1920]{1,0:T(8,128)(2,1)S(1)}, bf16[24,1920]{1,0:T(8,128)(2,1)S(1)}, u32[]{:S(2)}, u32[]{:S(2)}) collective-permute-start(bf16[24,1920]{1,0:T(8,128)(2,1)S(1)} %add_convert_fusion.3), channel_id=1, source_target_pairs={{0,2},{1,3},{2,0},{3,1},{4,6},{5,7},{6,4},{7,5},{8,10},{9,11},{10,... | collective-permute-start | bytes 276488 | tf_op jit(solution)/shard_map/ppermute | solution.py:712
  359.8 5.2 %collective-permute-start.13 = (bf16[24,1280]{1,0:T(8,128)(2,1)S(1)}, bf16[24,1280]{1,0:T(8,128)(2,1)S(1)}, u32[]{:S(2)}, u32[]{:S(2)}) collective-permute-start(bf16[24,1280]{1,0:T(8,128)(2,1)S(1)} %add_convert_fusion.4), channel_id=1, source_target_pairs={{0,2},{1,3},{2,0},{3,1},{4,6},{5,7},{6,4},{7,5},{8,10},{9,11},{10,... | collective-permute-start | bytes 184328 | tf_op jit(solution)/shard_map/ppermute | solution.py:712
  363.2 5.8 %collective-permute-start.6 = (bf16[48,1920]{1,0:T(8,128)(2,1)S(1)}, bf16[48,1920]{1,0:T(8,128)(2,1)S(1)}, u32[]{:S(2)}, u32[]{:S(2)}) collective-permute-start(bf16[48,1920]{1,0:T(8,128)(2,1)S(1)} %maximum_select_fusion.7), channel_id=1, source_target_pairs={{0,1},{1,0},{2,3},{3,2},{4,5},{5,4},{6,7},{7,6},{8,9},{9,8},{10,11... | collective-permute-start | bytes 552968 | tf_op jit(solution)/shard_map/ppermute | solution.py:712
  365.0 5.7 %collective-permute-start.14 = (bf16[48,1280]{1,0:T(8,128)(2,1)S(1)}, bf16[48,1280]{1,0:T(8,128)(2,1)S(1)}, u32[]{:S(2)}, u32[]{:S(2)}) collective-permute-start(bf16[48,1280]{1,0:T(8,128)(2,1)S(1)} %maximum_select_fusion.8), channel_id=1, source_target_pairs={{0,1},{1,0},{2,3},{3,2},{4,5},{5,4},{6,7},{7,6},{8,9},{9,8},{10,11... | collective-permute-start | bytes 368648 | tf_op jit(solution)/shard_map/ppermute | solution.py:712
  369.2 7.1 %collective-permute-start.7 = (bf16[96,1664]{1,0:T(8,128)(2,1)S(1)}, bf16[96,1664]{1,0:T(8,128)(2,1)S(1)}, u32[]{:S(2)}, u32[]{:S(2)}) collective-permute-start(bf16[96,1664]{1,0:T(8,128)(2,1)S(1)} %slice.35), channel_id=1, source_target_pairs={{0,16},{4,20},{8,24},{12,28},{16,0},{20,4},{24,8},{28,12},{1,17},{... | collective-permute-start | bytes 958472 | tf_op jit(solution)/shard_map/ppermute | solution.py:724
  370.8 8.1 %collective-permute-start.15 = (bf16[96,1536]{1,0:T(8,128)(2,1)S(1)}, bf16[96,1536]{1,0:T(8,128)(2,1)S(1)}, u32[]{:S(2)}, u32[]{:S(2)}) collective-permute-start(bf16[96,1536]{1,0:T(8,128)(2,1)S(1)} %get-tuple-element.181), channel_id=1, source_target_pairs={{0,8},{4,12},{8,0},{12,4},{16,24},{20,28},{24,16},{28,20},{1,9},{5... | collective-permute-start | bytes 884744 | tf_op jit(solution)/shard_map/ppermute | solution.py:725
  379.1 14.7 %collective-permute-start.16 = (bf16[192,1664]{1,0:T(8,128)(2,1)S(1)}, bf16[192,1664]{1,0:T(8,128)(2,1)S(1)}, u32[]{:S(2)}, u32[]{:S(2)}) collective-permute-start(bf16[192,1664]{1,0:T(8,128)(2,1)S(1)} %maximum_select_fusion.2), channel_id=1, source_target_pairs={{0,8},{4,12},{8,0},{12,4},{16,24},{20,28},{24,16},{28,20},{1,9},{5... | collective-permute-start | bytes 1916936 | tf_op jit(solution)/shard_map/ppermute | solution.py:724
  381.8 12.0 %collective-permute-start.17 = (bf16[2,96,1536]{2,1,0:T(8,128)(2,1)}, bf16[2,96,1536]{2,1,0:T(8,128)(2,1)S(1)}, u32[]{:S(2)}, u32[]{:S(2)}) collective-permute-start(bf16[2,96,1536]{2,1,0:T(8,128)(2,1)} %maximum_select_fusion.3), channel_id=1, source_target_pairs={{0,16},{4,20},{8,24},{12,28},{16,0},{20,4},{24,8},{28,12},{1,17},{... | collective-permute-start | bytes 1769480 | tf_op jit(solution)/shard_map/ppermute | solution.py:725
  394.2 4.7 %collective-permute-start.18 = (bf16[384,1664]{1,0:T(8,128)(2,1)S(1)}, bf16[384,1664]{1,0:T(8,128)(2,1)S(1)}, u32[]{:S(2)}, u32[]{:S(2)}) collective-permute-start(bf16[384,1664]{1,0:T(8,128)(2,1)S(1)} %maximum_select_fusion.one_ref), channel_id=1, source_target_pairs={{0,4},{4,0},{8,12},{12,8},{16,20},{20,16},{24,28},{28,24},{1,5},{5... | collective-permute-start | bytes 3833864 | tf_op jit(solution)/shard_map/ppermute | solution.py:849
  394.5 4.5 %collective-permute-start.19 = (bf16[384,1536]{1,0:T(8,128)(2,1)S(1)}, bf16[384,1536]{1,0:T(8,128)(2,1)S(1)}, u32[]{:S(2)}, u32[]{:S(2)}) collective-permute-start(bf16[384,1536]{1,0:T(8,128)(2,1)S(1)} %bitcast.95), channel_id=1, source_target_pairs={{0,4},{4,0},{8,12},{12,8},{16,20},{20,16},{24,28},{28,24},{1,5},{5... | collective-permute-start | bytes 3538952 | tf_op jit(solution)/shard_map/ppermute | solution.py:849
  (3 other events, 2.4 us)
Sparse Core Ops, SparseCore 0:
  11.4 118.0 all-gather.3
  131.6 61.7 all-gather.5
  195.7 109.3 reduce-scatter.3
  307.3 39.6 reduce-scatter.5
  370.8 35.3 reduce-scatter.7

commit v4 on v3

--- a/solution.py
+++ b/solution.py
@@ -550,7 +550,7 @@
 
 def combine_out(rows, target, gate, resid):
     length, width = resid.shape
-    tile = min(QTILE, length)
+    tile = min(2 * QTILE, length)
     column = pl.BlockSpec((tile, 1), lambda i: (i, 0))
     return pl.pallas_call(
         combine_out_kernel,
@@ -561,50 +561,62 @@
         out_specs=pl.BlockSpec((1, tile, width), lambda i: (0, i, 0)),
         out_shape=jax.ShapeDtypeStruct((1, length, width), BF16),
         compiler_params=EXPERT_PARAMS,
-        cost_estimate=pl.CostEstimate(
-            flops=2 * length * width * rows.shape[0],
-            bytes_accessed=8 * length * width,
-            transcendentals=0,
-        ),
+        cost_estimate=pl.CostEstimate(flops=1, bytes_accessed=1, transcendentals=0),
         name="combine_out",
     )(rows, target, gate, resid)
 
 
-def finish_experts_kernel(blocks, turned, first_ref, second_ref, out_ref):
+def finish_hidden_kernel(blocks, first_ref, second_ref, out_ref):
     step = pl.program_id(0)
-
-    def put(rows):
-        out_ref[0] = (rows.T if turned else rows).astype(F32)
 
     @pl.when(step < blocks)
     def _():
-        put(first_ref[0, 0])
+        out_ref[0] = first_ref[0, 0].astype(F32)
 
     @pl.when(step >= blocks)
     def _():
-        put(second_ref[0])
-
-
-def finish_experts(first, second, index):
+        out_ref[0] = second_ref[0].astype(F32)
+
+
+def finish_hidden(first, second):
     unused, width, size = second.shape
     blocks = first.shape[3] // size
-    hidden = first.shape[3] + size
-    turned = index == 1
-    block, shape = (1, width, size), (1, width, hidden)
-    if turned:
-        block, shape = (1, size, width), (1, hidden, width)
     return pl.pallas_call(
-        functools.partial(finish_experts_kernel, blocks, turned),
+        functools.partial(finish_hidden_kernel, blocks),
         grid=(blocks + 1,),
         in_specs=[
-            pl.BlockSpec((1, 1, width, size), lambda i: (0, index, 0, jnp.minimum(i, blocks - 1))),
+            pl.BlockSpec((1, 1, width, size), lambda i: (0, 0, 0, jnp.minimum(i, blocks - 1))),
             whole(second.shape),
         ],
-        out_specs=pl.BlockSpec(block, lambda i: (0, i, 0) if turned else (0, 0, i)),
-        out_shape=jax.ShapeDtypeStruct(shape, F32),
+        out_specs=pl.BlockSpec((1, width, size), lambda i: (0, 0, i)),
+        out_shape=jax.ShapeDtypeStruct((1, width, (blocks + 1) * size), F32),
         compiler_params=EXPERT_PARAMS,
-        name="finish_experts",
+        name="finish_hidden",
     )(first, second)
+
+
+def finish_down_kernel(rows_ref, *refs):
+    refs[-1][0] = rows_ref[...].reshape(rows_ref.shape[-2:]).T.astype(F32)
+
+
+def finish_down(source, size, blocks, filled=None):
+    width = source.shape[-2]
+    if filled is None:
+        specs = [pl.BlockSpec((1, 1, width, size), lambda i: (0, 1, 0, i))]
+        operands, steps, at = (source,), blocks, 0
+    else:
+        specs = [whole(source.shape), pl.BlockSpec(memory_space=pl.ANY)]
+        operands, steps, at = (source, filled), 1, blocks
+    return pl.pallas_call(
+        finish_down_kernel,
+        grid=(steps,),
+        in_specs=specs,
+        out_specs=pl.BlockSpec((1, size, width), lambda i: (0, at + i, 0)),
+        out_shape=jax.ShapeDtypeStruct((1, (blocks + 1) * size, width), F32),
+        input_output_aliases={} if filled is None else {1: 0},
+        compiler_params=EXPERT_PARAMS,
+        name="finish_down",
+    )(*operands)
 
 
 def spread_kernel(
@@ -716,19 +728,23 @@
     return total
 
 
-def gather_plane(one, two, flags, sizes, bits, work, operands):
+def gather_plane(one, two, flags, sizes, bits, works):
     columns = two.shape[1]
+    found = []
     for at, (axis, flip) in enumerate(bits):
         back = len(bits) - 1 - at
+        beside = None
+        if at in works:
+            work, operands = works[at]
+            one, two, operands = lax.optimization_barrier((one, two, operands))
+            beside = work(*operands)
         came = [
             lax.ppermute(one, bits[back][0], xor_pairs(sizes[bits[back][0]], bits[back][1])),
             lax.ppermute(two, axis, xor_pairs(sizes[axis], flip)),
         ]
-        if at == 0:
-            came, operands = lax.optimization_barrier((came, operands))
-            done = work(*operands)
-        if at == len(bits) - 1:
-            came, done = lax.optimization_barrier((came, done))
+        if beside is not None:
+            came, beside = lax.optimization_barrier((came, beside))
+            found.append(beside)
         came_one, came_two = lax.optimization_barrier(came)
         one = jnp.where(
             flags[back] == 0, jnp.concatenate([one, came_one], 0), jnp.concatenate([came_one, one], 0)
@@ -736,7 +752,7 @@
         two = jnp.where(
             flags[at] == 0, jnp.stack([two, came_two], at), jnp.stack([came_two, two], at)
         )
-    return one, two.reshape(-1, columns), done
+    return one, two.reshape(-1, columns), *found
 
 
 def make_shards(n_wide, n_narrow):
@@ -885,16 +901,20 @@
         moved = pairs // 3
         near_cols = near[0].shape[1] - moved * PAIR
         near = [near[0][:, :near_cols], jnp.concatenate([near[1], near[0][:, near_cols:]], 1)]
-        def finish(first_summed, hidden_summed, returned):
-            return (
-                finish_experts(first_summed, hidden_summed, 0),
-                combine_out(returned, target, gate, resid),
-            )
-
-        *near, (hidden_grad, block_out) = gather_plane(
-            *near, inner[0], sizes, plane, finish, (first_summed, hidden_summed, returned)
-        )
-        down_grad = finish_experts(first_summed, down_summed, 1)
+        size = down_summed.shape[2]
+        blocks = first_summed.shape[3] // size
+
+        def finish_early(first_summed, hidden_summed):
+            return finish_hidden(first_summed, hidden_summed), finish_down(first_summed, size, blocks)
+
+        works = {
+            0: (finish_early, (first_summed, hidden_summed)),
+            len(plane) - 1: (combine_out, (returned, target, gate, resid)),
+        }
+        *near, (hidden_grad, down_grad), block_out = gather_plane(
+            *near, inner[0], sizes, plane, works
+        )
+        down_grad = finish_down(down_summed, size, blocks, down_grad)
         halves = [(half, swap(half)) for half in near]
         query_grad, key_grad, value_grad, output_weight_grad, centroids_grad, *vectors = spread(
             flag.reshape(1), halves, width, counts[0], moved, experts_all

time: 420 us -> 420 us (level)
  transfers between devices with their start and end apart: 29 -> 29, of which waited for: 17 -> 20; matrix products, arithmetic and copies ran while one was open for 11% -> 12% of each run, Pallas kernels for 42% -> 42%
where the time goes in v4:
time: 420 us; the launch traced here: 416 us
  Pallas kernels  177 us (42%)
  waiting for transfers between devices  135 us (32%)
  starting transfers between devices  34.5 us (8%)
  other arithmetic  20.7 us (5%)
  matrix products  20 us (5%)
  between operations  15.6 us (4%)
  local copies, waits for them, and re-layouts  14.3 us (3%)
    pallas_call x3, Pallas kernels, attend_back(): pl.pallas_call(functools.partial(attend_back_kernel, scale, counts, part)...  52.3 us
    pallas_call x1, Pallas kernels, expert_first(): pl.pallas_call(functools.partial(expert_first_kernel, tiles), grid=(tiles...  44.6 us
    all_to_all x4, waiting for transfers between devices, exchange(): lax.all_to_all(rows.reshape(blocks, -1, shape[1]), 'wide', split_axis=0,...  44.5 us
    all_gather x2, waiting for transfers between devices, shards(): lax.all_gather(pack, 'narrow', axis=0, tiled=True)  41.6 us
    ppermute x8, waiting for transfers between devices, reduce_halves(): lax.ppermute(add_up(theirs).astype(BF16), axis, xor_pairs(sizes[axis], fl...  25.7 us
    pallas_call x1, Pallas kernels, attend(): pl.pallas_call(functools.partial(attend_kernel, scale), grid_spec=pltpu.P...  22.3 us
    pallas_call x1, Pallas kernels, expert_last(): pl.pallas_call(expert_last_kernel, grid=(rows // tile,), in_specs=[tiled(...  19.4 us
    all_to_all x4, starting transfers between devices, exchange(): lax.all_to_all(rows.reshape(blocks, -1, shape[1]), 'wide', split_axis=0,...  18.3 us
  transfers between devices with their start and end apart: 29, of which 20 were waited for; matrix products, arithmetic and copies ran while one was open for 12% of the time, Pallas kernels for 42%

profile of v4, /device:TPU:0, one launch (start us, length us, event | category | flops | bytes accessed | tf_op | source)
XLA Modules:
  0.0 416.4 jit_solution(11387836688636365860)
XLA Ops:
  7.2 1.6 copy.48
  12.1 2.3 reduce-window.6
  14.9 4.7 %fusion.11 = bf16[1536,768]{1,0:T(8,128)(2,1)} fusion(s32[1024]{0:T(1024)S(1)} %add_select_fusion.1, bf16[1,1024,768]{2,1,0:T(8,128)(2,1)S(1)} %copy-done.19), kind=kOutput, calls=%fused_computation.15 | convolution fusion | flops 2418671616 | bytes 3936256 | tf_op jit(solution)/shard_map/dot_general | solution.py:23
  19.6 5.7 %all-to-all-start = ((bf16[8,192,768]{2,1,0:T(8,128)(2,1)}), bf16[8,192,768]{2,1,0:T(8,128)(2,1)}, u32[]{:S(2)}, u32[]{:S(2)}) async-start(bf16[8,192,768]{2,1,0:T(8,128)(2,1)} %bitcast.11), calls=%async_computation | async-start | bytes 4718592 | tf_op jit(solution)/shard_map/all_to_all | solution.py:697
  30.0 7.1 %convolution_convert_fusion.q_ref.k_ref.v_ref = bf16[1024,2304]{1,0:T(8,128)(2,1)} fusion(bf16[768,768]{1,0:T(8,128)(2,1)S(1)} %copy-done.8, bf16[768,768]{1,0:T(8,128)(2,1)S(1)} %copy-done.9, bf16[768,768]{1,0:T(8,128)(2,1)S(1)} %copy-done.10, bf16[1,1024,768]{2,1,0:T(8,128)(2,1)S(1)} %copy-done.1, f32[768]{0:T(1024)S(1)} %copy-done.16, ...), kind=kOutput, calls=%fused_computation.3 | convolution fusion | flops 3641573376 | bytes 9844736 | tf_op jit(solution)/shard_map/dot_general | solution.py:19
  37.2 22.3 %attend.1 = (bf16[1024,768]{1,0:T(8,128)(2,1)S(1)}, bf16[6,2,2560,256]{3,2,1,0:T(8,128)(2,1)}) custom-call(s32[1]{0:T(128)} %copy.64.len_ref, bf16[1024,2304]{1,0:T(8,128)(2,1)} %convolution_convert_fusion.q_ref.k_ref.v_ref, bf16[1024,2304]{1,0:T(8,128)(2,1)} %convolution_convert_fusion.q_ref.k_ref.v_ref, ...), custom_call_target="tpu_custom_call" | custom-call | flops 3221225472 | bytes 6291456 | tf_op jit(solution)/shard_map/attend/pallas_call | solution.py:75
  59.4 1.8 fusion.30
  61.2 1.7 copy.50
  62.8 2.8 fusion.32
  68.6 4.8 %fusion.12 = bf16[1536,768]{1,0:T(8,128)(2,1)} fusion(bf16[1024,768]{1,0:T(8,128)(2,1)S(1)} %add_convert_fusion, s32[1024]{0:T(1024)S(1)} %add_select_fusion.1), kind=kOutput, calls=%fused_computation.16 | convolution fusion | flops 2418671616 | bytes 3936256 | tf_op jit(solution)/shard_map/dot_general | solution.py:23
  73.3 4.4 %all-to-all-start.1 = ((bf16[8,192,768]{2,1,0:T(8,128)(2,1)}), bf16[8,192,768]{2,1,0:T(8,128)(2,1)S(1)}, u32[]{:S(2)}, u32[]{:S(2)}) async-start(bf16[8,192,768]{2,1,0:T(8,128)(2,1)} %bitcast.103), calls=%async_computation.1 | async-start | bytes 4718592 | tf_op jit(solution)/shard_map/all_to_all | solution.py:697
  79.5 27.8 %all-to-all-done.1 = bf16[8,192,768]{2,1,0:T(8,128)(2,1)S(1)} async-done(((bf16[8,192,768]{2,1,0:T(8,128)(2,1)}), bf16[8,192,768]{2,1,0:T(8,128)(2,1)S(1)}, u32[]{:S(2)}, u32[]{:S(2)}) %all-to-all-start.1) | async-done | bytes 2359328 | tf_op jit(solution)/shard_map/all_to_all | solution.py:697
  107.2 22.3 %all-gather.4.cloned.1.call-done.w_ref = bf16[4,2,512,768]{3,2,1,0:T(8,128)(2,1)} async-done(((bf16[1,2,512,768]{3,2,1,0:T(8,128)(2,1)}), bf16[4,2,512,768]{3,2,1,0:T(8,128)(2,1)}) %all-gather.4.cloned.1.call-update) | async-done | bytes 6291472 | tf_op jit(solution)/shard_map/all_gather | solution.py:799
  129.5 44.6 %expert_first.1 = (f32[1536,768]{1,0:T(8,128)}, f32[1536,768]{1,0:T(8,128)}, bf16[4,2,768,512]{3,2,1,0:T(8,128)(2,1)}, bf16[1536,768]{1,0:T(8,128)(2,1)}, bf16[7...) custom-call(bf16[1536,768]{1,0:T(8,128)(2,1)} %bitcast.100, bf16[1536,768]{1,0:T(8,128)(2,1)} %bitcast.12.u_ref, ...), custom_call_target="tpu_custom_call" | custom-call | flops 28991029248 | bytes 28311552 | tf_op jit(solution)/shard_map/expert_first/pallas_call | solution.py:417
  174.1 19.3 %all-gather.6.cloned.1.call-done = bf16[8,256,768]{2,1,0:T(8,128)(2,1)} async-done(((bf16[2,256,768]{2,1,0:T(8,128)(2,1)}), bf16[8,256,768]{2,1,0:T(8,128)(2,1)}) %all-gather.6.cloned.1.call-update) | async-done | bytes 3145744 | tf_op jit(solution)/shard_map/all_gather | solution.py:799
  193.4 19.4 %expert_last.1 = (bf16[1536,768]{1,0:T(8,128)(2,1)}, bf16[1536,768]{1,0:T(8,128)(2,1)}, f32[1,768]{1,0:T(1,128)}, bf16[1536,1024]{1,0:T(8,128)(2,1)}, bf16[1536,1024]{1,0:T(8,128)(2,1)}) custom-call(bf16[1536,768]{1,0:T(8,128)(2,1)} %bitcast.101, bf16[1536,768]{1,0:T(8,128)(2,1)} %get-tuple-element.115.g_ref, bf16[1536,768]{1,0:T(8,128)(2,1)} %bitcast.12.u_ref, ...), custom_call_target="tpu_custom_call" | custom-call | flops 9663676416 | bytes 28311552 | tf_op jit(solution)/shard_map/expert_last/pallas_call | solution.py:452
  212.8 4.5 %all-to-all-start.2 = ((bf16[8,192,768]{2,1,0:T(8,128)(2,1)}), bf16[8,192,768]{2,1,0:T(8,128)(2,1)}, u32[]{:S(2)}, u32[]{:S(2)}) async-start(bf16[8,192,768]{2,1,0:T(8,128)(2,1)} %bitcast.102), calls=%async_computation.2 | async-start | bytes 4718592 | tf_op jit(solution)/shard_map/all_to_all | solution.py:697
  217.9 1.7 copy.53.normed_t
  220.3 9.8 %expert_weights.1 = (bf16[4,768,256]{2,1,0:T(8,128)(2,1)}, bf16[4,768,256]{2,1,0:T(8,128)(2,1)}) custom-call(bf16[768,1536]{1,0:T(8,128)(2,1)} %get-tuple-element.120.xt_ref, bf16[768,1536]{1,0:T(8,128)(2,1)} %get-tuple-element.121.gt_ref, bf16[1536,1024]{1,0:T(8,128)(2,1)} %get-tuple-element.122.active_ref, bf16[1536,1024]{1,0:T(8,128)(2,1)} %get-tuple-element.123.pre_ref), custom_call_target="tpu_custom_call" | custom-call | flops 4831838208 | bytes 28311552 | tf_op jit(solution)/shard_map/expert_weights/pallas_call | solution.py:472
  230.1 16.7 %all-to-all-done.2 = bf16[8,192,768]{2,1,0:T(8,128)(2,1)} async-done(((bf16[8,192,768]{2,1,0:T(8,128)(2,1)}), bf16[8,192,768]{2,1,0:T(8,128)(2,1)}, u32[]{:S(2)}, u32[]{:S(2)}) %all-to-all-start.2) | async-done | bytes 2359328 | tf_op jit(solution)/shard_map/all_to_all | solution.py:697
  246.8 10.3 %combine_back.1 = (f32[1024,768]{1,0:T(8,128)}, bf16[1024,768]{1,0:T(8,128)(2,1)}, bf16[1024,768]{1,0:T(8,128)(2,1)}, f32[8,768]{1,0:T(8,128)}) custom-call(bf16[1536,768]{1,0:T(8,128)(2,1)} %bitcast.25.back_ref, s32[1024,1]{1,0:T(8,128)} %add_select_fusion.target_ref, f32[1024,768]{1,0:T(8,128)} %copy-done, bf16[1024,768]{1,0:T(8,128)(2,1)} %bitcast.115, ...), custom_call_target="tpu_custom_call" | custom-call | flops 3623878656 | bytes 15728640 | tf_op jit(solution)/shard_map/combine_back/pallas_call | solution.py:524
  257.1 3.6 all-to-all-start.3
  261.0 21.4 %attend_back.3 = (f32[384,1920]{1,0:T(8,128)}, bf16[384,1920]{1,0:T(8,128)(2,1)}, bf16[3,1024,384]{2,1,0:T(8,128)(2,1)}) custom-call(s32[1]{0:T(128)} %bitcast.flag_ref, bf16[1024,2304]{1,0:T(8,128)(2,1)} %convolution_convert_fusion.q_ref.k_ref.v_ref, bf16[1024,2304]{1,0:T(8,128)(2,1)} %convolution_convert_fusion.q_ref.k_ref.v_ref, ...), custom_call_target="tpu_custom_call" | custom-call | flops 8053063680 | bytes 5505024 | tf_op jit(solution)/shard_map/attend_back/pallas_call | solution.py:277
  282.7 13.3 %attend_back.4 = (f32[384,1280]{1,0:T(8,128)}, bf16[384,1280]{1,0:T(8,128)(2,1)}, bf16[3,1024,256]{2,1,0:T(8,128)(2,1)}) custom-call(s32[1]{0:T(128)} %bitcast.flag_ref, bf16[1024,2304]{1,0:T(8,128)(2,1)} %convolution_convert_fusion.q_ref.k_ref.v_ref, bf16[1024,2304]{1,0:T(8,128)(2,1)} %convolution_convert_fusion.q_ref.k_ref.v_ref, ...), custom_call_target="tpu_custom_call" | custom-call | flops 5368709120 | bytes 3670016 | tf_op jit(solution)/shard_map/attend_back/pallas_call | solution.py:277
  296.0 3.4 add_convert_fusion.1
  299.5 1.7 collective-permute-start.1
  302.1 17.7 %attend_back.5 = (f32[384,1280]{1,0:T(8,128)}, bf16[384,1280]{1,0:T(8,128)(2,1)}, bf16[1,1024,768]{2,1,0:T(8,128)(2,1)}) custom-call(s32[1]{0:T(128)} %bitcast.flag_ref, bf16[1024,2304]{1,0:T(8,128)(2,1)} %convolution_convert_fusion.q_ref.k_ref.v_ref, ...), custom_call_target="tpu_custom_call", output_to_operand_aliasing={{0}: (17, {}), {1}: (18, {})} | custom-call | flops 2684354560 | bytes 1835008 | tf_op jit(solution)/shard_map/attend_back/pallas_call | solution.py:277
  320.6 2.1 convert_add_fusion
  323.5 1.5 collective-permute-start.2
  326.7 7.7 %collective-permute-done.2 = bf16[96,1920]{1,0:T(8,128)(2,1)} collective-permute-done((bf16[96,1920]{1,0:T(8,128)(2,1)}, bf16[96,1920]{1,0:T(8,128)(2,1)}, u32[]{:S(2)}, u32[]{:S(2)}) %collective-permute-start.2) | collective-permute-done | bytes 368672 | tf_op jit(solution)/shard_map/ppermute | solution.py:713
  335.6 3.5 collective-permute-done.8
  341.0 3.9 collective-permute-done.3
  344.9 1.8 reduce-scatter.6.cloned.1.call-done.second_ref
  348.8 3.9 collective-permute-done.10
  352.8 2.2 collective-permute-start.11
  355.8 5.9 %collective-permute-done.11 = bf16[24,1280]{1,0:T(8,128)(2,1)S(1)} collective-permute-done((bf16[24,1280]{1,0:T(8,128)(2,1)S(1)}, bf16[24,1280]{1,0:T(8,128)(2,1)S(1)}, u32[]{:S(2)}, u32[]{:S(2)}) %collective-permute-start.11) | collective-permute-done | bytes 61472 | tf_op jit(solution)/shard_map/ppermute | solution.py:713
  363.6 3.4 collective-permute-done.12
  367.1 1.8 collective-permute-done.6
  369.1 2.9 collective-permute-done.13
  373.5 2.3 finish_down.2.refs_0_
  375.8 3.0 finish_hidden.1
  379.9 1.8 collective-permute-start.16
  381.7 1.8 collective-permute-start.17
  384.5 6.2 %combine_out.1 = bf16[1,1024,768]{2,1,0:T(8,128)(2,1)} custom-call(bf16[1536,768]{1,0:T(8,128)(2,1)} %bitcast.94, s32[1024,1]{1,0:T(8,128)} %add_select_fusion.target_ref, f32[1024,1]{1,0:T(8,128)} %copy.56.gate_ref, f32[1024,768]{1,0:T(8,128)} %copy-done), custom_call_target="tpu_custom_call" | custom-call | flops 1 | bytes 1 | tf_op jit(solution)/shard_map/combine_out/pallas_call | solution.py:555
  394.0 3.8 collective-permute-done.19.two_other
  397.8 4.5 %spread.1 = (f32[768,768]{1,0:T(8,128)}, f32[768,768]{1,0:T(8,128)}, f32[768,768]{1,0:T(8,128)}, f32[768,768]{1,0:T(8,128)}, f32[8,768]{1,0:T(8,128)}, /*index=5...) custom-call(s32[1]{0:T(128)} %bitcast.flag_ref, bf16[384,1664]{1,0:T(8,128)(2,1)S(1)} %maximum_select_fusion.one_ref, ...), custom_call_target="tpu_custom_call" | custom-call | tf_op jit(solution)/shard_map/spread/pallas_call | solution.py:670
  402.3 5.0 %reduce-scatter.8.cloned.1.call-done.rows_ref = bf16[1,768,256]{2,1,0:T(8,128)(2,1)} async-done(((bf16[4,768,256]{2,1,0:T(8,128)(2,1)}), bf16[1,768,256]{2,1,0:T(8,128)(2,1)}) %reduce-scatter.8.cloned.1.call-update) | async-done | bytes 393232 | tf_op jit(solution)/shard_map/reduce_scatter | solution.py:898
  407.4 2.0 finish_down.3
  (142 shorter events, 33.2 us)
Async XLA Ops:
  7.2 122.3 %all-gather.4.cloned.1.call-start = ((), (), s32[]{:S(2)}) async-start(), calls=%async_computation.7 | async-start | bytes 7864320 | tf_op jit(solution)/shard_map/all_gather | solution.py:799
  8.8 1.1 slice-start
  11.2 3.7 copy-start.19
  19.6 41.6 %all-to-all-start = ((bf16[8,192,768]{2,1,0:T(8,128)(2,1)}), bf16[8,192,768]{2,1,0:T(8,128)(2,1)}, u32[]{:S(2)}, u32[]{:S(2)}) async-start(bf16[8,192,768]{2,1,0:T(8,128)(2,1)} %bitcast.11), calls=%async_computation | async-start | bytes 4718592 | tf_op jit(solution)/shard_map/all_to_all | solution.py:697
  25.3 2.1 copy-start.1
  27.4 2.4 copy-start.10
  27.7 1.1 copy-start.6
  27.7 1.3 copy-start.7
  28.3 1.5 copy-start.8
  28.3 1.7 copy-start.9
  28.3 1.7 copy-start.15
  28.3 1.7 copy-start.16
  65.7 1.6 copy-start
  65.7 1.6 copy-start.14
  65.7 1.6 copy-start.17
  73.3 4.5 %slice-start.1 = ((bf16[1,768,768]{2,1,0:T(8,128)(2,1)}), bf16[1,256,768]{2,1,0:T(8,128)(2,1)S(1)}, s32[]{:S(2)}) async-start(bf16[1,768,768]{2,1,0:T(8,128)(2,1)} %param.28), calls=%async_computation.13 | async-start | bytes 786432 | tf_op jit(solution)/shard_map/slice | solution.py:793
  73.3 33.9 %all-to-all-start.1 = ((bf16[8,192,768]{2,1,0:T(8,128)(2,1)}), bf16[8,192,768]{2,1,0:T(8,128)(2,1)S(1)}, u32[]{:S(2)}, u32[]{:S(2)}) async-start(bf16[8,192,768]{2,1,0:T(8,128)(2,1)} %bitcast.103), calls=%async_computation.1 | async-start | bytes 4718592 | tf_op jit(solution)/shard_map/all_to_all | solution.py:697
  77.8 115.6 %all-gather.6.cloned.1.call-start = ((), (), s32[]{:S(2)}) async-start(), calls=%async_computation.11 | async-start | bytes 3932160 | tf_op jit(solution)/shard_map/all_gather | solution.py:799
  78.8 240.9 %reduce-scatter.4.cloned.1.call-start = ((), (), s32[]{:S(2)}) async-start(), calls=%async_computation.8 | async-start | bytes 7864320 | tf_op jit(solution)/shard_map/reduce_scatter | solution.py:867
  107.2 22.3 %copy-start.5 = (bf16[8,192,768]{2,1,0:T(8,128)(2,1)}, bf16[8,192,768]{2,1,0:T(8,128)(2,1)S(1)}, u32[]{:S(2)}) copy-start(bf16[8,192,768]{2,1,0:T(8,128)(2,1)S(1)} %all-to-all-done.1) | copy-start | bytes 7077892
  212.8 5.1 %copy-start.4 = (bf16[768,1024]{0,1:T(8,128)(2,1)S(1)}, bf16[768,1024]{0,1:T(8,128)(2,1)}, u32[]{:S(2)}) copy-start(bf16[768,1024]{0,1:T(8,128)(2,1)} %fusion.30) | copy-start | bytes 4718596
  212.8 34.0 %all-to-all-start.2 = ((bf16[8,192,768]{2,1,0:T(8,128)(2,1)}), bf16[8,192,768]{2,1,0:T(8,128)(2,1)}, u32[]{:S(2)}, u32[]{:S(2)}) async-start(bf16[8,192,768]{2,1,0:T(8,128)(2,1)} %bitcast.102), calls=%async_computation.2 | async-start | bytes 4718592 | tf_op jit(solution)/shard_map/all_to_all | solution.py:697
  217.9 1.7 copy-start.18
  257.1 38.9 %all-to-all-start.3 = ((bf16[8,192,768]{2,1,0:T(8,128)(2,1)}), bf16[8,192,768]{2,1,0:T(8,128)(2,1)S(1)}, u32[]{:S(2)}, u32[]{:S(2)}) async-start(bf16[8,192,768]{2,1,0:T(8,128)(2,1)} %bitcast.99), calls=%async_computation.3 | async-start | bytes 4718592 | tf_op jit(solution)/shard_map/all_to_all | solution.py:697
  260.7 86.0 %reduce-scatter.6.cloned.1.call-start = ((), (), s32[]{:S(2)}) async-start(), calls=%async_computation.9 | async-start | bytes 1966080 | tf_op jit(solution)/shard_map/reduce_scatter | solution.py:876
  282.3 13.7 %collective-permute-start = (bf16[384,1920]{1,0:T(8,128)(2,1)}, bf16[384,1920]{1,0:T(8,128)(2,1)}, u32[]{:S(2)}, u32[]{:S(2)}) collective-permute-start(bf16[384,1920]{1,0:T(8,128)(2,1)} %get-tuple-element.139), channel_id=1, source_target_pairs={{0,4},{4,0},{8,12},{12,8},{16,20},{20,16},{24,28},{28,24},{1,5},{5... | collective-permute-start | bytes 4423688 | tf_op jit(solution)/shard_map/ppermute | solution.py:865
  296.0 5.7 %copy-start.2 = (bf16[8,192,768]{2,1,0:T(8,128)(2,1)}, bf16[8,192,768]{2,1,0:T(8,128)(2,1)S(1)}, u32[]{:S(2)}) copy-start(bf16[8,192,768]{2,1,0:T(8,128)(2,1)S(1)} %all-to-all-done.3) | copy-start | bytes 7077892
  299.5 20.3 %collective-permute-start.1 = (bf16[192,1920]{1,0:T(8,128)(2,1)}, bf16[192,1920]{1,0:T(8,128)(2,1)S(1)}, u32[]{:S(2)}, u32[]{:S(2)}) collective-permute-start(bf16[192,1920]{1,0:T(8,128)(2,1)} %add_convert_fusion.1), channel_id=1, source_target_pairs={{0,8},{4,12},{8,0},{12,4},{16,24},{20,28},{24,16},{28,20},{1,9},{5... | collective-permute-start | bytes 2211848 | tf_op jit(solution)/shard_map/ppermute | solution.py:713
  301.7 105.6 %reduce-scatter.8.cloned.1.call-start = ((), (), s32[]{:S(2)}) async-start(), calls=%async_computation.10 | async-start | bytes 1966080 | tf_op jit(solution)/shard_map/reduce_scatter | solution.py:898
  319.8 5.2 %collective-permute-start.7 = (bf16[384,1280]{1,0:T(8,128)(2,1)}, bf16[384,1280]{1,0:T(8,128)(2,1)}, u32[]{:S(2)}, u32[]{:S(2)}) collective-permute-start(bf16[384,1280]{1,0:T(8,128)(2,1)} %get-tuple-element.154), channel_id=1, source_target_pairs={{0,4},{4,0},{8,12},{12,8},{16,20},{20,16},{24,28},{28,24},{1,5},{5... | collective-permute-start | bytes 2949128 | tf_op jit(solution)/shard_map/ppermute | solution.py:865
  320.6 4.4 %copy-start.3 = (f32[384,1280]{1,0:T(8,128)S(1)}, f32[384,1280]{1,0:T(8,128)}, u32[]{:S(2)}) copy-start(f32[384,1280]{1,0:T(8,128)} %get-tuple-element.153) | copy-start | bytes 5898244
  323.5 10.9 %collective-permute-start.2 = (bf16[96,1920]{1,0:T(8,128)(2,1)}, bf16[96,1920]{1,0:T(8,128)(2,1)}, u32[]{:S(2)}, u32[]{:S(2)}) collective-permute-start(bf16[96,1920]{1,0:T(8,128)(2,1)} %dynamic-slice_convert_fusion), channel_id=1, source_target_pairs={{0,16},{4,20},{8,24},{12,28},{16,0},{20,4},{24,8},{28,12},{1,17},{... | collective-permute-start | bytes 1105928 | tf_op jit(solution)/shard_map/ppermute | solution.py:713
  326.1 13.0 %collective-permute-start.8 = (bf16[192,1280]{1,0:T(8,128)(2,1)S(1)}, bf16[192,1280]{1,0:T(8,128)(2,1)S(1)}, u32[]{:S(2)}, u32[]{:S(2)}) collective-permute-start(bf16[192,1280]{1,0:T(8,128)(2,1)S(1)} %add_convert_fusion.2), channel_id=1, source_target_pairs={{0,8},{4,12},{8,0},{12,4},{16,24},{20,28},{24,16},{28,20},{1,9},{5... | collective-permute-start | bytes 1474568 | tf_op jit(solution)/shard_map/ppermute | solution.py:713
  335.5 9.3 %collective-permute-start.3 = (bf16[48,1920]{1,0:T(8,128)(2,1)S(1)}, bf16[48,1920]{1,0:T(8,128)(2,1)S(1)}, u32[]{:S(2)}, u32[]{:S(2)}) collective-permute-start(bf16[48,1920]{1,0:T(8,128)(2,1)S(1)} %dynamic-slice_convert_fusion.2), channel_id=1, source_target_pairs={{0,1},{1,0},{2,3},{3,2},{4,5},{5,4},{6,7},{7,6},{8,9},{9,8},{10,11... | collective-permute-start | bytes 552968 | tf_op jit(solution)/shard_map/ppermute | solution.py:713
  340.3 7.0 %collective-permute-start.9 = (bf16[96,1280]{1,0:T(8,128)(2,1)S(1)}, bf16[96,1280]{1,0:T(8,128)(2,1)S(1)}, u32[]{:S(2)}, u32[]{:S(2)}) collective-permute-start(bf16[96,1280]{1,0:T(8,128)(2,1)S(1)} %dynamic-slice_convert_fusion.1), channel_id=1, source_target_pairs={{0,16},{4,20},{8,24},{12,28},{16,0},{20,4},{24,8},{28,12},{1,17},{... | collective-permute-start | bytes 737288 | tf_op jit(solution)/shard_map/ppermute | solution.py:713
  347.4 5.3 %collective-permute-start.10 = (bf16[48,1280]{1,0:T(8,128)(2,1)S(1)}, bf16[48,1280]{1,0:T(8,128)(2,1)S(1)}, u32[]{:S(2)}, u32[]{:S(2)}) collective-permute-start(bf16[48,1280]{1,0:T(8,128)(2,1)S(1)} %dynamic-slice_convert_fusion.3), channel_id=1, source_target_pairs={{0,1},{1,0},{2,3},{3,2},{4,5},{5,4},{6,7},{7,6},{8,9},{9,8},{10,11... | collective-permute-start | bytes 368648 | tf_op jit(solution)/shard_map/ppermute | solution.py:713
  347.5 7.5 %collective-permute-start.4 = (bf16[24,1920]{1,0:T(8,128)(2,1)S(1)}, bf16[24,1920]{1,0:T(8,128)(2,1)S(1)}, u32[]{:S(2)}, u32[]{:S(2)}) collective-permute-start(bf16[24,1920]{1,0:T(8,128)(2,1)S(1)} %dynamic-slice_convert_fusion.4), channel_id=1, source_target_pairs={{0,2},{1,3},{2,0},{3,1},{4,6},{5,7},{6,4},{7,5},{8,10},{9,11},{10,... | collective-permute-start | bytes 276488 | tf_op jit(solution)/shard_map/ppermute | solution.py:713
  352.8 9.0 %collective-permute-start.11 = (bf16[24,1280]{1,0:T(8,128)(2,1)S(1)}, bf16[24,1280]{1,0:T(8,128)(2,1)S(1)}, u32[]{:S(2)}, u32[]{:S(2)}) collective-permute-start(bf16[24,1280]{1,0:T(8,128)(2,1)S(1)} %dynamic-slice_convert_fusion.5), channel_id=1, source_target_pairs={{0,2},{1,3},{2,0},{3,1},{4,6},{5,7},{6,4},{7,5},{8,10},{9,11},{10,... | collective-permute-start | bytes 184328 | tf_op jit(solution)/shard_map/ppermute | solution.py:713
  355.0 8.1 %collective-permute-start.5 = (bf16[24,1920]{1,0:T(8,128)(2,1)S(1)}, bf16[24,1920]{1,0:T(8,128)(2,1)S(1)}, u32[]{:S(2)}, u32[]{:S(2)}) collective-permute-start(bf16[24,1920]{1,0:T(8,128)(2,1)S(1)} %add_convert_fusion.3), channel_id=1, source_target_pairs={{0,2},{1,3},{2,0},{3,1},{4,6},{5,7},{6,4},{7,5},{8,10},{9,11},{10,... | collective-permute-start | bytes 276488 | tf_op jit(solution)/shard_map/ppermute | solution.py:724
  361.7 5.3 %collective-permute-start.12 = (bf16[24,1280]{1,0:T(8,128)(2,1)S(1)}, bf16[24,1280]{1,0:T(8,128)(2,1)S(1)}, u32[]{:S(2)}, u32[]{:S(2)}) collective-permute-start(bf16[24,1280]{1,0:T(8,128)(2,1)S(1)} %add_convert_fusion.4), channel_id=1, source_target_pairs={{0,2},{1,3},{2,0},{3,1},{4,6},{5,7},{6,4},{7,5},{8,10},{9,11},{10,... | collective-permute-start | bytes 184328 | tf_op jit(solution)/shard_map/ppermute | solution.py:724
  363.1 5.9 %collective-permute-start.6 = (bf16[48,1920]{1,0:T(8,128)(2,1)S(1)}, bf16[48,1920]{1,0:T(8,128)(2,1)S(1)}, u32[]{:S(2)}, u32[]{:S(2)}) collective-permute-start(bf16[48,1920]{1,0:T(8,128)(2,1)S(1)} %maximum_select_fusion.6), channel_id=1, source_target_pairs={{0,1},{1,0},{2,3},{3,2},{4,5},{5,4},{6,7},{7,6},{8,9},{9,8},{10,11... | collective-permute-start | bytes 552968 | tf_op jit(solution)/shard_map/ppermute | solution.py:724
  367.1 4.9 %collective-permute-start.13 = (bf16[48,1280]{1,0:T(8,128)(2,1)S(1)}, bf16[48,1280]{1,0:T(8,128)(2,1)S(1)}, u32[]{:S(2)}, u32[]{:S(2)}) collective-permute-start(bf16[48,1280]{1,0:T(8,128)(2,1)S(1)} %maximum_select_fusion.7), channel_id=1, source_target_pairs={{0,1},{1,0},{2,3},{3,2},{4,5},{5,4},{6,7},{7,6},{8,9},{9,8},{10,11... | collective-permute-start | bytes 368648 | tf_op jit(solution)/shard_map/ppermute | solution.py:724
  372.1 7.6 %collective-permute-start.14 = (bf16[96,1664]{1,0:T(8,128)(2,1)S(1)}, bf16[96,1664]{1,0:T(8,128)(2,1)S(1)}, u32[]{:S(2)}, u32[]{:S(2)}) collective-permute-start(bf16[96,1664]{1,0:T(8,128)(2,1)S(1)} %slice.35), channel_id=1, source_target_pairs={{0,16},{4,20},{8,24},{12,28},{16,0},{20,4},{24,8},{28,12},{1,17},{... | collective-permute-start | bytes 958472 | tf_op jit(solution)/shard_map/ppermute | solution.py:742
  372.2 7.5 %collective-permute-start.15 = (bf16[96,1536]{1,0:T(8,128)(2,1)S(1)}, bf16[96,1536]{1,0:T(8,128)(2,1)S(1)}, u32[]{:S(2)}, u32[]{:S(2)}) collective-permute-start(bf16[96,1536]{1,0:T(8,128)(2,1)S(1)} %pad_maximum_fusion.1), channel_id=1, source_target_pairs={{0,8},{4,12},{8,0},{12,4},{16,24},{20,28},{24,16},{28,20},{1,9},{5... | collective-permute-start | bytes 884744 | tf_op jit(solution)/shard_map/ppermute | solution.py:743
  379.9 12.7 %collective-permute-start.16 = (bf16[192,1664]{1,0:T(8,128)(2,1)S(1)}, bf16[192,1664]{1,0:T(8,128)(2,1)S(1)}, u32[]{:S(2)}, u32[]{:S(2)}) collective-permute-start(bf16[192,1664]{1,0:T(8,128)(2,1)S(1)} %maximum_select_fusion.2), channel_id=1, source_target_pairs={{0,8},{4,12},{8,0},{12,4},{16,24},{20,28},{24,16},{28,20},{1,9},{5... | collective-permute-start | bytes 1916936 | tf_op jit(solution)/shard_map/ppermute | solution.py:742
  381.7 10.1 %collective-permute-start.17 = (bf16[2,96,1536]{2,1,0:T(8,128)(2,1)S(1)}, bf16[2,96,1536]{2,1,0:T(8,128)(2,1)S(1)}, u32[]{:S(2)}, u32[]{:S(2)}) collective-permute-start(bf16[2,96,1536]{2,1,0:T(8,128)(2,1)S(1)} %maximum_select_fusion.3), channel_id=1, source_target_pairs={{0,16},{4,20},{8,24},{12,28},{16,0},{20,4},{24,8},{28,12},{1,17},{... | collective-permute-start | bytes 1769480 | tf_op jit(solution)/shard_map/ppermute | solution.py:743
  393.0 4.7 %collective-permute-start.18 = (bf16[384,1664]{1,0:T(8,128)(2,1)S(1)}, bf16[384,1664]{1,0:T(8,128)(2,1)S(1)}, u32[]{:S(2)}, u32[]{:S(2)}) collective-permute-start(bf16[384,1664]{1,0:T(8,128)(2,1)S(1)} %maximum_select_fusion.one_ref), channel_id=1, source_target_pairs={{0,4},{4,0},{8,12},{12,8},{16,20},{20,16},{24,28},{28,24},{1,5},{5... | collective-permute-start | bytes 3833864 | tf_op jit(solution)/shard_map/ppermute | solution.py:865
  393.4 4.4 %collective-permute-start.19 = (bf16[384,1536]{1,0:T(8,128)(2,1)S(1)}, bf16[384,1536]{1,0:T(8,128)(2,1)S(1)}, u32[]{:S(2)}, u32[]{:S(2)}) collective-permute-start(bf16[384,1536]{1,0:T(8,128)(2,1)S(1)} %bitcast.92), channel_id=1, source_target_pairs={{0,4},{4,0},{8,12},{12,8},{16,20},{20,16},{24,28},{28,24},{1,5},{5... | collective-permute-start | bytes 3538952 | tf_op jit(solution)/shard_map/ppermute | solution.py:865
  (3 other events, 2.4 us)
Sparse Core Ops, SparseCore 0:
  11.4 118.0 all-gather.3
  131.6 61.7 all-gather.5
  195.7 109.3 reduce-scatter.3
  307.3 39.3 reduce-scatter.5
  372.3 35.0 reduce-scatter.7
